TPU v7x, 32 devices: a whole 2x2x4 slice. The times are simulated.
32 devices in a mesh: img: 8 (over y, x, core), row: 4 (over z).
Axes of the slice: x: 2, y: 2, z: 4, core: 2. Of those that a mesh axis runs over, the one named last changes fastest.
Arguments:
- tokens: bfloat16 [16, 1536, 1152], P('img', 'row'), may hold values from -6 to 6
- cotangent: bfloat16 [16, 1536, 1152], P('img', 'row'), may hold values from -0.03125 to 0.03125
- targets: bfloat16 [16, 1536, 768], P('img', 'row'), may hold values from -6 to 6
- time_table: bfloat16 [64, 1152], P(None, 'img'), may hold values from -6 to 6
- ada_weight: bfloat16 [1152, 6912], P('img'), may hold values from -0.1875 to 0.1875
- ada_bias: bfloat16 [6912], P('img'), may hold values from -3 to 3
- qkv_weight: bfloat16 [1152, 3456], P('img'), may hold values from -0.1875 to 0.1875
- out_weight: bfloat16 [1152, 1152], P('img'), may hold values from -2 to 2
- up_weight: bfloat16 [1152, 4608], P('img'), may hold values from -0.1875 to 0.1875
- up_bias: bfloat16 [4608], P('img'), may hold values from -3 to 3
- down_weight: bfloat16 [4608, 1152], P('img'), may hold values from -0.09375 to 0.09375
- proj_first: bfloat16 [1152, 2048], P('img'), may hold values from -0.1875 to 0.1875
- proj_second: bfloat16 [2048, 2048], P('img'), may hold values from -0.125 to 0.125
- proj_third: bfloat16 [2048, 768], P('img'), may hold values from -0.125 to 0.125
- time_bins: int32 [16], replicated, may hold values from 0 to 63
- image_order: int32 [16], P('img'), may hold values from 0 to 15, each once
- counts: int32 [16, 4], P('img'), may hold values from 1 to 12, 32 in all within a row
Outputs:
- block_out: bfloat16 [16, 1536, 1152], P('img', 'row')
- grad_tokens: bfloat16 [16, 1536, 1152], P('img', 'row')
- grad_time_table: float32 [64, 1152], P(None, 'img')
- grad_ada_weight: float32 [1152, 6912], P('img')
- grad_ada_bias: float32 [6912], P('img')
- grad_qkv_weight: float32 [1152, 3456], P('img')
- grad_out_weight: float32 [1152, 1152], P('img')
- grad_up_weight: float32 [1152, 4608], P('img')
- grad_up_bias: float32 [4608], P('img')
- grad_down_weight: float32 [4608, 1152], P('img')
- grad_proj_first: float32 [1152, 2048], P('img')
- grad_proj_second: float32 [2048, 2048], P('img')
- grad_proj_third: float32 [2048, 768], P('img')
Inputs may be any that keep to these rules, and one draw needn't show every extreme that they name: `counts`: each row sums to 32; entry [i, r] is the number of latent rows of image slot i on index r of row, and some entry of every row equals 12.
All inputs are finite; a program needn't handle non-finite values.
Results may differ from a plain program's by a relative error of at most 0.035.
Values may be sent and summed in bfloat16 or wider, within the bound.
A program may use at most 384 MiB of HBM per device.

v0:
```python
import jax
import jax.numpy as jnp
from jax import lax
from jax.sharding import PartitionSpec as P

HEADS = 16
HDIM = 72
RW = 32


def normalize(operand):
    centre = operand - jnp.mean(operand, axis=-1, keepdims=True)
    return centre * lax.rsqrt(jnp.mean(centre * centre, axis=-1, keepdims=True) + 1e-06)


def modulate(operand, shift_rows, scale_rows):
    return normalize(operand) * (1.0 + scale_rows[:, None, :]) + shift_rows[:, None, :]


def alignment(projected, targets):
    unit_proj = projected * lax.rsqrt(
        jnp.mean(projected * projected, axis=-1, keepdims=True) + 1e-06
    )
    unit_target = targets * lax.rsqrt(jnp.mean(targets * targets, axis=-1, keepdims=True) + 1e-06)
    return jnp.mean(unit_proj * unit_target, axis=-1)


def matmul(left_side, right_side):
    return jnp.dot(left_side, right_side, preferred_element_type=jnp.float32)


def transposed(left_side, right_side):
    return lax.dot_general(
        left_side,
        right_side,
        (((left_side.ndim - 1,), (1,)), ((), ())),
        preferred_element_type=jnp.float32,
    )


def weight_grad(left_side, right_side):
    flat_left = left_side.reshape(-1, left_side.shape[-1])
    flat_right = right_side.reshape(-1, right_side.shape[-1])
    return lax.dot_general(
        flat_left, flat_right, (((0,), (0,)), ((), ())), preferred_element_type=jnp.float32
    )


def silu_back(operand, gradient):
    return jax.vjp(jax.nn.silu, operand)[1](gradient)[0]


def gelu_tanh(operand):
    return jax.nn.gelu(operand, approximate=True)


def gelu_back(operand, gradient):
    return jax.vjp(gelu_tanh, operand)[1](gradient)[0]


def key_valid(counts, length, slot_len):
    position = jnp.arange(length)
    device = position // slot_len
    within = position % slot_len
    rank_ids = jnp.arange(counts.shape[1])
    limits = (
        jnp.sum(
            jnp.where(device[None, :, None] == rank_ids[None, None, :], counts[:, None, :], 0),
            axis=2,
        )
        * RW
    )
    return within[None, :] < limits


def local(
    tokens,
    cotangent,
    targets,
    time_table,
    ada_weight,
    ada_bias,
    qkv_weight,
    out_weight,
    up_weight,
    up_bias,
    down_weight,
    proj_first,
    proj_second,
    proj_third,
    time_bins,
    image_order,
    counts,
):
    fetched = (
        lax.all_gather(time_table, "img", axis=1, tiled=True),
        lax.all_gather(ada_weight, "img", axis=0, tiled=True),
        lax.all_gather(ada_bias, "img", axis=0, tiled=True),
        lax.all_gather(qkv_weight, "img", axis=0, tiled=True),
        lax.all_gather(out_weight, "img", axis=0, tiled=True),
        lax.all_gather(up_weight, "img", axis=0, tiled=True),
        lax.all_gather(up_bias, "img", axis=0, tiled=True),
        lax.all_gather(down_weight, "img", axis=0, tiled=True),
        lax.all_gather(proj_first, "img", axis=0, tiled=True),
        lax.all_gather(proj_second, "img", axis=0, tiled=True),
        lax.all_gather(proj_third, "img", axis=0, tiled=True),
    )
    (
        table_full,
        ada_full,
        ada_bias_full,
        qkv_full,
        out_full,
        up_full,
        up_bias_full,
        down_full,
        first_full,
        second_full,
        third_full,
    ) = fetched
    num_images, slot_len, model_width = tokens.shape
    scale_factor = HDIM ** (-0.5)
    total_images = time_bins.shape[0]
    chosen = jnp.sum(
        jnp.where(image_order[:, None] == jnp.arange(total_images)[None, :], time_bins[None, :], 0),
        axis=1,
    )
    select = (chosen[:, None] == jnp.arange(table_full.shape[0])[None, :]).astype(jnp.float32)
    condition = jnp.dot(select, table_full.astype(jnp.float32), precision=lax.Precision.HIGHEST)
    silu_cond = jax.nn.silu(condition).astype(jnp.bfloat16)
    modulation = matmul(silu_cond, ada_full) + ada_bias_full.astype(jnp.float32)
    shift_att, scale_att, gate_att, shift_mlp, scale_mlp, gate_mlp = jnp.split(
        modulation, 6, axis=1
    )
    row_rank = lax.axis_index("row")
    rank_ids = jnp.arange(counts.shape[1])
    own_rows = jnp.sum(jnp.where(rank_ids[None, :] == row_rank, counts, 0), axis=1) * RW
    slot_valid = (jnp.arange(slot_len)[None, :] < own_rows[:, None]).astype(jnp.float32)
    source = tokens.astype(jnp.float32)
    h_att = modulate(source, shift_att, scale_att).astype(jnp.bfloat16)
    qkv_rows = matmul(h_att, qkv_full).astype(jnp.bfloat16)
    queries = qkv_rows[:, :, :model_width]
    key_value = qkv_rows[:, :, model_width:]
    start_state = (
        jnp.full((num_images, HEADS, slot_len), -1e30, jnp.float32),
        jnp.zeros((num_images, HEADS, slot_len), jnp.float32),
        jnp.zeros((num_images, slot_len, HEADS, HDIM), jnp.float32),
    )
    pieces = lax.all_gather(key_value, "row", axis=1, tiled=True)
    usable = key_valid(counts, pieces.shape[1], slot_len)

    def forward_one_image(image_items):
        query_img, piece_img, usable_img, run_max, run_sum, run_acc = image_items
        heads_q = query_img.reshape(slot_len, HEADS, HDIM)
        heads_k = piece_img[:, :model_width].reshape(-1, HEADS, HDIM)
        heads_v = piece_img[:, model_width:].reshape(-1, HEADS, HDIM)
        scores = (
            jnp.einsum("qhd,khd->hqk", heads_q, heads_k, preferred_element_type=jnp.float32)
            * scale_factor
        )
        row_top = jnp.max(jnp.where(usable_img[None, None, :], scores, -1e30), axis=2)
        new_max = jnp.maximum(run_max, row_top)
        weight = jnp.where(usable_img[None, None, :], jnp.exp(scores - new_max[:, :, None]), 0.0)
        decay = jnp.exp(run_max - new_max)
        new_sum = run_sum * decay + jnp.sum(weight, axis=2)
        update = jnp.einsum(
            "hqk,khd->qhd", weight.astype(jnp.bfloat16), heads_v, preferred_element_type=jnp.float32
        )
        return (new_max, new_sum, run_acc * decay.T[:, :, None] + update)

    run_max, run_sum, run_acc = lax.map(forward_one_image, (queries, pieces, usable) + start_state)
    attended = run_acc / run_sum.transpose(0, 2, 1)[:, :, :, None]
    log_total = run_max + jnp.log(run_sum)
    head_mix = attended.reshape(num_images, slot_len, model_width).astype(jnp.bfloat16)
    attn_out = matmul(head_mix, out_full)
    residual = source + gate_att[:, None, :] * attn_out
    h_mlp = modulate(residual, shift_mlp, scale_mlp).astype(jnp.bfloat16)
    pre_act = matmul(h_mlp, up_full) + up_bias_full.astype(jnp.float32)
    gelu_out = gelu_tanh(pre_act).astype(jnp.bfloat16)
    mlp_out = matmul(gelu_out, down_full)
    block_full = slot_valid[:, :, None] * (residual + gate_mlp[:, None, :] * mlp_out)
    block_out = block_full.astype(jnp.bfloat16)
    lin_one = matmul(block_out, first_full)
    hid_one = jax.nn.silu(lin_one).astype(jnp.bfloat16)
    lin_two = matmul(hid_one, second_full)
    hid_two = jax.nn.silu(lin_two).astype(jnp.bfloat16)
    projected = matmul(hid_two, third_full)
    target_float = targets.astype(jnp.float32)

    def align_loss(operand):
        return -0.5 * jnp.sum(slot_valid * alignment(operand, target_float))

    d_proj = jax.vjp(align_loss, projected)[1](jnp.ones((), jnp.float32))[0].astype(jnp.bfloat16)
    grad_third = weight_grad(hid_two, d_proj)
    d_lin_two = silu_back(lin_two, transposed(d_proj, third_full)).astype(jnp.bfloat16)
    grad_second = weight_grad(hid_one, d_lin_two)
    d_lin_one = silu_back(lin_one, transposed(d_lin_two, second_full)).astype(jnp.bfloat16)
    grad_first = weight_grad(block_out, d_lin_one)
    d_res = slot_valid[:, :, None] * (
        cotangent.astype(jnp.float32) + transposed(d_lin_one, first_full)
    )
    d_gate_mlp = jnp.sum(d_res * mlp_out, axis=1)
    d_mlp = (d_res * gate_mlp[:, None, :]).astype(jnp.bfloat16)
    grad_down = weight_grad(gelu_out, d_mlp)
    d_pre = gelu_back(pre_act, transposed(d_mlp, down_full)).astype(jnp.bfloat16)
    grad_up_bias = jnp.sum(d_pre.astype(jnp.float32), axis=(0, 1))
    grad_up = weight_grad(h_mlp, d_pre)
    d_resid_norm, d_shift_mlp, d_scale_mlp = jax.vjp(modulate, residual, shift_mlp, scale_mlp)[1](
        transposed(d_pre, up_full)
    )
    d_residual = d_res + d_resid_norm
    d_gate_att = jnp.sum(d_residual * attn_out, axis=1)
    d_attn = (d_residual * gate_att[:, None, :]).astype(jnp.bfloat16)
    grad_out = weight_grad(head_mix, d_attn)
    d_mixed = transposed(d_attn, out_full).astype(jnp.bfloat16)
    delta = jnp.sum(
        d_mixed.reshape(num_images, slot_len, HEADS, HDIM).astype(jnp.float32) * attended, axis=3
    ).transpose(0, 2, 1)
    zero_q = jnp.zeros((num_images, slot_len, HEADS, HDIM), jnp.float32)
    pieces = lax.all_gather(key_value, "row", axis=1, tiled=True)
    usable = key_valid(counts, pieces.shape[1], slot_len)

    def backward_one_image(image_items):
        query_img, piece_img, usable_img, total_img, delta_img, dmix_img, dq_img = image_items
        heads_q = query_img.reshape(slot_len, HEADS, HDIM)
        heads_k = piece_img[:, :model_width].reshape(-1, HEADS, HDIM)
        heads_v = piece_img[:, model_width:].reshape(-1, HEADS, HDIM)
        heads_d = dmix_img.reshape(slot_len, HEADS, HDIM)
        scores = (
            jnp.einsum("qhd,khd->hqk", heads_q, heads_k, preferred_element_type=jnp.float32)
            * scale_factor
        )
        attn_prob = jnp.where(
            usable_img[None, None, :], jnp.exp(scores - total_img[:, :, None]), 0.0
        )
        d_prob = jnp.einsum("qhd,khd->hqk", heads_d, heads_v, preferred_element_type=jnp.float32)
        d_score = (attn_prob * (d_prob - delta_img[:, :, None])).astype(jnp.bfloat16)
        dq_new = (
            dq_img
            + jnp.einsum("hqk,khd->qhd", d_score, heads_k, preferred_element_type=jnp.float32)
            * scale_factor
        )
        d_key = (
            jnp.einsum("hqk,qhd->khd", d_score, heads_q, preferred_element_type=jnp.float32)
            * scale_factor
        )
        d_value = jnp.einsum(
            "hqk,qhd->khd",
            attn_prob.astype(jnp.bfloat16),
            heads_d,
            preferred_element_type=jnp.float32,
        )
        length = piece_img.shape[0]
        return (
            dq_new,
            jnp.concatenate([d_key.reshape(length, -1), d_value.reshape(length, -1)], axis=1),
        )

    new_q, piece_kv = lax.map(
        backward_one_image, (queries, pieces, usable, log_total, delta, d_mixed, zero_q)
    )
    kv_sum = lax.psum_scatter(piece_kv.astype(jnp.bfloat16), "row", scatter_dimension=1, tiled=True)
    d_qkv = jnp.concatenate(
        [new_q.reshape(num_images, slot_len, model_width).astype(jnp.bfloat16), kv_sum], axis=2
    )
    grad_qkv = weight_grad(h_att, d_qkv)
    d_source, d_shift_att, d_scale_att = jax.vjp(modulate, source, shift_att, scale_att)[1](
        transposed(d_qkv, qkv_full)
    )
    grad_tokens = (d_residual + d_source).astype(jnp.bfloat16)
    partial_mod = jnp.concatenate(
        [d_shift_att, d_scale_att, d_gate_att, d_shift_mlp, d_scale_mlp, d_gate_mlp], axis=1
    )
    total_mod = lax.psum(partial_mod.astype(jnp.bfloat16), "row")
    kept_mod = jnp.where(row_rank == 0, total_mod, jnp.zeros_like(total_mod))
    grad_ada = weight_grad(silu_cond, kept_mod)
    grad_ada_bias = jnp.sum(kept_mod.astype(jnp.float32), axis=0)
    d_cond = silu_back(condition, transposed(kept_mod, ada_full))
    grad_table = jnp.dot(select.T, d_cond, precision=lax.Precision.HIGHEST)
    (
        part_table,
        part_ada,
        part_ada_bias,
        part_qkv,
        part_out,
        part_up,
        part_up_bias,
        part_down,
        part_first,
        part_second,
        part_third,
    ) = (
        lax.psum_scatter(
            grad_table.astype(jnp.bfloat16), "img", scatter_dimension=1, tiled=True
        ).astype(jnp.float32),
        lax.psum_scatter(
            grad_ada.astype(jnp.bfloat16), "img", scatter_dimension=0, tiled=True
        ).astype(jnp.float32),
        lax.psum_scatter(
            grad_ada_bias.astype(jnp.bfloat16), "img", scatter_dimension=0, tiled=True
        ).astype(jnp.float32),
        lax.psum_scatter(
            grad_qkv.astype(jnp.bfloat16), "img", scatter_dimension=0, tiled=True
        ).astype(jnp.float32),
        lax.psum_scatter(
            grad_out.astype(jnp.bfloat16), "img", scatter_dimension=0, tiled=True
        ).astype(jnp.float32),
        lax.psum_scatter(
            grad_up.astype(jnp.bfloat16), "img", scatter_dimension=0, tiled=True
        ).astype(jnp.float32),
        lax.psum_scatter(
            grad_up_bias.astype(jnp.bfloat16), "img", scatter_dimension=0, tiled=True
        ).astype(jnp.float32),
        lax.psum_scatter(
            grad_down.astype(jnp.bfloat16), "img", scatter_dimension=0, tiled=True
        ).astype(jnp.float32),
        lax.psum_scatter(
            grad_first.astype(jnp.bfloat16), "img", scatter_dimension=0, tiled=True
        ).astype(jnp.float32),
        lax.psum_scatter(
            grad_second.astype(jnp.bfloat16), "img", scatter_dimension=0, tiled=True
        ).astype(jnp.float32),
        lax.psum_scatter(
            grad_third.astype(jnp.bfloat16), "img", scatter_dimension=0, tiled=True
        ).astype(jnp.float32),
    )
    summed = (
        lax.psum(part_table.astype(jnp.bfloat16), "row").astype(jnp.float32),
        lax.psum(part_ada.astype(jnp.bfloat16), "row").astype(jnp.float32),
        lax.psum(part_ada_bias.astype(jnp.bfloat16), "row").astype(jnp.float32),
        lax.psum(part_qkv.astype(jnp.bfloat16), "row").astype(jnp.float32),
        lax.psum(part_out.astype(jnp.bfloat16), "row").astype(jnp.float32),
        lax.psum(part_up.astype(jnp.bfloat16), "row").astype(jnp.float32),
        lax.psum(part_up_bias.astype(jnp.bfloat16), "row").astype(jnp.float32),
        lax.psum(part_down.astype(jnp.bfloat16), "row").astype(jnp.float32),
        lax.psum(part_first.astype(jnp.bfloat16), "row").astype(jnp.float32),
        lax.psum(part_second.astype(jnp.bfloat16), "row").astype(jnp.float32),
        lax.psum(part_third.astype(jnp.bfloat16), "row").astype(jnp.float32),
    )
    return (
        block_out,
        grad_tokens,
        summed[0],
        summed[1],
        summed[2],
        summed[3],
        summed[4],
        summed[5],
        summed[6],
        summed[7],
        summed[8],
        summed[9],
        summed[10],
    )


def solution(mesh):
    return jax.shard_map(
        local,
        mesh=mesh,
        in_specs=(
            P("img", "row", None),
            P("img", "row", None),
            P("img", "row", None),
            P(None, "img"),
            P("img", None),
            P("img"),
            P("img", None),
            P("img", None),
            P("img", None),
            P("img"),
            P("img", None),
            P("img", None),
            P("img", None),
            P("img", None),
            P(),
            P("img"),
            P("img", None),
        ),
        out_specs=(
            P("img", "row", None),
            P("img", "row", None),
            P(None, "img"),
            P("img", None),
            P("img"),
            P("img", None),
            P("img", None),
            P("img", None),
            P("img"),
            P("img", None),
            P("img", None),
            P("img", None),
            P("img", None),
        ),
        check_vma=False,
    )
```

profile of v0, /device:TPU:0, one launch (start us, length us, event | category | flops | bytes accessed | tf_op | source)
XLA Modules:
  0.0 2199.0 jit_solution(13334495030481224145)
XLA Ops:
  13.2 26.1 %all-reduce.5 = (bf16[6912]{0:T(1024)(128)(2,1)S(1)}, bf16[4608]{0:T(1024)(128)(2,1)S(1)}) all-reduce(bf16[6912]{0:T(1024)(128)(2,1)S(1)} %dynamic-update-slice, bf16[4608]{0:T(1024)(128)(2,1)S(1)} %dynamic-update-slice.1), channel_id=1, replica_groups=mesh['img'=8,'row'=4] {'img'}, use_global_device_ids=true, to_apply=%add | all-reduce | flops 11520 | bytes 46080
  50.6 49.2 %all-gather.11.cloned.1.call-done = bf16[1152,6912]{1,0:T(8,128)(2,1)} async-done(((bf16[144,6912]{1,0:T(8,128)(2,1)}), bf16[1152,6912]{1,0:T(8,128)(2,1)}) %all-gather.11.cloned.1.call-update) | async-done | bytes 15925264 | tf_op jit(solution)/shard_map/all_gather | solution.py:97
  108.2 46.2 %all-gather.13.cloned.1.call-done = bf16[1152,3456]{1,0:T(8,128)(2,1)} async-done(((bf16[144,3456]{1,0:T(8,128)(2,1)}), bf16[1152,3456]{1,0:T(8,128)(2,1)}) %all-gather.13.cloned.1.call-update) | async-done | bytes 7962640 | tf_op jit(solution)/shard_map/all_gather | solution.py:99
  183.2 229.9 %all-gather.15.cloned.1.call-done = bf16[2,1536,2304]{2,1,0:T(8,128)(2,1)} async-done(((bf16[2,384,2304]{2,1,0:T(8,128)(2,1)}), bf16[2,1536,2304]{2,1,0:T(8,128)(2,1)}) %all-gather.15.cloned.1.call-update) | async-done | bytes 14155792 | tf_op jit(solution)/shard_map/all_gather | solution.py:149
  413.1 18.6 copy.79
  431.7 116.1 %while.28 = (s32[]{:T(128)}, f32[2,16,384]{2,1,0:T(8,128)S(1)}, f32[2,16,384]{2,1,0:T(8,128)S(1)}, f32[2,384,16,72]{1,3,2,0:T(8,128)}, pred[2,1536]{1,0:T(4,128)...) while((s32[]{:T(128)}, f32[2,16,384]{2,1,0:T(8,128)S(1)}, ...), condition=%wide.region_8.9_spmd.clone, body=%wide.region_5.8_spmd.sunk.clone | while | flops 2822191104 | bytes 153362032 | solution.py:171
  453.9 17.6 bitcast_dynamic-update-slice_fusion.7
  471.5 18.3 fusion.206
  511.1 18.1 bitcast_dynamic-update-slice_fusion.7
  529.2 18.2 fusion.206
  579.9 20.9 multiply_convert_fusion.6
  625.3 46.4 %all-gather.25.cloned.1.call-done = bf16[2048,2048]{1,0:T(8,128)(2,1)} async-done(((bf16[256,2048]{1,0:T(8,128)(2,1)}), bf16[2048,2048]{1,0:T(8,128)(2,1)}) %all-gather.25.cloned.1.call-update) | async-done | bytes 8388624 | tf_op jit(solution)/shard_map/all_gather | solution.py:105
  686.1 19.8 all-gather.27.cloned.1.call-done
  741.6 25.3 %fusion.130 = (bf16[4608]{0:T(1024)(128)(2,1)}, bf16[2,384,4608]{2,1,0:T(8,128)(2,1)}) fusion(f32[2,384,4608]{2,1,0:T(8,128)} %fusion.34, f32[4608]{0:T(1024)} %convert_element_type.198, bf16[4608,1152]{1,0:T(8,128)(2,1)} %all-gather.21.cloned.1.call-done, f32[2,384,1152]{2,1,0:T(8,128)} %fusion.69, f32[2,1152]{1,0:T(2,128)} %get-tuple-element.241), kind=kOutput, calls=%fused_computation.217 | convolution fusion | flops 8233348608 | bytes 35426304 | tf_op jit(solution)/shard_map/dot_general | solution.py:33
  800.2 222.2 %while.29 = (s32[]{:T(128)}, bf16[2,384,16,72]{1,3,2,0:T(8,128)(2,1)}, bf16[2,1536,2304]{2,1,0:T(8,128)(2,1)}, bf16[2,1536,2304]{1,2,0:T(8,128)(2,1)}, pred[2,15...) while((s32[]{:T(128)}, ...), condition=%wide.region_18.19_spmd.clone, body=%wide.region_17.18_spmd.sunk.clone | while | flops 6907281408 | bytes 290765088 | solution.py:259
  825.5 17.3 fusion.220
  842.8 26.4 %multiply_convert_fusion.20 = bf16[16,384,1536]{2,1,0:T(8,128)(2,1)} fusion(f32[16,384,1536]{2,1,0:T(8,128)} %fusion.219, f32[16,384]{1,0:T(8,128)} %get-tuple-element.422, f32[16,384]{1,0:T(8,128)} %get-tuple-element.423, pred[1536]{0:T(1024)(128)(4,1)S(1)} %dynamic-slice_reduce_fusion.7, bf16[384,16,72]{0,2,1:T(8,128)(2,1)} %bitcast.279, ...), kind=kOutput, calls=%fused_computation.21.clone.1.clone | convolution fusion | flops 1415577600 | bytes 61097472 | tf_op jit(solution)/shard_map/while/body/eval_jaxpr/qhd,khd->hqk/dot_general | solution.py:236
  936.3 17.3 fusion.220
  953.6 26.4 %multiply_convert_fusion.20 = bf16[16,384,1536]{2,1,0:T(8,128)(2,1)} fusion(f32[16,384,1536]{2,1,0:T(8,128)} %fusion.219, f32[16,384]{1,0:T(8,128)} %get-tuple-element.422, f32[16,384]{1,0:T(8,128)} %get-tuple-element.423, pred[1536]{0:T(1024)(128)(4,1)S(1)} %dynamic-slice_reduce_fusion.7, bf16[384,16,72]{0,2,1:T(8,128)(2,1)} %bitcast.279, ...), kind=kOutput, calls=%fused_computation.21.clone.1.clone | convolution fusion | flops 1415577600 | bytes 61097472 | tf_op jit(solution)/shard_map/while/body/eval_jaxpr/qhd,khd->hqk/dot_general | solution.py:236
  1060.2 17.7 fusion.19
  1098.0 161.8 %reduce-scatter.13.cloned.1.call-done = bf16[2,384,2304]{2,1,0:T(8,128)(2,1)} async-done(((bf16[2,1536,2304]{2,1,0:T(8,128)(2,1)}), bf16[2,384,2304]{2,1,0:T(8,128)(2,1)}) %reduce-scatter.13.cloned.1.call-update) | async-done | bytes 3538960 | tf_op jit(solution)/shard_map/reduce_scatter | solution.py:262
  1289.9 18.9 psum.84
  1329.2 29.5 %reduce-scatter.29.cloned.1.call-done = bf16[256,768]{1,0:T(8,128)(2,1)} async-done(((bf16[2048,768]{1,0:T(8,128)(2,1)}), bf16[256,768]{1,0:T(8,128)(2,1)}) %reduce-scatter.29.cloned.1.call-update) | async-done | bytes 393232 | tf_op jit(solution)/shard_map/reduce_scatter | solution.py:323
  1358.7 57.3 %reduce-scatter.25.cloned.1.call-done = bf16[144,2048]{1,0:T(8,128)(2,1)} async-done(((bf16[1152,2048]{1,0:T(8,128)(2,1)}), bf16[144,2048]{1,0:T(8,128)(2,1)}) %reduce-scatter.25.cloned.1.call-update) | async-done | bytes 589840 | tf_op jit(solution)/shard_map/reduce_scatter | solution.py:317
  1416.0 75.0 %reduce-scatter.27.cloned.1.call-done = bf16[256,2048]{1,0:T(8,128)(2,1)} async-done(((bf16[2048,2048]{1,0:T(8,128)(2,1)}), bf16[256,2048]{1,0:T(8,128)(2,1)}) %reduce-scatter.27.cloned.1.call-update) | async-done | bytes 1048592 | tf_op jit(solution)/shard_map/reduce_scatter | solution.py:320
  1491.0 85.6 %reduce-scatter.23.cloned.1.call-done = bf16[576,1152]{1,0:T(8,128)(2,1)} async-done(((bf16[4608,1152]{1,0:T(8,128)(2,1)}), bf16[576,1152]{1,0:T(8,128)(2,1)}) %reduce-scatter.23.cloned.1.call-update) | async-done | bytes 1327120 | tf_op jit(solution)/shard_map/reduce_scatter | solution.py:314
  1576.6 85.6 %reduce-scatter.21.cloned.1.call-done = bf16[144,4608]{1,0:T(8,128)(2,1)} async-done(((bf16[1152,4608]{1,0:T(8,128)(2,1)}), bf16[144,4608]{1,0:T(8,128)(2,1)}) %reduce-scatter.21.cloned.1.call-update) | async-done | bytes 1327120 | tf_op jit(solution)/shard_map/reduce_scatter | solution.py:308
  1662.3 73.4 %reduce-scatter.17.cloned.1.call-done = bf16[144,3456]{1,0:T(8,128)(2,1)} async-done(((bf16[1152,3456]{1,0:T(8,128)(2,1)}), bf16[144,3456]{1,0:T(8,128)(2,1)}) %reduce-scatter.17.cloned.1.call-update) | async-done | bytes 995344 | tf_op jit(solution)/shard_map/reduce_scatter | solution.py:302
  1735.7 116.8 %reduce-scatter.15.cloned.1.call-done = bf16[144,6912]{1,0:T(8,128)(2,1)} async-done(((bf16[1152,6912]{1,0:T(8,128)(2,1)}), bf16[144,6912]{1,0:T(8,128)(2,1)}) %reduce-scatter.15.cloned.1.call-update) | async-done | bytes 1990672 | tf_op jit(solution)/shard_map/reduce_scatter | solution.py:296
  1853.9 23.1 %all-reduce.4 = (bf16[6912]{0:T(1024)(128)(2,1)S(1)}, bf16[4608]{0:T(1024)(128)(2,1)S(1)}) all-reduce(bf16[6912]{0:T(1024)(128)(2,1)S(1)} %fusion.116, bf16[4608]{0:T(1024)(128)(2,1)S(1)} %copy-done.57), channel_id=5, replica_groups=mesh['img'=8,'row'=4] {'img'}, use_global_device_ids=true, to_apply=%region_34.35.clone | all-reduce | flops 11520 | bytes 46080
  1889.9 20.7 all-reduce.6
  1912.4 264.4 %all-reduce.10.cloned.1.call-done = (bf16[144,6912]{1,0:T(8,128)(2,1)}, bf16[144,3456]{1,0:T(8,128)(2,1)}, bf16[144,1152]{1,0:T(8,128)(2,1)}, bf16[144,4608]{1,0...) async-done(((bf16[144,6912]{1,0:T(8,128)(2,1)}, bf16[144,3456]{1,0:T(8,128)(2,1)}, ...) | async-done | bytes 8003600 | tf_op jit(solution)/shard_map/psum | solution.py:329
  (354 shorter events, 507.9 us)
Async XLA Ops:
  7.2 41.5 %copy-start.69 = (s32[2]{0:T(128)S(1)}, s32[2]{0:T(128)}, u32[]{:S(2)}) copy-start(s32[2]{0:T(128)} %param.36) | copy-start | bytes 28
  7.2 41.7 %copy-start.6 = (bf16[2,384,1152]{2,1,0:T(8,128)(2,1)S(1)}, bf16[2,384,1152]{2,1,0:T(8,128)(2,1)}, u32[]{:S(2)}) copy-start(bf16[2,384,1152]{2,1,0:T(8,128)(2,1)} %param.21) | copy-start | bytes 5308420
  7.2 92.6 %all-gather.11.cloned.1.call-start = ((), (), s32[]{:S(2)}) async-start(), calls=%async_computation.10 | async-start | bytes 17915904 | tf_op jit(solution)/shard_map/all_gather | solution.py:97
  7.9 146.4 %all-gather.13.cloned.1.call-start = ((), (), s32[]{:S(2)}) async-start(), calls=%async_computation.11 | async-start | bytes 8957952 | tf_op jit(solution)/shard_map/all_gather | solution.py:99
  8.7 404.4 %all-gather.15.cloned.1.call-start = ((), (), s32[]{:S(2)}) async-start(), calls=%async_computation.12 | async-start | bytes 17694720 | tf_op jit(solution)/shard_map/all_gather | solution.py:149
  48.9 58.6 %copy-start.71 = (s32[2]{0:T(128)}, s32[2]{0:T(128)S(1)}, u32[]{:S(2)}) copy-start(s32[2]{0:T(128)S(1)} %fusion.114) | copy-start | bytes 28
  49.2 105.1 %copy-start.39 = (f32[2,384]{1,0:T(2,128)}, f32[2,384]{1,0:T(2,128)S(1)}, u32[]{:S(2)}) copy-start(f32[2,384]{1,0:T(2,128)S(1)} %broadcast_multiply_fusion.1) | copy-start | bytes 9220
  50.4 103.9 %copy-start.43 = (f32[2,384]{1,0:T(2,128)}, f32[2,384]{1,0:T(2,128)S(1)}, u32[]{:S(2)}) copy-start(f32[2,384]{1,0:T(2,128)S(1)} %fusion.111) | copy-start | bytes 9220
  50.6 49.2 %copy-start.37 = (f32[2,1152]{1,0:T(2,128)}, f32[2,1152]{1,0:T(2,128)S(1)}, u32[]{:S(2)}) copy-start(f32[2,1152]{1,0:T(2,128)S(1)} %fusion.115) | copy-start | bytes 27652
  108.2 56.4 %copy-start.33 = (f32[2,1152]{1,0:T(2,128)}, f32[2,1152]{1,0:T(2,128)S(1)}, u32[]{:S(2)}) copy-start(f32[2,1152]{1,0:T(2,128)S(1)} %get-tuple-element.245) | copy-start | bytes 27652
  108.2 56.4 %copy-start.58 = (f32[2,1152]{1,0:T(2,128)}, f32[2,1152]{1,0:T(2,128)S(1)}, u32[]{:S(2)}) copy-start(f32[2,1152]{1,0:T(2,128)S(1)} %get-tuple-element.244) | copy-start | bytes 27652
  169.0 383.0 %all-gather.17.cloned.1.call-start = ((), (), s32[]{:S(2)}) async-start(), calls=%async_computation.13 | async-start | bytes 2985984 | tf_op jit(solution)/shard_map/all_gather | solution.py:100
  169.6 393.6 %all-gather.19.cloned.1.call-start = ((), (), s32[]{:S(2)}) async-start(), calls=%async_computation.14 | async-start | bytes 11943936 | tf_op jit(solution)/shard_map/all_gather | solution.py:101
  170.2 409.7 %all-gather.21.cloned.1.call-start = ((), (), s32[]{:S(2)}) async-start(), calls=%async_computation.15 | async-start | bytes 11943936 | tf_op jit(solution)/shard_map/all_gather | solution.py:103
  170.8 444.6 %all-gather.23.cloned.1.call-start = ((), (), s32[]{:S(2)}) async-start(), calls=%async_computation.16 | async-start | bytes 5308416 | tf_op jit(solution)/shard_map/all_gather | solution.py:104
  171.5 500.1 %all-gather.25.cloned.1.call-start = ((), (), s32[]{:S(2)}) async-start(), calls=%async_computation.17 | async-start | bytes 9437184 | tf_op jit(solution)/shard_map/all_gather | solution.py:105
  172.3 533.6 %all-gather.27.cloned.1.call-start = ((), (), s32[]{:S(2)}) async-start(), calls=%async_computation.18 | async-start | bytes 3538944 | tf_op jit(solution)/shard_map/all_gather | solution.py:106
  173.0 1086.8 %reduce-scatter.13.cloned.1.call-start = ((), (), s32[]{:S(2)}) async-start(), calls=%async_computation.19 | async-start | bytes 17694720 | tf_op jit(solution)/shard_map/reduce_scatter | solution.py:262
  559.8 224.3 %copy-start.41 = (f32[2,384]{1,0:T(2,128)}, f32[2,384]{1,0:T(2,128)S(1)}, u32[]{:S(2)}) copy-start(f32[2,384]{1,0:T(2,128)S(1)} %broadcast_multiply_fusion) | copy-start | bytes 9220
  1022.5 306.7 %reduce-scatter.19.cloned.1.call-start = ((), (), s32[]{:S(2)}) async-start(), calls=%async_computation.22 | async-start | bytes 2985984 | tf_op jit(solution)/shard_map/reduce_scatter | solution.py:305
  1030.1 328.6 %reduce-scatter.29.cloned.1.call-start = ((), (), s32[]{:S(2)}) async-start(), calls=%async_computation.27 | async-start | bytes 3538944 | tf_op jit(solution)/shard_map/reduce_scatter | solution.py:323
  1036.9 379.1 %reduce-scatter.25.cloned.1.call-start = ((), (), s32[]{:S(2)}) async-start(), calls=%async_computation.25 | async-start | bytes 5308416 | tf_op jit(solution)/shard_map/reduce_scatter | solution.py:317
  1044.3 446.7 %reduce-scatter.27.cloned.1.call-start = ((), (), s32[]{:S(2)}) async-start(), calls=%async_computation.26 | async-start | bytes 9437184 | tf_op jit(solution)/shard_map/reduce_scatter | solution.py:320
  1058.2 518.5 %reduce-scatter.23.cloned.1.call-start = ((), (), s32[]{:S(2)}) async-start(), calls=%async_computation.24 | async-start | bytes 11943936 | tf_op jit(solution)/shard_map/reduce_scatter | solution.py:314
  1077.9 584.4 %reduce-scatter.21.cloned.1.call-start = ((), (), s32[]{:S(2)}) async-start(), calls=%async_computation.23 | async-start | bytes 11943936 | tf_op jit(solution)/shard_map/reduce_scatter | solution.py:308
  1094.0 165.8 %copy-start.7 = (bf16[2,384,1152]{2,1,0:T(8,128)(2,1)S(1)}, bf16[2,384,1152]{2,1,0:T(8,128)(2,1)}, u32[]{:S(2)}) copy-start(bf16[2,384,1152]{2,1,0:T(8,128)(2,1)} %param.21) | copy-start | bytes 5308420
  1094.1 165.8 %copy-start.34 = (f32[2,1152]{1,0:T(2,128)S(1)}, f32[2,1152]{1,0:T(2,128)}, u32[]{:S(2)}) copy-start(f32[2,1152]{1,0:T(2,128)} %copy-done.33) | copy-start | bytes 27652
  1094.1 165.8 %copy-start.40 = (f32[2,384]{1,0:T(2,128)S(1)}, f32[2,384]{1,0:T(2,128)}, u32[]{:S(2)}) copy-start(f32[2,384]{1,0:T(2,128)} %copy-done.39) | copy-start | bytes 9220
  1094.1 641.6 %reduce-scatter.17.cloned.1.call-start = ((), (), s32[]{:S(2)}) async-start(), calls=%async_computation.21 | async-start | bytes 8957952 | tf_op jit(solution)/shard_map/reduce_scatter | solution.py:302
  1272.3 580.2 %reduce-scatter.15.cloned.1.call-start = ((), (), s32[]{:S(2)}) async-start(), calls=%async_computation.20 | async-start | bytes 17915904 | tf_op jit(solution)/shard_map/reduce_scatter | solution.py:296
  1316.6 572.4 %reduce-scatter.31.cloned.1.call-start = ((), (), s32[]{:S(2)}) async-start(), calls=%async_computation.28 | async-start | bytes 331776
  1329.1 847.8 %all-reduce.10.cloned.1.call-start = ((), (), s32[]{:S(2)}) async-start(), calls=%async_computation.29 | async-start | bytes 16007168 | tf_op jit(solution)/shard_map/psum | solution.py:329
  (72 other events, 470.0 us)
Sparse Core Ops, SparseCore 0:
  9.9 89.8 all-gather.10
  101.7 52.5 all-gather.12
  169.1 243.9 all-gather.14
  414.8 28.4 all-gather.16
  445.1 63.8 all-gather.18
  510.7 63.8 all-gather.20
  576.4 38.9 all-gather.22
  617.2 54.3 all-gather.24
  673.5 32.3 all-gather.26
  1022.6 237.2 reduce-scatter.12
  1263.9 44.8 reduce-scatter.18
  1312.4 46.2 reduce-scatter.28
  1362.1 53.8 reduce-scatter.24
  1419.7 71.2 reduce-scatter.26
  1494.4 82.2 reduce-scatter.22
  1580.0 82.2 reduce-scatter.20
  1665.6 70.0 reduce-scatter.16
  1739.6 112.8 reduce-scatter.14
  1856.1 32.8 reduce-scatter.30
  1892.3 284.4 all-reduce.9
where the time goes:
time: 2210 us; the launch traced here: 2200 us
  waiting for transfers between devices  1370 us (62%)
  matrix products  496 us (22%)
  local copies, waits for them, and re-layouts  125 us (6%)
  blocking collectives  97.8 us (4%)
  other arithmetic  92.1 us (4%)
    psum x1, waiting for transfers between devices, local(): lax.psum(part_ada.astype(jnp.bfloat16), 'row').astype(jnp.float32)  264 us
    all_gather x1, waiting for transfers between devices, local(): pieces = lax.all_gather(key_value, 'row', axis=1, tiled=True)  230 us
    reduce_scatter x1, waiting for transfers between devices, local(): lax.psum_scatter(piece_kv.astype(jnp.bfloat16), 'row', scatter_dimension=...  162 us
    reduce_scatter x1, waiting for transfers between devices, local(): lax.psum_scatter(grad_ada.astype(jnp.bfloat16), 'img', scatter_dimension=...  117 us
    dot_general x8, matrix products, matmul(): return jnp.dot(left_side, right_side, preferred_element_type=jnp.float32)  93.7 us
    dot_general x8, matrix products, transposed(): lax.dot_general(left_side, right_side, (((left_side.ndim - 1,), (1,)), ((...  93.2 us
    reduce_scatter x1, waiting for transfers between devices, local(): lax.psum_scatter(grad_up.astype(jnp.bfloat16), 'img', scatter_dimension=0...  85.6 us
    reduce_scatter x1, waiting for transfers between devices, local(): lax.psum_scatter(grad_down.astype(jnp.bfloat16), 'img', scatter_dimension...  85.6 us
  transfers between devices with their start and end apart: 20, of which 16 were waited for; matrix products, arithmetic and copies ran while one was open for 16% of the time, Pallas kernels for 0%

commit v1 on v0

v1 whole, which is shorter than its diff:
```python
import functools

import jax
import jax.numpy as jnp
from jax import lax
from jax.experimental import pallas as pl
from jax.experimental.pallas import tpu as pltpu
from jax.sharding import PartitionSpec as P

HEADS = 16
HDIM = 72
RW = 32
LROWS = 32
TOTAL = LROWS * RW
SCALE = HDIM ** (-0.5)
LAST = (((1,), (1,)), ((), ()))
FIRST = (((0,), (0,)), ((), ()))


def normalize(operand):
    centre = operand - jnp.mean(operand, axis=-1, keepdims=True)
    return centre * lax.rsqrt(jnp.mean(centre * centre, axis=-1, keepdims=True) + 1e-06)


def modulate(operand, shift_row, scale_row):
    return normalize(operand) * (1.0 + scale_row) + shift_row


def alignment(projected, targets):
    unit_proj = projected * lax.rsqrt(
        jnp.mean(projected * projected, axis=-1, keepdims=True) + 1e-06
    )
    unit_target = targets * lax.rsqrt(jnp.mean(targets * targets, axis=-1, keepdims=True) + 1e-06)
    return jnp.mean(unit_proj * unit_target, axis=-1)


def matmul(left_side, right_side):
    return jnp.dot(left_side, right_side, preferred_element_type=jnp.float32)


def transposed(left_side, right_side):
    return lax.dot_general(left_side, right_side, LAST, preferred_element_type=jnp.float32)


def weight_grad(left_side, right_side):
    return lax.dot_general(left_side, right_side, FIRST, preferred_element_type=jnp.float32)


def silu_back(operand, gradient):
    return jax.vjp(jax.nn.silu, operand)[1](gradient)[0]


def gelu_tanh(operand):
    return jax.nn.gelu(operand, approximate=True)


def gelu_back(operand, gradient):
    return jax.vjp(gelu_tanh, operand)[1](gradient)[0]


def attend_kernel(q_ref, k_ref, v_ref, o_ref, lse_ref):
    length = q_ref.shape[1]
    block = min(256, length)
    keys, values = k_ref[0], v_ref[0]
    for at in range(0, length, block):
        rows = pl.ds(at, block)
        scores = lax.dot_general(q_ref[0, rows, :], keys, LAST, preferred_element_type=jnp.float32)
        scores = scores * SCALE
        top = jnp.max(scores, axis=1, keepdims=True)
        weight = jnp.exp(scores - top)
        total = jnp.sum(weight, axis=1, keepdims=True)
        mixed = jnp.dot(weight.astype(jnp.bfloat16), values, preferred_element_type=jnp.float32)
        o_ref[0, rows, :] = (mixed / total).astype(o_ref.dtype)
        log_total = jnp.broadcast_to(top + jnp.log(total), (block, 128))
        lse_ref[0, :, rows] = log_total.T[:1, :]


def attend(queries, keys, values):
    heads, length, width = queries.shape
    span = keys.shape[1]
    return pl.pallas_call(
        attend_kernel,
        grid=(heads,),
        in_specs=[
            pl.BlockSpec((1, length, width), lambda h: (h, 0, 0)),
            pl.BlockSpec((1, span, width), lambda h: (h, 0, 0)),
            pl.BlockSpec((1, span, width), lambda h: (h, 0, 0)),
        ],
        out_specs=[
            pl.BlockSpec((1, length, width), lambda h: (h, 0, 0)),
            pl.BlockSpec((1, 1, length), lambda h: (h, 0, 0)),
        ],
        out_shape=[
            jax.ShapeDtypeStruct((heads, length, width), jnp.bfloat16),
            jax.ShapeDtypeStruct((heads, 1, length), jnp.float32),
        ],
        compiler_params=pltpu.CompilerParams(vmem_limit_bytes=48 * 1024 * 1024),
        cost_estimate=pl.CostEstimate(
            flops=4 * heads * length * span * 256,
            bytes_accessed=4 * heads * (length + span) * 128,
            transcendentals=heads * length * span,
        ),
        name="attend",
    )(queries, keys, values)


def attend_back_kernel(q_ref, k_ref, v_ref, o_ref, d_ref, lse_ref, dq_ref, dk_ref, dv_ref):
    length, width = q_ref.shape[1], q_ref.shape[2]
    span = k_ref.shape[1]
    block = 256
    queries, d_mix = q_ref[0], d_ref[0]
    product = d_mix.astype(jnp.float32) * o_ref[0].astype(jnp.float32)
    delta = lax.dot_general(
        jnp.ones((8, width), jnp.float32),
        product,
        LAST,
        precision=lax.Precision.HIGHEST,
        preferred_element_type=jnp.float32,
    )[:1, :]
    log_total = lse_ref[0]
    d_query = jnp.zeros((length, width), jnp.float32)
    for at in range(0, span, block):
        rows = pl.ds(at, block)
        keys, values = k_ref[0, rows, :], v_ref[0, rows, :]
        scores = lax.dot_general(keys, queries, LAST, preferred_element_type=jnp.float32) * SCALE
        prob = jnp.exp(scores - log_total)
        d_prob = lax.dot_general(values, d_mix, LAST, preferred_element_type=jnp.float32)
        d_score = (prob * (d_prob - delta)).astype(jnp.bfloat16)
        dv_ref[0, rows, :] = jnp.dot(
            prob.astype(jnp.bfloat16), d_mix, preferred_element_type=jnp.float32
        ).astype(dv_ref.dtype)
        dk_ref[0, rows, :] = (
            jnp.dot(d_score, queries, preferred_element_type=jnp.float32) * SCALE
        ).astype(dk_ref.dtype)
        d_query += lax.dot_general(d_score, keys, FIRST, preferred_element_type=jnp.float32)
    dq_ref[0] = (d_query * SCALE).astype(dq_ref.dtype)


def attend_back(queries, keys, values, mixed, d_mix, log_total):
    heads, length, width = queries.shape
    span = keys.shape[1]
    short = pl.BlockSpec((1, length, width), lambda h: (h, 0, 0))
    long = pl.BlockSpec((1, span, width), lambda h: (h, 0, 0))
    return pl.pallas_call(
        attend_back_kernel,
        grid=(heads,),
        in_specs=[
            short,
            long,
            long,
            short,
            short,
            pl.BlockSpec((1, 1, length), lambda h: (h, 0, 0)),
        ],
        out_specs=[short, long, long],
        out_shape=[
            jax.ShapeDtypeStruct((heads, length, width), jnp.bfloat16),
            jax.ShapeDtypeStruct((heads, span, width), jnp.bfloat16),
            jax.ShapeDtypeStruct((heads, span, width), jnp.bfloat16),
        ],
        compiler_params=pltpu.CompilerParams(vmem_limit_bytes=48 * 1024 * 1024),
        cost_estimate=pl.CostEstimate(
            flops=10 * heads * length * span * 256,
            bytes_accessed=10 * heads * (length + span) * 128,
            transcendentals=heads * length * span,
        ),
        name="attend_back",
    )(queries, keys, values, mixed, d_mix, log_total)


def split_heads(operand):
    return operand.reshape(operand.shape[0], HEADS, HDIM).transpose(1, 0, 2)


def join_heads(operand):
    return operand.transpose(1, 0, 2).reshape(operand.shape[1], HEADS * HDIM)


def local(
    n_img,
    n_row,
    tokens,
    cotangent,
    targets,
    time_table,
    ada_weight,
    ada_bias,
    qkv_weight,
    out_weight,
    up_weight,
    up_bias,
    down_weight,
    proj_first,
    proj_second,
    proj_third,
    time_bins,
    image_order,
    counts,
):
    f32, bf16 = jnp.float32, jnp.bfloat16
    per, slot_len, width = tokens.shape
    column = 2 * per
    group = n_row // column
    length = TOTAL // (2 * group)
    n_images = time_bins.shape[0]
    img_rank, row_rank = lax.axis_index("img"), lax.axis_index("row")
    core = img_rank % 2
    place = row_rank // group
    receives = place // per == core

    def swap(operand, axis, bit):
        size = n_img if axis == "img" else n_row
        return lax.ppermute(operand, axis, [(at, at ^ bit) for at in range(size)])

    def route(shift, back):
        pairs = [
            (img * n_row + (row + shift) % n_row, img * n_row + row)
            for img in range(n_img)
            for row in range(n_row)
            if (row // group) // per == img % 2
        ]
        return [(b, a) for a, b in pairs] if back else pairs

    own_counts = lax.dynamic_index_in_dim(counts, place % per, 0, keepdims=False)
    first_of = (jnp.cumsum(own_counts) - own_counts) * RW
    position = jnp.arange(slot_len)
    kept = (row_rank % group) * 2 * length + jnp.arange(2 * length)
    picks = []
    for shift in range(n_row):
        source_row = (row_rank + shift) % n_row
        begin = lax.dynamic_index_in_dim(first_of, source_row, 0, keepdims=False)
        limit = lax.dynamic_index_in_dim(own_counts, source_row, 0, keepdims=False) * RW
        hit = (kept[:, None] == begin + position[None, :]) & (position[None, :] < limit)
        picks.append(hit)
    pick = jnp.concatenate(picks, axis=1).astype(bf16)

    def image_of(shift):
        return (((row_rank - shift) % n_row) // group) % per

    def bring(operand):
        pieces = []
        for shift in range(n_row):
            piece = lax.dynamic_index_in_dim(operand, image_of(shift), 0, keepdims=False)
            if shift:
                piece = lax.ppermute(piece, ("img", "row"), route(shift, False))
            pieces.append(piece)
        packed = matmul(pick, jnp.concatenate(pieces, axis=0)).astype(bf16)
        own = lax.dynamic_slice_in_dim(packed, core * length, length, 0)
        other = lax.dynamic_slice_in_dim(packed, (1 - core) * length, length, 0)
        return jnp.where(receives, own, swap(other, "img", 1))

    def give(operand):
        other = swap(operand, "img", 1)
        both = jnp.where(
            core == 0,
            jnp.concatenate([operand, other], axis=0),
            jnp.concatenate([other, operand], axis=0),
        )
        spread = weight_grad(pick, both).astype(bf16)
        images = [jnp.zeros((slot_len, operand.shape[1]), bf16) for _ in range(per)]
        for shift in range(n_row):
            piece = spread[shift * slot_len : (shift + 1) * slot_len]
            if shift:
                piece = lax.ppermute(piece, ("img", "row"), route(shift, True))
            else:
                piece = jnp.where(receives, piece, jnp.zeros_like(piece))
            images = [
                image + jnp.where(image_of(shift) == at, piece, jnp.zeros_like(piece))
                for at, image in enumerate(images)
            ]
        return jnp.stack(images)

    def fetch(operand):
        return lax.all_gather(operand, "img", axis=0, tiled=True)

    order = lax.all_gather(image_order, "img", axis=0, tiled=True)
    chosen = jnp.sum(
        jnp.where(order[:, None] == jnp.arange(n_images)[None, :], time_bins[None, :], 0), axis=1
    )
    select = (chosen[:, None] == jnp.arange(time_table.shape[0])[None, :]).astype(f32)
    condition = jnp.dot(select, time_table.astype(f32), precision=lax.Precision.HIGHEST)
    silu_cond = jax.nn.silu(condition).astype(bf16)
    row_cond = lax.dynamic_index_in_dim(
        silu_cond.reshape(n_img // 2, column, -1), place, 1, keepdims=False
    )
    mod_width = ada_weight.shape[1]
    ff_width = up_weight.shape[1]
    bias_part = lax.dynamic_update_slice(
        jnp.zeros((mod_width,), f32), ada_bias.astype(f32), (img_rank * ada_bias.shape[0],)
    )
    up_bias_part = lax.dynamic_update_slice(
        jnp.zeros((ff_width,), f32), up_bias.astype(f32), (img_rank * up_bias.shape[0],)
    )
    mod_part = matmul(row_cond, ada_weight) + bias_part[None, :]
    summed_rows = lax.psum(jnp.concatenate([mod_part.reshape(-1), up_bias_part]), "img")
    modulation = lax.dynamic_index_in_dim(
        summed_rows[: (n_img // 2) * mod_width].reshape(n_img // 2, mod_width),
        img_rank // 2,
        0,
        keepdims=True,
    )
    up_bias_full = summed_rows[(n_img // 2) * mod_width :]
    shift_att, scale_att, gate_att, shift_mlp, scale_mlp, gate_mlp = jnp.split(
        modulation, 6, axis=1
    )

    qkv_full = fetch(qkv_weight)
    out_full = fetch(out_weight)
    up_full = fetch(up_weight)
    down_full = fetch(down_weight)
    first_full = fetch(proj_first)
    second_full = fetch(proj_second)
    third_full = fetch(proj_third)

    source = bring(tokens).astype(f32)
    outside = bring(jnp.concatenate([cotangent, targets], axis=2))
    own_cotangent = outside[:, :width].astype(f32)
    own_targets = outside[:, width:].astype(f32)

    h_att = modulate(source, shift_att, scale_att).astype(bf16)
    qkv_rows = matmul(h_att, qkv_full).astype(bf16)
    key_value = qkv_rows[:, width:]
    key_value = jnp.concatenate([key_value, swap(key_value, "img", 1)], axis=0)
    bits = [1 << at for at in range(group.bit_length() - 1)]
    for bit in bits:
        key_value = jnp.concatenate([key_value, swap(key_value, "row", bit)], axis=0)
    queries = split_heads(qkv_rows[:, :width])
    keys = split_heads(key_value[:, :width])
    values = split_heads(key_value[:, width:])
    mixed, log_total = attend(queries, keys, values)
    head_mix = join_heads(mixed)
    attn_out = matmul(head_mix, out_full)
    residual = source + gate_att * attn_out
    h_mlp = modulate(residual, shift_mlp, scale_mlp).astype(bf16)
    pre_act = matmul(h_mlp, up_full) + up_bias_full
    gelu_out = gelu_tanh(pre_act).astype(bf16)
    mlp_out = matmul(gelu_out, down_full)
    block_own = (residual + gate_mlp * mlp_out).astype(bf16)
    block_out = give(block_own)
    lin_one = matmul(block_own, first_full)
    hid_one = jax.nn.silu(lin_one).astype(bf16)
    lin_two = matmul(hid_one, second_full)
    hid_two = jax.nn.silu(lin_two).astype(bf16)
    projected = matmul(hid_two, third_full)

    def align_loss(operand):
        return -0.5 * jnp.sum(alignment(operand, own_targets))

    def scatter(grad):
        part = lax.psum_scatter(grad.astype(bf16), "img", scatter_dimension=0, tiled=True)
        part = part.astype(f32)
        for at in range(n_row.bit_length() - 1):
            part = part + swap(part.astype(bf16), "row", 1 << at).astype(f32)
        return part

    d_proj = jax.vjp(align_loss, projected)[1](jnp.ones((), f32))[0].astype(bf16)
    grad_third = scatter(weight_grad(hid_two, d_proj))
    d_lin_two = silu_back(lin_two, transposed(d_proj, third_full)).astype(bf16)
    grad_second = scatter(weight_grad(hid_one, d_lin_two))
    d_lin_one = silu_back(lin_one, transposed(d_lin_two, second_full)).astype(bf16)
    grad_first = scatter(weight_grad(block_own, d_lin_one))
    d_res = own_cotangent + transposed(d_lin_one, first_full)
    d_gate_mlp = jnp.sum(d_res * mlp_out, axis=0)
    d_mlp = (d_res * gate_mlp).astype(bf16)
    grad_down = scatter(weight_grad(gelu_out, d_mlp))
    d_pre = gelu_back(pre_act, transposed(d_mlp, down_full)).astype(bf16)
    bias_sum = jnp.sum(d_pre.astype(f32), axis=0)
    grad_up = scatter(weight_grad(h_mlp, d_pre))
    d_resid_norm, d_shift_mlp, d_scale_mlp = jax.vjp(modulate, residual, shift_mlp, scale_mlp)[1](
        transposed(d_pre, up_full)
    )
    d_residual = d_res + d_resid_norm
    d_gate_att = jnp.sum(d_residual * attn_out, axis=0)
    d_attn = (d_residual * gate_att).astype(bf16)
    grad_out = scatter(weight_grad(head_mix, d_attn))
    d_mixed = transposed(d_attn, out_full).astype(bf16)
    d_query, d_key, d_value = attend_back(
        queries, keys, values, mixed, split_heads(d_mixed), log_total
    )
    d_key_value = jnp.concatenate([join_heads(d_key), join_heads(d_value)], axis=1)
    for axis, bit in [("row", bit) for bit in reversed(bits)] + [("img", 1)]:
        half = d_key_value.shape[0] // 2
        arrived = swap(d_key_value[half:], axis, bit)
        d_key_value = (d_key_value[:half].astype(f32) + arrived.astype(f32)).astype(bf16)
    d_qkv = jnp.concatenate([join_heads(d_query), d_key_value], axis=1)
    grad_qkv = scatter(weight_grad(h_att, d_qkv))
    d_source, d_shift_att, d_scale_att = jax.vjp(modulate, source, shift_att, scale_att)[1](
        transposed(d_qkv, qkv_full)
    )
    grad_tokens = give((d_residual + d_source).astype(bf16))

    own_mod = jnp.concatenate(
        [d_shift_att[0], d_scale_att[0], d_gate_att, d_shift_mlp[0], d_scale_mlp[0], d_gate_mlp]
    )[None, :]
    own_mod = own_mod + swap(own_mod, "img", 1)
    for bit in bits:
        own_mod = own_mod + swap(own_mod, "row", bit)
    own_mod = own_mod.astype(bf16)
    column_mod = lax.all_gather(own_mod, "row", axis=0, tiled=True)[::group]
    same_core = [[2 * at + side for at in range(n_img // 2)] for side in range(2)]
    d_mod = lax.all_gather(
        column_mod, "img", axis=0, tiled=True, axis_index_groups=same_core
    )
    grad_ada = weight_grad(silu_cond, d_mod)
    grad_ada_bias = jnp.sum(
        lax.dynamic_slice_in_dim(d_mod, img_rank * ada_bias.shape[0], ada_bias.shape[0], 1).astype(
            f32
        ),
        axis=0,
    )
    d_cond = silu_back(condition, transposed(d_mod, ada_weight))
    grad_table = jnp.dot(select.T, d_cond, precision=lax.Precision.HIGHEST)
    grad_up_bias = lax.dynamic_slice_in_dim(
        lax.psum(bias_sum, ("img", "row")), img_rank * up_bias.shape[0], up_bias.shape[0], 0
    )
    return (
        block_out,
        grad_tokens,
        grad_table,
        grad_ada,
        grad_ada_bias,
        grad_qkv,
        grad_out,
        grad_up,
        grad_up_bias,
        grad_down,
        grad_first,
        grad_second,
        grad_third,
    )


def solution(mesh):
    return jax.shard_map(
        functools.partial(local, mesh.shape["img"], mesh.shape["row"]),
        mesh=mesh,
        in_specs=(
            P("img", "row", None),
            P("img", "row", None),
            P("img", "row", None),
            P(None, "img"),
            P("img", None),
            P("img"),
            P("img", None),
            P("img", None),
            P("img", None),
            P("img"),
            P("img", None),
            P("img", None),
            P("img", None),
            P("img", None),
            P(),
            P("img"),
            P("img", None),
        ),
        out_specs=(
            P("img", "row", None),
            P("img", "row", None),
            P(None, "img"),
            P("img", None),
            P("img"),
            P("img", None),
            P("img", None),
            P("img", None),
            P("img"),
            P("img", None),
            P("img", None),
            P("img", None),
            P("img", None),
        ),
        check_vma=False,
    )
```

time: 2210 us -> 1140 us (0.52)
  waiting for transfers between devices: 1370 us -> 515 us
  matrix products: 496 us -> 229 us
  starting transfers between devices: 1.27 us -> 71.1 us
  Pallas kernels: 0 us -> 54.2 us
  local copies, waits for them, and re-layouts: 125 us -> 90.3 us
  other arithmetic: 92.1 us -> 69.4 us
    reduce_scatter x9 -> x7, waiting for transfers between devices: 685 us -> 51.3 us  [scatter(): lax.psum_scatter(grad.astype(bf16), 'img', scatter_dimension=0, tiled=True)]
    ppermute x0 -> x33, waiting for transfers between devices: none -> 307 us  [the longest x21 246 us: swap(): return lax.ppermute(operand, axis, [(at, at ^ bit) for at in range(size)])]
    all_gather x9 -> x7, waiting for transfers between devices: 406 us -> 143 us  [fetch(): return lax.all_gather(operand, 'img', axis=0, tiled=True)]
    dot_general x31 -> x19, matrix products: 402 us -> 145 us  [the longest x10 77.3 us: weight_grad(): lax.dot_general(left_side, right_side, FIRST, preferred_element_type=jnp....]
    psum x1, waiting for transfers between devices: 264 us -> 10.7 us  [local(): lax.psum(jnp.concatenate([mod_part.reshape(-1), up_bias_part]), 'img')]
    ppermute x0 -> x33, starting transfers between devices: none -> 70.2 us  [the longest x21 40.9 us: swap(): return lax.ppermute(operand, axis, [(at, at ^ bit) for at in range(size)])]
    pallas_call x0 -> x2, Pallas kernels: none -> 54.2 us  [the longest x1 32.2 us: attend_back(): pl.pallas_call(attend_back_kernel, grid=(heads,), in_specs=[short, long,...]
    reduce_sum x10 -> x4, other arithmetic: 48.8 us -> 3.51 us  [the longest x1 1.13 us: modulate(): return normalize(operand) * (1.0 + scale_row) + shift_row]
  transfers between devices with their start and end apart: 20 -> 48, of which waited for: 16 -> 18; matrix products, arithmetic and copies ran while one was open for 16% -> 26% of each run, Pallas kernels for 0% -> 5%
where the time goes in v1:
time: 1140 us
  waiting for transfers between devices  515 us (45%)
  matrix products  229 us (20%)
  local copies, waits for them, and re-layouts  90.3 us (8%)
  blocking collectives  88.9 us (8%)
  starting transfers between devices  71.1 us (6%)
  other arithmetic  69.4 us (6%)
  Pallas kernels  54.2 us (5%)
  between operations  18.8 us (2%)
    ppermute x21, waiting for transfers between devices, swap(): return lax.ppermute(operand, axis, [(at, at ^ bit) for at in range(size)])  246 us
    all_gather x7, waiting for transfers between devices, fetch(): return lax.all_gather(operand, 'img', axis=0, tiled=True)  143 us
    dot_general x10, matrix products, matmul(): return jnp.dot(left_side, right_side, preferred_element_type=jnp.float32)  82.4 us
    dot_general x10, matrix products, weight_grad(): lax.dot_general(left_side, right_side, FIRST, preferred_element_type=jnp....  77.3 us
    dot_general x8, matrix products, transposed(): lax.dot_general(left_side, right_side, LAST, preferred_element_type=jnp.f...  66.5 us
    ppermute x6, waiting for transfers between devices, bring(): piece = lax.ppermute(piece, ('img', 'row'), route(shift, False))  60.8 us
    psum x1, blocking collectives, local(): lax.psum(bias_sum, ('img', 'row'))  56.2 us
    reduce_scatter x7, waiting for transfers between devices, scatter(): lax.psum_scatter(grad.astype(bf16), 'img', scatter_dimension=0, tiled=True)  51.3 us
  transfers between devices with their start and end apart: 48, of which 18 were waited for; matrix products, arithmetic and copies ran while one was open for 26% of the time, Pallas kernels for 5%

profile of v1, /device:TPU:0, one launch (start us, length us, event | category | flops | bytes accessed | tf_op | source)
XLA Modules:
  0.0 1136.7 jit_solution(13585398648064993822)
XLA Ops:
  10.1 9.5 all-reduce
  66.2 10.7 all-reduce.3.cloned.1.call-done
  81.0 43.3 %collective-permute-done.1 = bf16[384,1152]{1,0:T(8,128)(2,1)} collective-permute-done((bf16[384,1152]{1,0:T(8,128)(2,1)}, bf16[384,1152]{1,0:T(8,128)(2,1)}, u32[]{:S(2)}, u32[]{:S(2)}) %collective-permute-start.1) | collective-permute-done | bytes 884768 | tf_op jit(solution)/shard_map/ppermute | solution.py:245
  152.2 9.2 convolution_convert_fusion.8
  203.3 22.1 %attend.1 = (bf16[16,512,72]{2,1,0:T(8,128)(2,1)S(1)}, f32[16,1,512]{2,1,0:T(1,128)S(1)}) custom-call(bf16[16,512,72]{2,1,0:T(8,128)(2,1)S(1)} %bitcast.99, bf16[16,1024,72]{2,1,0:T(8,128)(2,1)} %bitcast.113, bf16[16,1024,72]{2,1,0:T(8,128)(2,1)} %bitcast.115), custom_call_target="tpu_custom_call" | custom-call | flops 8589934592 | bytes 12582912 | tf_op jit(solution)/shard_map/attend/pallas_call | solution.py:81
  237.7 13.1 %fusion.103 = f32[512,4608]{1,0:T(8,128)} fusion(bf16[1152,4608]{1,0:T(8,128)(2,1)} %all-gather.14.cloned.1.call-done, f32[512,1152]{1,0:T(8,128)} %copy-done.7, f32[1152]{0:T(1024)S(1)} %get-tuple-element.36, f32[1152]{0:T(1024)S(1)} %get-tuple-element.32, f32[512]{0:T(512)S(1)} %fusion.90, f32[512]{0:T(512)S(1)} %broadcast_multiply_fusion), kind=kOutput, calls=%fused_computation.241 | convolution fusion | flops 5438767104 | bytes 22426624 | tf_op jit(solution)/shard_map/dot_general | solution.py:38
  250.8 44.5 %all-gather.16.cloned.1.call-done = bf16[4608,1152]{1,0:T(8,128)(2,1)} async-done(((bf16[576,1152]{1,0:T(8,128)(2,1)}), bf16[4608,1152]{1,0:T(8,128)(2,1)}) %all-gather.16.cloned.1.call-update) | async-done | bytes 10616848 | tf_op jit(solution)/shard_map/all_gather | solution.py:274
  295.3 14.2 %add_convert_fusion.2 = (bf16[512,1152]{1,0:T(8,128)(2,1)S(1)}, f32[512,1152]{1,0:T(8,128)}) fusion(f32[512,1152]{1,0:T(8,128)} %copy-done.7, f32[1152]{0:T(1024)S(1)} %get-tuple-element.31, bf16[4608,1152]{1,0:T(8,128)(2,1)} %all-gather.16.cloned.1.call-done, f32[512,4608]{1,0:T(8,128)} %fusion.103, f32[4608]{0:T(1024)S(1)} %slice.77), kind=kOutput, calls=%fused_computation.107 | convolution fusion | flops 5461180416 | bytes 25975296 | tf_op jit(solution)/shard_map/dot_general | solution.py:38
  309.5 26.7 %all-gather.18.cloned.1.call-done = bf16[1152,2048]{1,0:T(8,128)(2,1)} async-done(((bf16[144,2048]{1,0:T(8,128)(2,1)}), bf16[1152,2048]{1,0:T(8,128)(2,1)}) %all-gather.18.cloned.1.call-update) | async-done | bytes 4718608 | tf_op jit(solution)/shard_map/all_gather | solution.py:274
  343.2 49.5 %all-gather.20.cloned.1.call-done = bf16[2048,2048]{1,0:T(8,128)(2,1)} async-done(((bf16[256,2048]{1,0:T(8,128)(2,1)}), bf16[2048,2048]{1,0:T(8,128)(2,1)}) %all-gather.20.cloned.1.call-update) | async-done | bytes 8388624 | tf_op jit(solution)/shard_map/all_gather | solution.py:274
  392.6 12.4 %multiply_convert_fusion.1 = (bf16[512,2048]{1,0:T(8,128)(2,1)}, f32[512,2048]{1,0:T(8,128)}) fusion(bf16[2048,2048]{1,0:T(8,128)(2,1)} %all-gather.20.cloned.1.call-done, f32[512,2048]{1,0:T(8,128)} %fusion.118), kind=kOutput, calls=%fused_computation.43 | convolution fusion | flops 4305453056 | bytes 18874368 | tf_op jit(solution)/shard_map/dot_general | solution.py:38
  405.0 22.0 %all-gather.22.cloned.1.call-done = bf16[2048,768]{1,0:T(8,128)(2,1)} async-done(((bf16[256,768]{1,0:T(8,128)(2,1)}), bf16[2048,768]{1,0:T(8,128)(2,1)}) %all-gather.22.cloned.1.call-update) | async-done | bytes 3145744 | tf_op jit(solution)/shard_map/all_gather | solution.py:274
  437.7 9.1 fusion.20
  454.0 16.3 %convert_reduce_fusion = (f32[4608]{0:T(1024)S(1)}, bf16[512,4608]{1,0:T(8,128)(2,1)S(1)}) fusion(f32[512,4608]{1,0:T(8,128)} %fusion.103, f32[4608]{0:T(1024)S(1)} %slice.77, bf16[512,1152]{1,0:T(8,128)(2,1)S(1)} %get-tuple-element.86, bf16[4608,1152]{1,0:T(8,128)(2,1)} %all-gather.16.cloned.1.call-done), kind=kOutput, calls=%fused_computation.12 | convolution fusion | flops 5490077184 | bytes 25989120 | tf_op jit(solution)/shard_map/dot_general | solution.py:42
  470.4 13.7 %multiply_reduce_fusion.1 = (f32[1152]{0:T(1024)S(1)}, f32[512]{0:T(512)S(1)}, f32[1152]{0:T(1024)S(1)}, f32[512,1152]{1,0:T(8,128)}) fusion(f32[512,1152]{1,0:T(8,128)S(1)} %copy-done.8, f32[512]{0:T(512)S(1)} %fusion.90, f32[512]{0:T(512)S(1)} %broadcast_multiply_fusion, f32[1152]{0:T(1024)S(1)} %get-tuple-element.32, ...), kind=kOutput, calls=%fused_computation.99 | convolution fusion | flops 5440534016 | bytes 20073984 | tf_op jit(solution)/shard_map/dot_general | solution.py:42
  506.5 10.8 convolution_convert_fusion.3
  528.4 32.2 %attend_back.1 = (bf16[16,512,72]{2,1,0:T(8,128)(2,1)S(1)}, bf16[16,1024,72]{2,1,0:T(8,128)(2,1)}, bf16[16,1024,72]{2,1,0:T(8,128)(2,1)}) custom-call(bf16[16,512,72]{2,1,0:T(8,128)(2,1)S(1)} %bitcast.100, bf16[16,1024,72]{2,1,0:T(8,128)(2,1)} %bitcast.114, bf16[16,1024,72]{2,1,0:T(8,128)(2,1)} %bitcast.116, bf16[16,512,72]{2,1,0:T(8,128)(2,1)} %copy-done.3, ...), custom_call_target="tpu_custom_call" | custom-call | flops 21474836480 | bytes 31457280 | tf_op jit(solution)/shard_map/attend_back/pallas_call | solution.py:144
  595.2 13.5 %convolution_convert_fusion = bf16[4608,1152]{1,0:T(8,128)(2,1)} fusion(bf16[512,1152]{1,0:T(8,128)(2,1)} %copy-done.66, f32[512,4608]{1,0:T(8,128)} %fusion.103, f32[4608]{0:T(1024)S(1)} %slice.77), kind=kOutput, calls=%fused_computation | convolution fusion | flops 5464719360 | bytes 21252096 | tf_op jit(solution)/shard_map/dot_general | solution.py:46
  609.4 11.1 convolution_convert_fusion.1
  639.2 56.2 %psum.15 = f32[4608]{0:T(1024)S(1)} all-reduce(f32[4608]{0:T(1024)S(1)} %get-tuple-element.37), channel_id=1, replica_groups=mesh['img'=8,'row'=4] {'img','row'}, use_global_device_ids=true, to_apply=%region_25.26 | all-reduce | flops 4608 | bytes 36864 | tf_op jit(solution)/shard_map/psum | solution.py:414
  713.5 13.3 %all-gather = bf16[4,1,6912]{2,1,0:T(2,128)(2,1)S(1)} all-gather(bf16[1,1,6912]{2,1,0:T(2,128)(2,1)S(1)} %convert_bitcast_fusion), channel_id=1, replica_groups=mesh['img'=8,'row'=4] {'row'}, dimensions={0}, use_global_device_ids=true | all-gather | bytes 69120 | tf_op jit(solution)/shard_map/all_gather | solution.py:399
  726.8 9.9 all-gather.1
  762.2 23.0 %collective-permute-done.21 = bf16[144,1152]{1,0:T(8,128)(2,1)S(1)} collective-permute-done((bf16[144,1152]{1,0:T(8,128)(2,1)}, bf16[144,1152]{1,0:T(8,128)(2,1)S(1)}, u32[]{:S(2)}, u32[]{:S(2)}) %collective-permute-start.21) | collective-permute-done | bytes 331808 | tf_op jit(solution)/shard_map/ppermute | solution.py:213
  791.6 12.8 %collective-permute-start.29 = (bf16[256,2048]{1,0:T(8,128)(2,1)}, bf16[256,2048]{1,0:T(8,128)(2,1)S(1)}, u32[]{:S(2)}, u32[]{:S(2)}) collective-permute-start(bf16[256,2048]{1,0:T(8,128)(2,1)} %reduce-scatter.18.cloned.1.call-done), channel_id=1, source_target_pairs={{0,1},{1,0},{2,3},{3,2},{4,5},{5,4},{6,7},{7,6},{8,9},{9,8},{10,11... | collective-permute-start | bytes 3145736 | tf_op jit(solution)/shard_map/ppermute | solution.py:213
  814.0 12.5 %collective-permute-done.27 = bf16[144,2048]{1,0:T(8,128)(2,1)} collective-permute-done((bf16[144,2048]{1,0:T(8,128)(2,1)}, bf16[144,2048]{1,0:T(8,128)(2,1)}, u32[]{:S(2)}, u32[]{:S(2)}) %collective-permute-start.27) | collective-permute-done | bytes 589856 | tf_op jit(solution)/shard_map/ppermute | solution.py:213
  831.7 22.9 %collective-permute-done.29 = bf16[256,2048]{1,0:T(8,128)(2,1)S(1)} collective-permute-done((bf16[256,2048]{1,0:T(8,128)(2,1)}, bf16[256,2048]{1,0:T(8,128)(2,1)S(1)}, u32[]{:S(2)}, u32[]{:S(2)}) %collective-permute-start.29) | collective-permute-done | bytes 1048608 | tf_op jit(solution)/shard_map/ppermute | solution.py:213
  866.6 23.2 %collective-permute-done.28 = bf16[144,2048]{1,0:T(8,128)(2,1)} collective-permute-done((bf16[144,2048]{1,0:T(8,128)(2,1)}, bf16[144,2048]{1,0:T(8,128)(2,1)}, u32[]{:S(2)}, u32[]{:S(2)}) %collective-permute-start.28) | collective-permute-done | bytes 589856 | tf_op jit(solution)/shard_map/ppermute | solution.py:213
  894.7 15.9 %collective-permute-done.30 = bf16[256,2048]{1,0:T(8,128)(2,1)} collective-permute-done((bf16[256,2048]{1,0:T(8,128)(2,1)}, bf16[256,2048]{1,0:T(8,128)(2,1)}, u32[]{:S(2)}, u32[]{:S(2)}) %collective-permute-start.30) | collective-permute-done | bytes 1048608 | tf_op jit(solution)/shard_map/ppermute | solution.py:213
  913.9 51.2 %reduce-scatter.12.cloned.1.call-done = bf16[144,4608]{1,0:T(8,128)(2,1)} async-done(((bf16[1152,4608]{1,0:T(8,128)(2,1)}), bf16[144,4608]{1,0:T(8,128)(2,1)}) %reduce-scatter.12.cloned.1.call-update) | async-done | bytes 1327120 | tf_op jit(solution)/shard_map/reduce_scatter | solution.py:350
  973.2 49.7 %collective-permute-done.23 = bf16[144,4608]{1,0:T(8,128)(2,1)S(1)} collective-permute-done((bf16[144,4608]{1,0:T(8,128)(2,1)}, bf16[144,4608]{1,0:T(8,128)(2,1)S(1)}, u32[]{:S(2)}, u32[]{:S(2)}) %collective-permute-start.23) | collective-permute-done | bytes 1327136 | tf_op jit(solution)/shard_map/ppermute | solution.py:213
  1026.6 74.3 %collective-permute-done.26 = bf16[576,1152]{1,0:T(8,128)(2,1)S(1)} collective-permute-done((bf16[576,1152]{1,0:T(8,128)(2,1)S(1)}, bf16[576,1152]{1,0:T(8,128)(2,1)S(1)}, u32[]{:S(2)}, u32[]{:S(2)}) %collective-permute-start.26) | collective-permute-done | bytes 1327136 | tf_op jit(solution)/shard_map/ppermute | solution.py:213
  1104.4 23.6 %collective-permute-done.24 = bf16[144,4608]{1,0:T(8,128)(2,1)S(1)} collective-permute-done((bf16[144,4608]{1,0:T(8,128)(2,1)S(1)}, bf16[144,4608]{1,0:T(8,128)(2,1)S(1)}, u32[]{:S(2)}, u32[]{:S(2)}) %collective-permute-start.24) | collective-permute-done | bytes 1327136 | tf_op jit(solution)/shard_map/ppermute | solution.py:213
  (362 shorter events, 345.7 us)
Async XLA Ops:
  7.2 69.7 %all-reduce.3.cloned.1.call-start = ((), (), s32[]{:S(2)}) async-start(), calls=%async_computation.7 | async-start | bytes 262144 | tf_op jit(solution)/shard_map/psum | solution.py:295
  24.1 128.0 %all-gather.10.cloned.1.call-start = ((), (), s32[]{:S(2)}) async-start(), calls=%async_computation.8 | async-start | bytes 8957952 | tf_op jit(solution)/shard_map/all_gather | solution.py:274
  24.9 205.5 %all-gather.12.cloned.1.call-start = ((), (), s32[]{:S(2)}) async-start(), calls=%async_computation.9 | async-start | bytes 2985984 | tf_op jit(solution)/shard_map/all_gather | solution.py:274
  25.6 212.1 %all-gather.14.cloned.1.call-start = ((), (), s32[]{:S(2)}) async-start(), calls=%async_computation.10 | async-start | bytes 11943936 | tf_op jit(solution)/shard_map/all_gather | solution.py:274
  26.2 269.1 %all-gather.16.cloned.1.call-start = ((), (), s32[]{:S(2)}) async-start(), calls=%async_computation.11 | async-start | bytes 11943936 | tf_op jit(solution)/shard_map/all_gather | solution.py:274
  26.8 309.4 %all-gather.18.cloned.1.call-start = ((), (), s32[]{:S(2)}) async-start(), calls=%async_computation.12 | async-start | bytes 5308416 | tf_op jit(solution)/shard_map/all_gather | solution.py:274
  27.4 365.3 %all-gather.20.cloned.1.call-start = ((), (), s32[]{:S(2)}) async-start(), calls=%async_computation.13 | async-start | bytes 9437184 | tf_op jit(solution)/shard_map/all_gather | solution.py:274
  28.1 398.9 %all-gather.22.cloned.1.call-start = ((), (), s32[]{:S(2)}) async-start(), calls=%async_computation.14 | async-start | bytes 3538944 | tf_op jit(solution)/shard_map/all_gather | solution.py:274
  32.3 99.1 %collective-permute-start.10 = (bf16[384,1920]{1,0:T(8,128)(2,1)}, bf16[384,1920]{1,0:T(8,128)(2,1)}, u32[]{:S(2)}, u32[]{:S(2)}) collective-permute-start(bf16[384,1920]{1,0:T(8,128)(2,1)} %get-tuple-element.62), channel_id=1, source_target_pairs={{2,0},{3,1},{4,6},{5,7},{10,8},{11,9},{12,14},{13,15},{18,16},{19,... | collective-permute-start | bytes 4423688 | tf_op jit(solution)/shard_map/ppermute | solution.py:245
  33.6 97.8 %collective-permute-start.11 = (bf16[384,1920]{1,0:T(8,128)(2,1)}, bf16[384,1920]{1,0:T(8,128)(2,1)}, u32[]{:S(2)}, u32[]{:S(2)}) collective-permute-start(bf16[384,1920]{1,0:T(8,128)(2,1)} %get-tuple-element.61), channel_id=1, source_target_pairs={{3,0},{0,1},{5,6},{6,7},{11,8},{8,9},{13,14},{14,15},{19,16},{16,1... | collective-permute-start | bytes 4423688 | tf_op jit(solution)/shard_map/ppermute | solution.py:245
  40.2 84.1 %collective-permute-start.1 = (bf16[384,1152]{1,0:T(8,128)(2,1)}, bf16[384,1152]{1,0:T(8,128)(2,1)}, u32[]{:S(2)}, u32[]{:S(2)}) collective-permute-start(bf16[384,1152]{1,0:T(8,128)(2,1)} %get-tuple-element.67), channel_id=1, source_target_pairs={{2,0},{3,1},{4,6},{5,7},{10,8},{11,9},{12,14},{13,15},{18,16},{19,... | collective-permute-start | bytes 2654216 | tf_op jit(solution)/shard_map/ppermute | solution.py:245
  41.5 82.8 %collective-permute-start.2 = (bf16[384,1152]{1,0:T(8,128)(2,1)}, bf16[384,1152]{1,0:T(8,128)(2,1)}, u32[]{:S(2)}, u32[]{:S(2)}) collective-permute-start(bf16[384,1152]{1,0:T(8,128)(2,1)} %get-tuple-element.66), channel_id=1, source_target_pairs={{3,0},{0,1},{5,6},{6,7},{11,8},{8,9},{13,14},{14,15},{19,16},{16,1... | collective-permute-start | bytes 2654216 | tf_op jit(solution)/shard_map/ppermute | solution.py:245
  63.2 76.8 %collective-permute-start.9 = (bf16[384,1920]{1,0:T(8,128)(2,1)}, bf16[384,1920]{1,0:T(8,128)(2,1)}, u32[]{:S(2)}, u32[]{:S(2)}) collective-permute-start(bf16[384,1920]{1,0:T(8,128)(2,1)} %get-tuple-element.63), channel_id=1, source_target_pairs={{1,0},{2,1},{7,6},{4,7},{9,8},{10,9},{15,14},{12,15},{17,16},{18,1... | collective-permute-start | bytes 4423688 | tf_op jit(solution)/shard_map/ppermute | solution.py:245
  164.0 590.9 %reduce-scatter.10.cloned.1.call-start = ((), (), s32[]{:S(2)}) async-start(), calls=%async_computation.16 | async-start | bytes 2985984 | tf_op jit(solution)/shard_map/reduce_scatter | solution.py:350
  493.5 292.6 %reduce-scatter.20.cloned.1.call-start = ((), (), s32[]{:S(2)}) async-start(), calls=%async_computation.21 | async-start | bytes 3538944 | tf_op jit(solution)/shard_map/reduce_scatter | solution.py:350
  499.5 287.8 %reduce-scatter.16.cloned.1.call-start = ((), (), s32[]{:S(2)}) async-start(), calls=%async_computation.19 | async-start | bytes 5308416 | tf_op jit(solution)/shard_map/reduce_scatter | solution.py:350
  506.2 285.3 %reduce-scatter.18.cloned.1.call-start = ((), (), s32[]{:S(2)}) async-start(), calls=%async_computation.20 | async-start | bytes 9437184 | tf_op jit(solution)/shard_map/reduce_scatter | solution.py:350
  517.3 346.9 %reduce-scatter.8.cloned.1.call-start = ((), (), s32[]{:S(2)}) async-start(), calls=%async_computation.15 | async-start | bytes 8957952 | tf_op jit(solution)/shard_map/reduce_scatter | solution.py:350
  594.9 297.9 %reduce-scatter.14.cloned.1.call-start = ((), (), s32[]{:S(2)}) async-start(), calls=%async_computation.18 | async-start | bytes 11943936 | tf_op jit(solution)/shard_map/reduce_scatter | solution.py:350
  608.7 356.4 %reduce-scatter.12.cloned.1.call-start = ((), (), s32[]{:S(2)}) async-start(), calls=%async_computation.17 | async-start | bytes 11943936 | tf_op jit(solution)/shard_map/reduce_scatter | solution.py:350
  630.4 65.6 %collective-permute-start.6 = (bf16[384,1152]{1,0:T(8,128)(2,1)}, bf16[384,1152]{1,0:T(8,128)(2,1)}, u32[]{:S(2)}, u32[]{:S(2)}) collective-permute-start(bf16[384,1152]{1,0:T(8,128)(2,1)} %get-tuple-element.57), channel_id=1, source_target_pairs={{0,1},{1,2},{6,7},{7,4},{8,9},{9,10},{14,15},{15,12},{16,17},{17,1... | collective-permute-start | bytes 2654216 | tf_op jit(solution)/shard_map/ppermute | solution.py:264
  634.6 61.4 %collective-permute-start.7 = (bf16[384,1152]{1,0:T(8,128)(2,1)}, bf16[384,1152]{1,0:T(8,128)(2,1)}, u32[]{:S(2)}, u32[]{:S(2)}) collective-permute-start(bf16[384,1152]{1,0:T(8,128)(2,1)} %get-tuple-element.59), channel_id=1, source_target_pairs={{0,2},{1,3},{6,4},{7,5},{8,10},{9,11},{14,12},{15,13},{16,18},{17,... | collective-permute-start | bytes 2654216 | tf_op jit(solution)/shard_map/ppermute | solution.py:264
  636.8 59.2 %collective-permute-start.8 = (bf16[384,1152]{1,0:T(8,128)(2,1)}, bf16[384,1152]{1,0:T(8,128)(2,1)}, u32[]{:S(2)}, u32[]{:S(2)}) collective-permute-start(bf16[384,1152]{1,0:T(8,128)(2,1)} %get-tuple-element.58), channel_id=1, source_target_pairs={{0,3},{1,0},{6,5},{7,6},{8,11},{9,8},{14,13},{15,14},{16,19},{17,1... | collective-permute-start | bytes 2654216 | tf_op jit(solution)/shard_map/ppermute | solution.py:264
  786.0 74.1 %collective-permute-start.22 = (bf16[144,1152]{1,0:T(8,128)(2,1)}, bf16[144,1152]{1,0:T(8,128)(2,1)}, u32[]{:S(2)}, u32[]{:S(2)}) collective-permute-start(bf16[144,1152]{1,0:T(8,128)(2,1)} %fusion.73), channel_id=1, source_target_pairs={{0,2},{1,3},{2,0},{3,1},{4,6},{5,7},{6,4},{7,5},{8,10},{9,11},{10,... | collective-permute-start | bytes 995336 | tf_op jit(solution)/shard_map/ppermute | solution.py:213
  791.6 63.0 %collective-permute-start.29 = (bf16[256,2048]{1,0:T(8,128)(2,1)}, bf16[256,2048]{1,0:T(8,128)(2,1)S(1)}, u32[]{:S(2)}, u32[]{:S(2)}) collective-permute-start(bf16[256,2048]{1,0:T(8,128)(2,1)} %reduce-scatter.18.cloned.1.call-done), channel_id=1, source_target_pairs={{0,1},{1,0},{2,3},{3,2},{4,5},{5,4},{6,7},{7,6},{8,9},{9,8},{10,11... | collective-permute-start | bytes 3145736 | tf_op jit(solution)/shard_map/ppermute | solution.py:213
  828.5 61.3 %collective-permute-start.28 = (bf16[144,2048]{1,0:T(8,128)(2,1)}, bf16[144,2048]{1,0:T(8,128)(2,1)}, u32[]{:S(2)}, u32[]{:S(2)}) collective-permute-start(bf16[144,2048]{1,0:T(8,128)(2,1)} %fusion.71), channel_id=1, source_target_pairs={{0,2},{1,3},{2,0},{3,1},{4,6},{5,7},{6,4},{7,5},{8,10},{9,11},{10,... | collective-permute-start | bytes 1769480 | tf_op jit(solution)/shard_map/ppermute | solution.py:213
  864.2 102.5 %collective-permute-start.19 = (bf16[144,3456]{1,0:T(8,128)(2,1)}, bf16[144,3456]{1,0:T(8,128)(2,1)}, u32[]{:S(2)}, u32[]{:S(2)}) collective-permute-start(bf16[144,3456]{1,0:T(8,128)(2,1)} %reduce-scatter.8.cloned.1.call-done), channel_id=1, source_target_pairs={{0,1},{1,0},{2,3},{3,2},{4,5},{5,4},{6,7},{7,6},{8,9},{9,8},{10,11... | collective-permute-start | bytes 2985992 | tf_op jit(solution)/shard_map/ppermute | solution.py:213
  892.8 78.1 %collective-permute-start.25 = (bf16[576,1152]{1,0:T(8,128)(2,1)}, bf16[576,1152]{1,0:T(8,128)(2,1)}, u32[]{:S(2)}, u32[]{:S(2)}) collective-permute-start(bf16[576,1152]{1,0:T(8,128)(2,1)} %reduce-scatter.14.cloned.1.call-done), channel_id=1, source_target_pairs={{0,1},{1,0},{2,3},{3,2},{4,5},{5,4},{6,7},{7,6},{8,9},{9,8},{10,11... | collective-permute-start | bytes 3981320 | tf_op jit(solution)/shard_map/ppermute | solution.py:213
  965.2 57.7 %collective-permute-start.23 = (bf16[144,4608]{1,0:T(8,128)(2,1)}, bf16[144,4608]{1,0:T(8,128)(2,1)S(1)}, u32[]{:S(2)}, u32[]{:S(2)}) collective-permute-start(bf16[144,4608]{1,0:T(8,128)(2,1)} %reduce-scatter.12.cloned.1.call-done), channel_id=1, source_target_pairs={{0,1},{1,0},{2,3},{3,2},{4,5},{5,4},{6,7},{7,6},{8,9},{9,8},{10,11... | collective-permute-start | bytes 3981320 | tf_op jit(solution)/shard_map/ppermute | solution.py:213
  968.4 55.4 %collective-permute-start.20 = (bf16[144,3456]{1,0:T(8,128)(2,1)S(1)}, bf16[144,3456]{1,0:T(8,128)(2,1)S(1)}, u32[]{:S(2)}, u32[]{:S(2)}) collective-permute-start(bf16[144,3456]{1,0:T(8,128)(2,1)S(1)} %fusion.62), channel_id=1, source_target_pairs={{0,2},{1,3},{2,0},{3,1},{4,6},{5,7},{6,4},{7,5},{8,10},{9,11},{10,... | collective-permute-start | bytes 2985992 | tf_op jit(solution)/shard_map/ppermute | solution.py:213
  972.6 128.4 %collective-permute-start.26 = (bf16[576,1152]{1,0:T(8,128)(2,1)S(1)}, bf16[576,1152]{1,0:T(8,128)(2,1)S(1)}, u32[]{:S(2)}, u32[]{:S(2)}) collective-permute-start(bf16[576,1152]{1,0:T(8,128)(2,1)S(1)} %fusion.38), channel_id=1, source_target_pairs={{0,2},{1,3},{2,0},{3,1},{4,6},{5,7},{6,4},{7,5},{8,10},{9,11},{10,... | collective-permute-start | bytes 3981320 | tf_op jit(solution)/shard_map/ppermute | solution.py:213
  1023.2 104.8 %collective-permute-start.24 = (bf16[144,4608]{1,0:T(8,128)(2,1)S(1)}, bf16[144,4608]{1,0:T(8,128)(2,1)S(1)}, u32[]{:S(2)}, u32[]{:S(2)}) collective-permute-start(bf16[144,4608]{1,0:T(8,128)(2,1)S(1)} %fusion.37), channel_id=1, source_target_pairs={{0,2},{1,3},{2,0},{3,1},{4,6},{5,7},{6,4},{7,5},{8,10},{9,11},{10,... | collective-permute-start | bytes 3981320 | tf_op jit(solution)/shard_map/ppermute | solution.py:213
  (86 other events, 1754.2 us)
Sparse Core Ops, SparseCore 0:
  24.3 52.6 all-reduce.2
  79.0 51.9 all-gather.9
  133.0 30.2 all-gather.11
  165.2 64.3 all-gather.13
  231.5 63.8 all-gather.15
  297.2 38.9 all-gather.17
  338.2 54.3 all-gather.19
  394.7 32.3 all-gather.21
  493.6 43.7 reduce-scatter.9
  540.6 46.2 reduce-scatter.19
  590.7 53.8 reduce-scatter.15
  648.0 71.9 reduce-scatter.17
  723.9 70.0 reduce-scatter.7
  797.4 82.1 reduce-scatter.13
  882.9 82.1 reduce-scatter.11

commit v2 on v1

--- a/solution.py
+++ b/solution.py
@@ -166,6 +166,609 @@
         ),
         name="attend_back",
     )(queries, keys, values, mixed, d_mix, log_total)
+
+
+MESH = pl.DeviceIdType.MESH
+TILE_ROWS = 144
+TILE_COLUMNS = 384
+CUT = 80
+SLOTS = 4
+LINE_SLOTS = 8
+LINE_TILE = 256
+SIDE_PACE = 3
+GIVE_ROWS = 16
+
+
+def add(one, other):
+    return (one.astype(jnp.float32) + other.astype(jnp.float32)).astype(jnp.bfloat16)
+
+
+def mates():
+    me = lax.axis_index("img")
+    core, x, y = lax.rem(me, 2), lax.rem(me // 2, 2), me // 4
+    return me, (core, x, y), (me + 1 - 2 * core, me + 2 - 4 * x, me + 4 - 8 * y)
+
+
+def greet(where):
+    barrier = pltpu.get_barrier_semaphore()
+    pl.semaphore_signal(barrier, inc=1, device_id=where, device_id_type=MESH)
+
+
+def gather_kernel(count, *refs):
+    blocks, wholes = refs[:count], refs[count : 2 * count]
+    send_sem, recv_sem, local_sem = refs[2 * count :]
+    me, (core, x, y), (sibling, x_mate, y_mate) = mates()
+    far = x_mate + 4 - 8 * y
+    for mate in (sibling, x_mate, y_mate):
+        greet({"img": mate})
+    pl.semaphore_wait(pltpu.get_barrier_semaphore(), 3)
+
+    def halves(at):
+        rows = blocks[at].shape[0]
+        cut = (rows // 2 + 15) // 16 * 16
+        return pl.ds(0, cut), pl.ds(cut, rows - cut)
+
+    def copy(at, kind, source, owner, rows, where):
+        return pltpu.make_async_remote_copy(
+            src_ref=source,
+            dst_ref=wholes[at].at[owner, rows, :],
+            send_sem=send_sem.at[at, kind],
+            recv_sem=recv_sem.at[at, kind],
+            device_id={"img": where},
+            device_id_type=MESH,
+        )
+
+    def copies(at):
+        upper, lower = halves(at)
+        block, whole = blocks[at], wholes[at]
+        found = [
+            copy(at, 0, block.at[upper, :], me, upper, x_mate),
+            copy(at, 1, block.at[lower, :], me, lower, y_mate),
+            copy(at, 2, block.at[upper, :], me, upper, y_mate),
+            copy(at, 3, block.at[lower, :], me, lower, x_mate),
+            copy(at, 4, whole.at[x_mate, upper, :], x_mate, upper, y_mate),
+            copy(at, 5, whole.at[y_mate, lower, :], y_mate, lower, x_mate),
+            copy(at, 6, block.at[upper, :], me, upper, sibling),
+            copy(at, 7, block.at[lower, :], me, lower, sibling),
+        ]
+        for kind, (owner, rows) in enumerate(
+            [
+                (x_mate, upper),
+                (y_mate, lower),
+                (y_mate, upper),
+                (x_mate, lower),
+                (far, upper),
+                (far, lower),
+            ]
+        ):
+            found.append(copy(at, 8 + kind, whole.at[owner, rows, :], owner, rows, sibling))
+        return found
+
+    every = [copies(at) for at in range(count)]
+    locals_ = [
+        pltpu.make_async_copy(blocks[at], wholes[at].at[me], local_sem.at[at])
+        for at in range(count)
+    ]
+    for at in range(count):
+        for kind in (0, 1, 6, 7):
+            every[at][kind].start()
+        locals_[at].start()
+    for at in range(count):
+        found = every[at]
+        found[0].wait_recv()
+        found[4].start()
+        found[2].start()
+        found[8].start()
+        found[1].wait_recv()
+        found[5].start()
+        found[3].start()
+        found[9].start()
+    for at in range(count):
+        found = every[at]
+        for kind in (4, 5, 2, 3):
+            found[kind].wait_recv()
+            found[8 + kind].start()
+    for at in range(count):
+        for kind, one in enumerate(every[at]):
+            if kind >= 6:
+                one.wait_recv()
+            one.wait_send()
+        locals_[at].wait()
+
+
+def gather_weights(blocks):
+    count = len(blocks)
+    results = pl.pallas_call(
+        functools.partial(gather_kernel, count),
+        in_specs=[pl.BlockSpec(memory_space=pl.ANY)] * count,
+        out_specs=[pl.BlockSpec(memory_space=pl.ANY)] * count,
+        out_shape=[jax.ShapeDtypeStruct((8, *block.shape), block.dtype) for block in blocks],
+        scratch_shapes=[
+            pltpu.SemaphoreType.DMA((count, 14)),
+            pltpu.SemaphoreType.DMA((count, 14)),
+            pltpu.SemaphoreType.DMA((count,)),
+        ],
+        compiler_params=pltpu.CompilerParams(collective_id=1, has_side_effects=True),
+        cost_estimate=pl.CostEstimate(flops=0, bytes_accessed=200000000, transcendentals=0),
+        name="gather_weights",
+    )(*blocks)
+    return [whole.reshape(-1, whole.shape[-1]) for whole in results]
+
+
+class Line:
+    def __init__(self, first_stage, buffers, sems):
+        self.first_stage = first_stage
+        self.shard, self.line_one, self.line_two, self.whole, self.line_three = buffers
+        self.send_sem, self.recv_sem, self.store_sem, self.credit = sems
+        row = lax.axis_index("row")
+        self.is_end = (row == 0) | (row == 3)
+        self.is_middle = (row == 1) | (row == 2)
+        self.inner = {"row": jnp.where(row == 0, 1, 2)}
+        self.outer = {"row": jnp.where(row == 1, 0, 3)}
+        self.across = {"row": jnp.where(row == 1, 2, 1)}
+
+    def remote(self, stage, slot, source, target, where):
+        return pltpu.make_async_remote_copy(
+            src_ref=source,
+            dst_ref=target,
+            send_sem=self.send_sem.at[self.first_stage + stage, slot],
+            recv_sem=self.recv_sem.at[self.first_stage + stage, slot],
+            device_id=where,
+            device_id_type=MESH,
+        )
+
+    def inward(self, slot):
+        return self.remote(0, slot, self.shard.at[slot], self.line_one.at[slot], self.inner)
+
+    def crosswise(self, slot):
+        return self.remote(1, slot, self.shard.at[slot], self.line_two.at[slot], self.across)
+
+    def outward(self, slot):
+        return self.remote(2, slot, self.whole.at[slot], self.line_three.at[slot], self.outer)
+
+    def spend(self, stage, chunk):
+        @pl.when(chunk >= LINE_SLOTS)
+        def _():
+            pl.semaphore_wait(self.credit.at[self.first_stage + stage], 1)
+
+    def repay(self, stage, where):
+        pl.semaphore_signal(
+            self.credit.at[self.first_stage + stage],
+            inc=1,
+            device_id=where,
+            device_id_type=MESH,
+        )
+
+    def load(self, chunk, slot, begin):
+        def one(source):
+            copy = pltpu.make_async_copy(source, self.shard.at[slot], self.load_sem.at[slot])
+            copy.start() if begin else copy.wait()
+
+        self.sources(chunk, one)
+
+    def loaded(self, chunk, slot):
+        self.load(chunk, slot, False)
+        self.enter(chunk, slot)
+
+    def enter(self, chunk, slot):
+        @pl.when(self.is_end)
+        def _():
+            self.spend(0, chunk)
+            self.inward(slot).start()
+
+    def second(self, chunk, slot):
+        @pl.when(self.is_middle)
+        def _():
+            self.inward(slot).wait_recv()
+            self.shard[slot] = add(self.shard[slot], self.line_one[slot])
+            self.repay(0, self.outer)
+            self.spend(1, chunk)
+            self.crosswise(slot).start()
+
+    def third(self, chunk, slot):
+        @pl.when(self.is_middle)
+        def _():
+            self.crosswise(slot).wait()
+            self.whole[slot] = add(self.shard[slot], self.line_two[slot])
+            self.repay(1, self.across)
+            self.spend(2, chunk)
+            self.outward(slot).start()
+            self.store(chunk, slot, self.whole, True)
+
+    def last(self, chunk, slot):
+        @pl.when(self.is_end)
+        def _():
+            self.inward(slot).wait_send()
+            self.outward(slot).wait_recv()
+            self.store(chunk, slot, self.line_three, True)
+
+    def end(self, chunk, slot):
+        @pl.when(self.is_end)
+        def _():
+            self.store(chunk, slot, self.line_three, False)
+            self.repay(2, self.inner)
+
+        @pl.when(self.is_middle)
+        def _():
+            self.store(chunk, slot, self.whole, False)
+            self.outward(slot).wait_send()
+
+    def store(self, chunk, slot, origin, begin):
+        def one(target):
+            copy = pltpu.make_async_copy(origin.at[slot], target, self.store_sem.at[slot])
+            copy.start() if begin else copy.wait()
+
+        self.targets(chunk, one)
+
+    def drain(self):
+        @pl.when(self.is_end)
+        def _():
+            pl.semaphore_wait(self.credit.at[self.first_stage], LINE_SLOTS)
+
+        @pl.when(self.is_middle)
+        def _():
+            pl.semaphore_wait(self.credit.at[self.first_stage + 1], LINE_SLOTS)
+            pl.semaphore_wait(self.credit.at[self.first_stage + 2], LINE_SLOTS)
+
+
+def pieces(lengths, chunk, body):
+    low = 0
+    for which, amount in enumerate(lengths):
+
+        @pl.when((chunk >= low) & (chunk < low + amount))
+        def _(low=low, which=which):
+            body(which, chunk - low)
+
+        low += amount
+
+
+def tile_columns(at, width):
+    return pl.ds(pl.multiple_of(at * width, width), width)
+
+
+def sum_kernel(count, group, per, *refs):
+    take = iter(refs)
+    lefts = [next(take) for _ in range(count)]
+    rights = [next(take) for _ in range(count)]
+    image_part, bias_part, spread = next(take), next(take), next(take)
+    parts = [next(take) for _ in range(3)]
+    results = [next(take) for _ in range(count)]
+    every_image, bias_total, given = next(take), next(take), next(take)
+    part_results = [next(take) for _ in range(3)]
+    grads, core_in, pair, upper_in, lower_in, upper_two, lower_two = [next(take) for _ in range(7)]
+    main_buffers = [next(take) for _ in range(5)]
+    tall_buffers = [next(take) for _ in range(5)]
+    flat_buffers = [next(take) for _ in range(5)]
+    image_in, bias_in, small_send, small_recv = [next(take) for _ in range(4)]
+    send_sem, recv_sem, store_sem, load_sem, give_send, give_recv, credit = take
+    row = lax.axis_index("row")
+    near_row, far_row = row + 1 - 2 * lax.rem(row, 2), lax.rem(row + 2, 4)
+    main = Line(5, main_buffers, (send_sem, recv_sem, store_sem.at[0], credit))
+    tall = Line(8, tall_buffers, (send_sem, recv_sem, store_sem.at[1], credit))
+    flat = Line(11, flat_buffers, (send_sem, recv_sem, store_sem.at[2], credit))
+    tall.load_sem, flat.load_sem = load_sem.at[0], load_sem.at[1]
+    lengths = [
+        left.shape[1] * (right.shape[1] // TILE_COLUMNS) for left, right in zip(lefts, rights)
+    ]
+    chunks = sum(lengths)
+    _, (core, x, y), (sibling, x_mate, y_mate) = mates()
+    upper, lower = pl.ds(0, CUT), pl.ds(CUT, TILE_ROWS - CUT)
+
+    def main_targets(chunk, body):
+        def one(which, at):
+            result = results[which]
+            per_row = result.shape[2] // TILE_COLUMNS
+            columns = tile_columns(lax.rem(at, per_row), TILE_COLUMNS)
+            body(result.at[at // per_row, :, columns])
+
+        pieces(lengths, chunk, one)
+
+    main.targets = main_targets
+
+    def side_tiles(line, origins, ends):
+        amounts = [origin.shape[1] // LINE_TILE for origin in origins]
+
+        def view(refs):
+            def visit(chunk, body):
+                def one(which, at):
+                    body(refs[which].at[:, tile_columns(at, LINE_TILE)])
+
+                pieces(amounts, chunk, one)
+
+            return visit
+
+        line.sources, line.targets = view(origins), view(ends)
+        return sum(amounts)
+
+    tall_tiles = side_tiles(tall, parts[1:], part_results[1:])
+    flat_tiles = side_tiles(flat, parts[:1], part_results[:1])
+
+    def remote(stage, slot, source, target, where):
+        return pltpu.make_async_remote_copy(
+            src_ref=source,
+            dst_ref=target,
+            send_sem=send_sem.at[stage, slot],
+            recv_sem=recv_sem.at[stage, slot],
+            device_id={"img": where},
+            device_id_type=MESH,
+        )
+
+    def to_sibling(slot):
+        return remote(0, slot, grads.at[slot, :, :, 1 - core], core_in.at[slot], sibling)
+
+    def upper_first(slot):
+        return remote(1, slot, pair.at[slot, :, 1 - x, upper, :], upper_in.at[slot], x_mate)
+
+    def lower_first(slot):
+        return remote(2, slot, pair.at[slot, 1 - y, :, lower, :], lower_in.at[slot], y_mate)
+
+    def upper_second(slot):
+        return remote(3, slot, pair.at[slot, 1 - y, x, upper, :], upper_two.at[slot], y_mate)
+
+    def lower_second(slot):
+        return remote(4, slot, pair.at[slot, y, 1 - x, lower, :], lower_two.at[slot], x_mate)
+
+    def spend(stage, chunk):
+        @pl.when(chunk >= SLOTS)
+        def _():
+            pl.semaphore_wait(credit.at[stage], 1)
+
+    def repay(stage, where):
+        pl.semaphore_signal(
+            credit.at[stage], inc=1, device_id={"img": where}, device_id_type=MESH
+        )
+
+    for mate in (sibling, x_mate, y_mate):
+        greet({"img": mate})
+    for shift in range(1, 4):
+        greet({"row": lax.rem(row + shift, 4)})
+    pl.semaphore_wait(pltpu.get_barrier_semaphore(), 6)
+
+    def small(kind, source, target, where):
+        return pltpu.make_async_remote_copy(
+            src_ref=source,
+            dst_ref=target,
+            send_sem=small_send.at[kind],
+            recv_sem=small_recv.at[kind],
+            device_id=where,
+            device_id_type=MESH,
+        )
+
+    own_half = pl.ds(2 * (row // 2), 2)
+    image_hops = [
+        (image_part, image_in, {"img": sibling}),
+        (every_image.at[row, y, x], every_image.at[row, y, x], {"img": y_mate}),
+        (every_image.at[row, :, x], every_image.at[row, :, x], {"img": x_mate}),
+        (every_image.at[row], every_image.at[row], {"row": near_row}),
+        (every_image.at[own_half], every_image.at[own_half], {"row": far_row}),
+    ]
+
+    def small_hop(hop, begin):
+        source, target, where = image_hops[hop]
+        image = small(2 * hop, source, target, where)
+        bias = small(2 * hop + 1, bias_total if hop else bias_part, bias_in.at[hop], where)
+        if begin:
+            image.start()
+            bias.start()
+            return
+        image.wait()
+        bias.wait()
+        if hop == 0:
+            summed = image_part[...] + image_in[...]
+            every_image[row, y, x] = summed.astype(jnp.bfloat16)
+        bias_total[...] = (bias_total if hop else bias_part)[...] + bias_in[hop]
+
+    slot_len = given.shape[1]
+
+    def giving(shift, rows):
+        return pltpu.make_async_remote_copy(
+            src_ref=spread.at[shift, rows, :],
+            dst_ref=given.at[shift - 1, rows, :],
+            send_sem=give_send.at[shift - 1],
+            recv_sem=give_recv.at[shift - 1],
+            device_id={"row": lax.rem(row + shift, 4)},
+            device_id_type=MESH,
+        )
+
+    def owner_core(place):
+        return (place // group) // per
+
+    def give_some(at):
+        @pl.when((at < slot_len // GIVE_ROWS) & (owner_core(row) == core))
+        def _():
+            for shift in range(1, 4):
+                giving(shift, pl.ds(pl.multiple_of(at * GIVE_ROWS, GIVE_ROWS), GIVE_ROWS)).start()
+
+    def give_wait():
+        for shift in range(1, 4):
+            whole = giving(shift, pl.ds(0, slot_len))
+
+            @pl.when(owner_core(row) == core)
+            def _(whole=whole):
+                whole.wait_send()
+
+            @pl.when(owner_core(lax.rem(row + 4 - shift, 4)) == core)
+            def _(whole=whole):
+                whole.wait_recv()
+
+    def own_shard(chunk, slot):
+        line_slot = lax.rem(chunk, LINE_SLOTS)
+        upper_second(slot).wait()
+        main.shard[line_slot, upper, :] = add(pair[slot, y, x, upper, :], upper_two[slot])
+        repay(3, y_mate)
+        lower_second(slot).wait()
+        main.shard[line_slot, lower, :] = add(pair[slot, y, x, lower, :], lower_two[slot])
+        repay(4, x_mate)
+        main.enter(chunk, line_slot)
+
+    def second_axis(chunk, slot):
+        upper_first(slot).wait()
+        for at in range(2):
+            pair[slot, at, x, upper, :] = add(pair[slot, at, x, upper, :], upper_in[slot, at])
+        repay(1, x_mate)
+        spend(3, chunk)
+        upper_second(slot).start()
+        lower_first(slot).wait()
+        for at in range(2):
+            pair[slot, y, at, lower, :] = add(pair[slot, y, at, lower, :], lower_in[slot, at])
+        repay(2, y_mate)
+        spend(4, chunk)
+        lower_second(slot).start()
+
+    def first_axis(chunk, slot):
+        to_sibling(slot).wait()
+        for at_y in range(2):
+            for at_x in range(2):
+                pair[slot, at_y, at_x] = add(
+                    grads[slot, at_y, at_x, core], core_in[slot, at_y, at_x]
+                )
+        repay(0, sibling)
+        spend(1, chunk)
+        upper_first(slot).start()
+        spend(2, chunk)
+        lower_first(slot).start()
+
+    def multiply(chunk, slot):
+        def one(which, at):
+            left, right = lefts[which], rights[which]
+            per_row = right.shape[1] // TILE_COLUMNS
+            values = right[:, tile_columns(lax.rem(at, per_row), TILE_COLUMNS)]
+            for half in range(2):
+                rows = left[pl.ds(4 * half, 4), at // per_row]
+                product = jnp.dot(
+                    rows.reshape(4 * TILE_ROWS, -1), values, preferred_element_type=jnp.float32
+                )
+                grads[slot, half] = product.astype(jnp.bfloat16).reshape(
+                    2, 2, TILE_ROWS, TILE_COLUMNS
+                )
+
+        pieces(lengths, chunk, one)
+        spend(0, chunk)
+        to_sibling(slot).start()
+
+    stages = [
+        (12, LINE_SLOTS, main.end),
+        (11, LINE_SLOTS, main.last),
+        (9, LINE_SLOTS, main.third),
+        (7, LINE_SLOTS, main.second),
+        (5, SLOTS, own_shard),
+        (3, SLOTS, second_axis),
+        (1, SLOTS, first_axis),
+        (0, SLOTS, multiply),
+    ]
+
+    def step(at, carry):
+        for hop in range(5):
+
+            @pl.when(at == 4 * hop)
+            def _(hop=hop):
+                small_hop(hop, True)
+
+            @pl.when(at == 4 * hop + 3)
+            def _(hop=hop):
+                small_hop(hop, False)
+
+        give_some(at)
+        for line, tiles in ((tall, tall_tiles), (flat, flat_tiles)):
+            for lag, body in (
+                (8, line.end),
+                (7, line.last),
+                (5, line.third),
+                (3, line.second),
+                (1, line.loaded),
+                (0, functools.partial(line.load, begin=True)),
+            ):
+                tile = (at - lag) // SIDE_PACE
+                due = lax.rem(at - lag, SIDE_PACE) == 0
+
+                @pl.when((at >= lag) & due & (tile < tiles))
+                def _(tile=tile, body=body):
+                    body(tile, lax.rem(tile, LINE_SLOTS))
+
+        for lag, slots, body in stages:
+            chunk = at - lag
+
+            @pl.when((chunk >= 0) & (chunk < chunks))
+            def _(chunk=chunk, slots=slots, body=body):
+                body(chunk, lax.rem(chunk, slots))
+
+        return carry
+
+    lax.fori_loop(0, chunks + 12, step, 0)
+    for stage in range(5):
+        pl.semaphore_wait(credit.at[stage], SLOTS)
+    for line in (main, tall, flat):
+        line.drain()
+    give_wait()
+
+
+def turn(operand):
+    blocks = operand.shape[1] // (8 * TILE_ROWS)
+    return operand.T.reshape(8, blocks, TILE_ROWS, operand.shape[0])
+
+
+def sum_gradients(lefts, rights, image_part, bias_part, spread, parts, group, per):
+    bf16 = jnp.bfloat16
+    shapes = [
+        jax.ShapeDtypeStruct((left.shape[1], TILE_ROWS, right.shape[1]), bf16)
+        for left, right in zip(lefts, rights)
+    ]
+    image_rows, bias_rows = image_part.size // 128, bias_part.size // 128
+    padded = -(-image_rows // 16) * 16
+    image_part = jnp.pad(image_part.reshape(image_rows, 128), ((0, padded - image_rows), (0, 0)))
+    bias_part = bias_part.reshape(bias_rows, 128)
+    shapes += [
+        jax.ShapeDtypeStruct((4, 2, 2, padded, 128), bf16),
+        jax.ShapeDtypeStruct((bias_rows, 128), jnp.float32),
+        jax.ShapeDtypeStruct((3, *spread.shape[1:]), bf16),
+        *[jax.ShapeDtypeStruct(part.shape, bf16) for part in parts],
+    ]
+    tile = (TILE_ROWS, TILE_COLUMNS)
+    vmem, hbm = pl.BlockSpec(memory_space=pltpu.VMEM), pl.BlockSpec(memory_space=pl.ANY)
+    flops = 2 * sum(left.size * right.shape[1] for left, right in zip(lefts, rights))
+    results = pl.pallas_call(
+        functools.partial(sum_kernel, len(lefts), group, per),
+        in_specs=[vmem] * (2 * len(lefts) + 2) + [hbm] * 4,
+        out_specs=[hbm] * len(lefts) + [vmem] * 2 + [hbm] * 4,
+        out_shape=shapes,
+        scratch_shapes=[
+            pltpu.VMEM((SLOTS, 2, 2, 2, *tile), bf16),
+            pltpu.VMEM((SLOTS, 2, 2, *tile), bf16),
+            pltpu.VMEM((SLOTS, 2, 2, *tile), bf16),
+            pltpu.VMEM((SLOTS, 2, CUT, TILE_COLUMNS), bf16),
+            pltpu.VMEM((SLOTS, 2, TILE_ROWS - CUT, TILE_COLUMNS), bf16),
+            pltpu.VMEM((SLOTS, CUT, TILE_COLUMNS), bf16),
+            pltpu.VMEM((SLOTS, TILE_ROWS - CUT, TILE_COLUMNS), bf16),
+            *[pltpu.VMEM((LINE_SLOTS, *tile), bf16)] * 5,
+            *[pltpu.VMEM((LINE_SLOTS, parts[1].shape[0], LINE_TILE), bf16)] * 5,
+            *[pltpu.VMEM((LINE_SLOTS, parts[0].shape[0], LINE_TILE), bf16)] * 5,
+            pltpu.VMEM((padded, 128), jnp.float32),
+            pltpu.VMEM((5, bias_rows, 128), jnp.float32),
+            pltpu.SemaphoreType.DMA((10,)),
+            pltpu.SemaphoreType.DMA((10,)),
+            pltpu.SemaphoreType.DMA((14, LINE_SLOTS)),
+            pltpu.SemaphoreType.DMA((14, LINE_SLOTS)),
+            pltpu.SemaphoreType.DMA((3, LINE_SLOTS)),
+            pltpu.SemaphoreType.DMA((2, LINE_SLOTS)),
+            pltpu.SemaphoreType.DMA((3,)),
+            pltpu.SemaphoreType.DMA((3,)),
+            pltpu.SemaphoreType.REGULAR((14,)),
+        ],
+        compiler_params=pltpu.CompilerParams(
+            collective_id=0, has_side_effects=True, vmem_limit_bytes=56 * 1024 * 1024
+        ),
+        cost_estimate=pl.CostEstimate(
+            flops=flops, bytes_accessed=600000000, transcendentals=0
+        ),
+        name="sum_gradients",
+    )(*lefts, *rights, image_part, bias_part, spread, *parts)
+    summed = [
+        result.reshape(-1, result.shape[2]).astype(jnp.float32) for result in results[: len(lefts)]
+    ]
+    every_image, bias_total, given = results[len(lefts) : len(lefts) + 3]
+    parts = [part.astype(jnp.float32) for part in results[len(lefts) + 3 :]]
+    every_image = every_image[:, :, :, :image_rows].reshape(4, 4, -1).transpose(1, 0, 2)
+    return summed, every_image.reshape(16, -1), bias_total.reshape(-1), given, parts
 
 
 def split_heads(operand):
@@ -237,30 +840,38 @@
     def image_of(shift):
         return (((row_rank - shift) % n_row) // group) % per
 
-    def bring(operand):
+    def bring_start(operand):
         pieces = []
         for shift in range(n_row):
             piece = lax.dynamic_index_in_dim(operand, image_of(shift), 0, keepdims=False)
             if shift:
                 piece = lax.ppermute(piece, ("img", "row"), route(shift, False))
             pieces.append(piece)
+        return pieces
+
+    def bring_end(pieces):
         packed = matmul(pick, jnp.concatenate(pieces, axis=0)).astype(bf16)
         own = lax.dynamic_slice_in_dim(packed, core * length, length, 0)
         other = lax.dynamic_slice_in_dim(packed, (1 - core) * length, length, 0)
         return jnp.where(receives, own, swap(other, "img", 1))
 
-    def give(operand):
+    def give_start(operand):
         other = swap(operand, "img", 1)
         both = jnp.where(
             core == 0,
             jnp.concatenate([operand, other], axis=0),
             jnp.concatenate([other, operand], axis=0),
         )
-        spread = weight_grad(pick, both).astype(bf16)
-        images = [jnp.zeros((slot_len, operand.shape[1]), bf16) for _ in range(per)]
+        return weight_grad(pick, both).astype(bf16)
+
+    def give_end(spread, given=None):
+        images = [jnp.zeros((slot_len, spread.shape[1]), bf16) for _ in range(per)]
         for shift in range(n_row):
             piece = spread[shift * slot_len : (shift + 1) * slot_len]
-            if shift:
+            if shift and given is not None:
+                sender = ((row_rank - shift) % n_row) // group
+                piece = jnp.where(sender // per == core, given[shift - 1], jnp.zeros_like(piece))
+            elif shift:
                 piece = lax.ppermute(piece, ("img", "row"), route(shift, True))
             else:
                 piece = jnp.where(receives, piece, jnp.zeros_like(piece))
@@ -273,7 +884,44 @@
     def fetch(operand):
         return lax.all_gather(operand, "img", axis=0, tiled=True)
 
-    order = lax.all_gather(image_order, "img", axis=0, tiled=True)
+    chip_bits = [1 << at for at in range(1, n_img.bit_length() - 1)]
+    forth, back = chip_bits, chip_bits[-1:] + chip_bits[:-1]
+
+    def side(bit):
+        return (img_rank // bit) % 2
+
+    def together(operand, bit, axis):
+        blocks = jnp.stack([operand, swap(operand, "img", bit)], axis=axis)
+        return jnp.where(side(bit) == 0, blocks, jnp.flip(blocks, axis=axis))
+
+    def scattered(grad):
+        return lax.psum_scatter(grad, "img", scatter_dimension=0, tiled=True)
+
+    def offload_shards(left, right):
+        return scattered(weight_grad(left, right).astype(bf16))
+
+    def row_sum(part, turn_by):
+        ranks = [(at + turn_by) % n_row for at in range(n_row)]
+        return lax.psum(part, "row", axis_index_groups=[ranks]).astype(f32)
+
+    fold = n_row // 4
+    line_rank = row_rank // fold
+
+    def over_row(part):
+        def hop(operand, pairs):
+            routes = [(a * fold + low, b * fold + low) for a, b in pairs for low in range(fold)]
+            return lax.ppermute(operand, "row", routes)
+
+        for at in range(fold.bit_length() - 1):
+            part = (part.astype(f32) + swap(part, "row", 1 << at).astype(f32)).astype(bf16)
+        part = (part.astype(f32) + hop(part, [(0, 1), (3, 2)]).astype(f32)).astype(bf16)
+        part = (part.astype(f32) + hop(part, [(1, 2), (2, 1)]).astype(f32)).astype(bf16)
+        outer = hop(part, [(1, 0), (2, 3)])
+        return jnp.where((line_rank == 0) | (line_rank == 3), outer, part).astype(f32)
+
+    order = image_order
+    for bit in [1] + chip_bits:
+        order = together(order, bit, 0).reshape(-1)
     chosen = jnp.sum(
         jnp.where(order[:, None] == jnp.arange(n_images)[None, :], time_bins[None, :], 0), axis=1
     )
@@ -292,7 +940,9 @@
         jnp.zeros((ff_width,), f32), up_bias.astype(f32), (img_rank * up_bias.shape[0],)
     )
     mod_part = matmul(row_cond, ada_weight) + bias_part[None, :]
-    summed_rows = lax.psum(jnp.concatenate([mod_part.reshape(-1), up_bias_part]), "img")
+    summed_rows = jnp.concatenate([mod_part.reshape(-1), up_bias_part])
+    for bit in [1] + chip_bits:
+        summed_rows = summed_rows + swap(summed_rows, "img", bit)
     modulation = lax.dynamic_index_in_dim(
         summed_rows[: (n_img // 2) * mod_width].reshape(n_img // 2, mod_width),
         img_rank // 2,
@@ -300,22 +950,27 @@
         keepdims=True,
     )
     up_bias_full = summed_rows[(n_img // 2) * mod_width :]
-    shift_att, scale_att, gate_att, shift_mlp, scale_mlp, gate_mlp = jnp.split(
-        modulation, 6, axis=1
-    )
-
-    qkv_full = fetch(qkv_weight)
-    out_full = fetch(out_weight)
+    small_plane = n_img == 8 and n_row == 4
+    early = [qkv_weight, out_weight, proj_third]
+    if small_plane:
+        early, modulation = lax.optimization_barrier((early, modulation))
+        qkv_full, out_full, third_full = gather_weights(early)
+    else:
+        qkv_full, out_full, third_full = [fetch(one) for one in early]
     up_full = fetch(up_weight)
     down_full = fetch(down_weight)
     first_full = fetch(proj_first)
     second_full = fetch(proj_second)
-    third_full = fetch(proj_third)
-
-    source = bring(tokens).astype(f32)
-    outside = bring(jnp.concatenate([cotangent, targets], axis=2))
-    own_cotangent = outside[:, :width].astype(f32)
-    own_targets = outside[:, width:].astype(f32)
+
+    shift_att, scale_att, gate_att, shift_mlp, scale_mlp, gate_mlp = jnp.split(
+        modulation, 6, axis=1
+    )
+    arriving, qkv_full = lax.optimization_barrier((bring_start(tokens), qkv_full))
+    source = bring_end(arriving).astype(f32)
+    later, source = lax.optimization_barrier(
+        (jnp.concatenate([cotangent, targets], axis=2), source)
+    )
+    outside = bring_start(later)
 
     h_att = modulate(source, shift_att, scale_att).astype(bf16)
     qkv_rows = matmul(h_att, qkv_full).astype(bf16)
@@ -332,11 +987,18 @@
     attn_out = matmul(head_mix, out_full)
     residual = source + gate_att * attn_out
     h_mlp = modulate(residual, shift_mlp, scale_mlp).astype(bf16)
+    outside, h_mlp = lax.optimization_barrier((outside, h_mlp))
+    outside = bring_end(outside)
+    own_cotangent = outside[:, :width].astype(f32)
+    own_targets = outside[:, width:].astype(f32)
     pre_act = matmul(h_mlp, up_full) + up_bias_full
     gelu_out = gelu_tanh(pre_act).astype(bf16)
     mlp_out = matmul(gelu_out, down_full)
+    lefts = [gelu_out, h_mlp, head_mix, h_att]
+    if small_plane:
+        lefts = [turn(left) for left in lefts]
+        lefts, mlp_out = lax.optimization_barrier((lefts, mlp_out))
     block_own = (residual + gate_mlp * mlp_out).astype(bf16)
-    block_out = give(block_own)
     lin_one = matmul(block_own, first_full)
     hid_one = jax.nn.silu(lin_one).astype(bf16)
     lin_two = matmul(hid_one, second_full)
@@ -346,61 +1008,71 @@
     def align_loss(operand):
         return -0.5 * jnp.sum(alignment(operand, own_targets))
 
-    def scatter(grad):
-        part = lax.psum_scatter(grad.astype(bf16), "img", scatter_dimension=0, tiled=True)
-        part = part.astype(f32)
-        for at in range(n_row.bit_length() - 1):
-            part = part + swap(part.astype(bf16), "row", 1 << at).astype(f32)
-        return part
-
     d_proj = jax.vjp(align_loss, projected)[1](jnp.ones((), f32))[0].astype(bf16)
-    grad_third = scatter(weight_grad(hid_two, d_proj))
+    third_sum = weight_grad(hid_two, d_proj).astype(bf16)
+    third_sum, d_proj = lax.optimization_barrier((third_sum, d_proj))
+    third_part = scattered(third_sum)
     d_lin_two = silu_back(lin_two, transposed(d_proj, third_full)).astype(bf16)
-    grad_second = scatter(weight_grad(hid_one, d_lin_two))
+    second_sum = weight_grad(hid_one, d_lin_two).astype(bf16)
+    second_sum, d_lin_two = lax.optimization_barrier((second_sum, d_lin_two))
+    second_part = scattered(second_sum)
     d_lin_one = silu_back(lin_one, transposed(d_lin_two, second_full)).astype(bf16)
-    grad_first = scatter(weight_grad(block_own, d_lin_one))
+    first_sum = weight_grad(block_own, d_lin_one).astype(bf16)
+    first_sum, d_lin_one = lax.optimization_barrier((first_sum, d_lin_one))
+    first_part = scattered(first_sum)
     d_res = own_cotangent + transposed(d_lin_one, first_full)
     d_gate_mlp = jnp.sum(d_res * mlp_out, axis=0)
     d_mlp = (d_res * gate_mlp).astype(bf16)
-    grad_down = scatter(weight_grad(gelu_out, d_mlp))
     d_pre = gelu_back(pre_act, transposed(d_mlp, down_full)).astype(bf16)
     bias_sum = jnp.sum(d_pre.astype(f32), axis=0)
-    grad_up = scatter(weight_grad(h_mlp, d_pre))
     d_resid_norm, d_shift_mlp, d_scale_mlp = jax.vjp(modulate, residual, shift_mlp, scale_mlp)[1](
         transposed(d_pre, up_full)
     )
     d_residual = d_res + d_resid_norm
     d_gate_att = jnp.sum(d_residual * attn_out, axis=0)
     d_attn = (d_residual * gate_att).astype(bf16)
-    grad_out = scatter(weight_grad(head_mix, d_attn))
     d_mixed = transposed(d_attn, out_full).astype(bf16)
+    third_part, d_mixed = lax.optimization_barrier((third_part, d_mixed))
     d_query, d_key, d_value = attend_back(
         queries, keys, values, mixed, split_heads(d_mixed), log_total
     )
+    second_part, d_key = lax.optimization_barrier((second_part, d_key))
     d_key_value = jnp.concatenate([join_heads(d_key), join_heads(d_value)], axis=1)
     for axis, bit in [("row", bit) for bit in reversed(bits)] + [("img", 1)]:
         half = d_key_value.shape[0] // 2
         arrived = swap(d_key_value[half:], axis, bit)
         d_key_value = (d_key_value[:half].astype(f32) + arrived.astype(f32)).astype(bf16)
     d_qkv = jnp.concatenate([join_heads(d_query), d_key_value], axis=1)
-    grad_qkv = scatter(weight_grad(h_att, d_qkv))
     d_source, d_shift_att, d_scale_att = jax.vjp(modulate, source, shift_att, scale_att)[1](
         transposed(d_qkv, qkv_full)
     )
-    grad_tokens = give((d_residual + d_source).astype(bf16))
-
+    spread = give_start((d_residual + d_source).astype(bf16))
+    block_out = give_end(give_start(block_own))
     own_mod = jnp.concatenate(
         [d_shift_att[0], d_scale_att[0], d_gate_att, d_shift_mlp[0], d_scale_mlp[0], d_gate_mlp]
-    )[None, :]
-    own_mod = own_mod + swap(own_mod, "img", 1)
-    for bit in bits:
-        own_mod = own_mod + swap(own_mod, "row", bit)
-    own_mod = own_mod.astype(bf16)
-    column_mod = lax.all_gather(own_mod, "row", axis=0, tiled=True)[::group]
-    same_core = [[2 * at + side for at in range(n_img // 2)] for side in range(2)]
-    d_mod = lax.all_gather(
-        column_mod, "img", axis=0, tiled=True, axis_index_groups=same_core
-    )
+    )
+    rights = [d_mlp, d_pre, d_attn, d_qkv]
+    proj_parts = [first_part, second_part, third_part]
+    if small_plane:
+        tied = (spread, proj_parts, rights, own_mod, bias_sum)
+        spread, proj_parts, rights, own_mod, bias_sum = lax.optimization_barrier(tied)
+        blocks = spread.reshape(n_row, slot_len, width)
+        large, d_mod, bias_sum, given, proj_grads = sum_gradients(
+            lefts, rights, own_mod, bias_sum, blocks, proj_parts, group, per
+        )
+        grad_tokens = give_end(spread, given)
+    else:
+        grad_tokens = give_end(spread)
+        proj_grads = [row_sum(part, at) for at, part in enumerate(proj_parts)]
+        large = [over_row(offload_shards(*pair)) for pair in zip(lefts, rights)]
+        slot_id = column * (img_rank // 2) + place
+        placed = jnp.zeros((n_images, mod_width), f32)
+        placed = lax.dynamic_update_slice(placed, own_mod[None, :], (slot_id, 0))
+        d_mod, bias_sum = lax.psum((placed, bias_sum), ("img", "row"))
+        d_mod = d_mod.astype(bf16)
+    grad_first, grad_second, grad_third = proj_grads
+    grad_down, grad_up, grad_out, grad_qkv = large
+
     grad_ada = weight_grad(silu_cond, d_mod)
     grad_ada_bias = jnp.sum(
         lax.dynamic_slice_in_dim(d_mod, img_rank * ada_bias.shape[0], ada_bias.shape[0], 1).astype(
@@ -411,7 +1083,7 @@
     d_cond = silu_back(condition, transposed(d_mod, ada_weight))
     grad_table = jnp.dot(select.T, d_cond, precision=lax.Precision.HIGHEST)
     grad_up_bias = lax.dynamic_slice_in_dim(
-        lax.psum(bias_sum, ("img", "row")), img_rank * up_bias.shape[0], up_bias.shape[0], 0
+        bias_sum, img_rank * up_bias.shape[0], up_bias.shape[0], 0
     )
     return (
         block_out,

time: 1140 us -> 827 us (0.73)
  waiting for transfers between devices: 515 us -> 40.8 us
  Pallas kernels: 54.2 us -> 354 us
  blocking collectives: 88.9 us -> 0 us
  matrix products: 229 us -> 180 us
  local copies, waits for them, and re-layouts: 90.3 us -> 117 us
  starting transfers between devices: 71.1 us -> 46.3 us
    pallas_call x0 -> x2, Pallas kernels: none -> 300 us  [the longest x1 202 us: sum_gradients(): pl.pallas_call(functools.partial(sum_kernel, len(lefts), group, per), in_...]
    ppermute x21 -> x12, waiting for transfers between devices: 246 us -> 14.2 us  [swap(): return lax.ppermute(operand, axis, [(at, at ^ bit) for at in range(size)])]
    all_gather x7 -> x4, waiting for transfers between devices: 143 us -> 0.06 us  [fetch(): return lax.all_gather(operand, 'img', axis=0, tiled=True)]
    psum x1 -> x0, blocking collectives: 56.2 us -> none  [local(): lax.psum(bias_sum, ('img', 'row'))]
    reduce_scatter x7 -> x3, waiting for transfers between devices: 51.3 us -> 0.01 us  [scattered(): return lax.psum_scatter(grad, 'img', scatter_dimension=0, tiled=True)]
    dot_general x10 -> x6, matrix products: 77.3 us -> 32.4 us  [weight_grad(): lax.dot_general(left_side, right_side, FIRST, preferred_element_type=jnp....]
    ppermute x12 -> x9, waiting for transfers between devices: 60.9 us -> 25 us  [the longest x3 25 us: give_end(): piece = lax.ppermute(piece, ('img', 'row'), route(shift, True))]
    all_gather x2 -> x0, blocking collectives: 23.2 us -> none  [the longest x1 13.3 us: local(): column_mod = lax.all_gather(own_mod, 'row', axis=0, tiled=True)[::group]]
  transfers between devices with their start and end apart: 48 -> 28, of which waited for: 18 -> 8; matrix products, arithmetic and copies ran while one was open for 26% -> 34% of each run, Pallas kernels for 5% -> 19%
where the time goes in v2:
time: 827 us; the launch traced here: 816 us
  Pallas kernels  354 us (43%)
  matrix products  180 us (22%)
  local copies, waits for them, and re-layouts  117 us (14%)
  other arithmetic  58.9 us (7%)
  starting transfers between devices  46.3 us (6%)
  waiting for transfers between devices  40.8 us (5%)
  between operations  18.7 us (2%)
    pallas_call x1, Pallas kernels, sum_gradients(): pl.pallas_call(functools.partial(sum_kernel, len(lefts), group, per), in_...  202 us
    pallas_call x1, Pallas kernels, gather_weights(): pl.pallas_call(functools.partial(gather_kernel, count), in_specs=[pl.Bloc...  98 us
    dot_general x10, matrix products, matmul(): return jnp.dot(left_side, right_side, preferred_element_type=jnp.float32)  77.3 us
    dot_general x8, matrix products, transposed(): lax.dot_general(left_side, right_side, LAST, preferred_element_type=jnp.f...  68.6 us
    dot_general x6, matrix products, weight_grad(): lax.dot_general(left_side, right_side, FIRST, preferred_element_type=jnp....  32.4 us
    pallas_call x1, Pallas kernels, attend_back(): pl.pallas_call(attend_back_kernel, grid=(heads,), in_specs=[short, long,...  32.2 us
    ppermute x12, starting transfers between devices, swap(): return lax.ppermute(operand, axis, [(at, at ^ bit) for at in range(size)])  26.6 us
    unnamed x175, local copies, waits for them, and re-layouts  26.4 us
  transfers between devices with their start and end apart: 28, of which 8 were waited for; matrix products, arithmetic and copies ran while one was open for 34% of the time, Pallas kernels for 19%

profile of v2, /device:TPU:0, one launch (start us, length us, event | category | flops | bytes accessed | tf_op | source)
XLA Modules:
  0.0 815.8 jit_solution(4523882846709540163)
XLA Ops:
  49.8 5.5 collective-permute-done.8
  55.4 98.0 %gather_weights.1 = (bf16[8,144,3456]{2,1,0:T(8,128)(2,1)}, bf16[8,144,1152]{2,1,0:T(8,128)(2,1)}, bf16[8,256,768]{2,1,0:T(8,128)(2,1)}) custom-call(bf16[144,3456]{1,0:T(8,128)(2,1)} %refs_0_, bf16[144,1152]{1,0:T(8,128)(2,1)} %refs_1_, bf16[256,768]{1,0:T(8,128)(2,1)} %refs_2_), custom_call_target="tpu_custom_call" | custom-call | bytes 200000000 | tf_op jit(solution)/shard_map/gather_weights/pallas_call | solution.py:281
  153.5 6.4 convolution_convert_fusion.5
  173.2 8.8 %convolution_convert_fusion.4 = bf16[512,3456]{1,0:T(8,128)(2,1)S(1)} fusion(bf16[1152,3456]{1,0:T(8,128)(2,1)} %bitcast.194, f32[512,1152]{1,0:T(8,128)S(1)} %copy-done.5, f32[1152]{0:T(1024)S(1)} %get-tuple-element.142, f32[1152]{0:T(1024)S(1)} %get-tuple-element.143, f32[512]{0:T(512)S(1)} %fusion.79, f32[512]{0:T(512)S(1)} %broadcast_multiply_fusion.1), kind=kOutput, calls=%fused_computation.28 | convolution fusion | flops 4081582080 | bytes 13874176 | tf_op jit(solution)/shard_map/dot_general | solution.py:38
  187.1 5.9 dynamic-slice_bitcast_fusion
  203.3 4.9 pad_maximum_fusion.3
  212.5 5.7 copy.64
  222.6 5.8 copy.62
  230.2 22.1 %attend.1 = (bf16[16,512,72]{2,1,0:T(8,128)(2,1)S(1)}, f32[16,1,512]{2,1,0:T(1,128)S(1)}) custom-call(bf16[16,512,72]{2,1,0:T(8,128)(2,1)S(1)} %bitcast.156, bf16[16,1024,72]{2,1,0:T(8,128)(2,1)} %bitcast.173, bf16[16,1024,72]{2,1,0:T(8,128)(2,1)} %bitcast.171), custom_call_target="tpu_custom_call" | custom-call | flops 8589934592 | bytes 12582912 | tf_op jit(solution)/shard_map/attend/pallas_call | solution.py:81
  265.3 8.9 %fusion.30 = bf16[1024,1920]{1,0:T(8,128)(2,1)S(1)} fusion(bf16[384,1920]{1,0:T(8,128)(2,1)} %collective-permute-done.13, bf16[384,1920]{1,0:T(8,128)(2,1)} %collective-permute-done.12, bf16[384,1920]{1,0:T(8,128)(2,1)} %collective-permute-done.11, bf16[384,1920]{1,0:T(8,128)(2,1)S(1)} %copy-done.29, pred[1024,384]{1,0:T(32,128)(4,1)S(1)} %copy-done.46, ...), kind=kOutput, calls=%fused_computation.53 | convolution fusion | flops 6070075392 | bytes 11403264 | tf_op jit(solution)/shard_map/dot_general | solution.py:38
  277.7 4.7 collective-permute-start.18
  290.2 14.8 %fusion.14 = (bf16[4608,512]{0,1:T(8,128)(2,1)}, f32[512,4608]{1,0:T(8,128)}) fusion(f32[4608]{0:T(1024)S(1)} %slice.81, bf16[512,1152]{1,0:T(8,128)(2,1)S(1)} %copy-done.22, bf16[1152,4608]{1,0:T(8,128)(2,1)} %all-gather.5.cloned.1.call-done), kind=kOutput, calls=%fused_computation.17 | convolution fusion | flops 5459410944 | bytes 25970688 | tf_op jit(solution)/shard_map/dot_general | solution.py:38
  305.0 6.7 copy.66
  311.7 13.0 %fusion.23 = f32[512,1152]{1,0:T(8,128)S(1)} fusion(bf16[4608,1152]{1,0:T(8,128)(2,1)} %all-gather.7.cloned.1.call-done, f32[512,4608]{1,0:T(8,128)} %get-tuple-element.185, f32[4608]{0:T(1024)S(1)} %slice.81), kind=kOutput, calls=%fused_computation.42 | convolution fusion | flops 5459410944 | bytes 22431744 | tf_op jit(solution)/shard_map/dot_general | solution.py:38
  326.5 7.0 fusion.104
  333.6 11.7 %multiply_convert_fusion.2 = (bf16[512,2048]{1,0:T(8,128)(2,1)S(1)}, f32[512,2048]{1,0:T(8,128)}) fusion(bf16[2048,2048]{1,0:T(8,128)(2,1)} %all-gather.11.cloned.1.call-done, f32[512,2048]{1,0:T(8,128)} %fusion.104), kind=kOutput, calls=%fused_computation.49 | convolution fusion | flops 4305453056 | bytes 18874368 | tf_op jit(solution)/shard_map/dot_general | solution.py:38
  353.1 6.3 fusion.26
  360.7 7.2 convolution_convert_fusion.2
  368.0 11.0 %fusion.29 = bf16[512,2048]{1,0:T(8,128)(2,1)S(1)} fusion(f32[512,2048]{1,0:T(8,128)} %fusion.104, bf16[512,2048]{1,0:T(8,128)(2,1)} %copy-done.84, bf16[2048,2048]{1,0:T(8,128)(2,1)} %all-gather.11.cloned.1.call-done), kind=kOutput, calls=%fused_computation.48 | convolution fusion | flops 4305453056 | bytes 16777216 | tf_op jit(solution)/shard_map/dot_general | solution.py:42
  385.0 7.6 multiply_convert_fusion.5
  392.6 18.1 %convert_reduce_fusion = (f32[4608]{0:T(1024)}, bf16[512,4608]{1,0:T(8,128)(2,1)}) fusion(f32[512,4608]{1,0:T(8,128)} %get-tuple-element.185, f32[4608]{0:T(1024)S(1)} %slice.81, bf16[512,1152]{1,0:T(8,128)(2,1)S(1)} %get-tuple-element.112.refs_4_, bf16[4608,1152]{1,0:T(8,128)(2,1)} %all-gather.7.cloned.1.call-done), kind=kOutput, calls=%fused_computation.18 | convolution fusion | flops 5490077184 | bytes 25989120 | tf_op jit(solution)/shard_map/dot_general | solution.py:42
  410.8 13.6 %multiply_reduce_fusion.1 = (f32[1152]{0:T(1024)S(1)}, f32[512]{0:T(512)S(1)}, f32[1152]{0:T(1024)S(1)}, f32[512,1152]{1,0:T(8,128)S(1)}) fusion(f32[512,1152]{1,0:T(8,128)S(1)} %copy-done.10, f32[512]{0:T(512)S(1)} %copy-done.66, f32[512]{0:T(512)S(1)} %copy-done.60, f32[1152]{0:T(1024)S(1)} %copy-done.56, ...), kind=kOutput, calls=%fused_computation.86 | convolution fusion | flops 5440534016 | bytes 20073984 | tf_op jit(solution)/shard_map/dot_general | solution.py:42
  436.3 8.0 convolution_convert_fusion.3
  450.1 32.2 %attend_back.1 = (bf16[16,512,72]{2,1,0:T(8,128)(2,1)S(1)}, bf16[16,1024,72]{2,1,0:T(8,128)(2,1)}, bf16[16,1024,72]{2,1,0:T(8,128)(2,1)}) custom-call(bf16[16,512,72]{2,1,0:T(8,128)(2,1)S(1)} %bitcast.157, bf16[16,1024,72]{2,1,0:T(8,128)(2,1)} %bitcast.174, bf16[16,1024,72]{2,1,0:T(8,128)(2,1)} %bitcast.172, bf16[16,512,72]{2,1,0:T(8,128)(2,1)} %copy-done.3, ...), custom_call_target="tpu_custom_call" | custom-call | flops 21474836480 | bytes 31457280 | tf_op jit(solution)/shard_map/attend_back/pallas_call | solution.py:144
  483.6 5.8 copy.73
  493.8 5.8 copy.72
  515.2 6.0 collective-permute-done.15
  521.2 15.9 %collective-permute-done.17 = bf16[384,1152]{1,0:T(8,128)(2,1)} collective-permute-done((bf16[384,1152]{1,0:T(8,128)(2,1)}, bf16[384,1152]{1,0:T(8,128)(2,1)}, u32[]{:S(2)}, u32[]{:S(2)}) %collective-permute-start.17) | collective-permute-done | bytes 884768 | tf_op jit(solution)/shard_map/ppermute | solution.py:875
  552.5 8.5 %multiply_reduce_fusion.3 = (f32[1152]{0:T(1024)S(1)}, f32[512]{0:T(512)S(1)}, f32[1152]{0:T(1024)S(1)}, f32[512,1152]{1,0:T(8,128)S(1)}) fusion(f32[512,1152]{1,0:T(8,128)S(1)} %copy-done.7, f32[512]{0:T(512)S(1)} %copy-done.64, f32[512]{0:T(512)S(1)} %copy-done.58, f32[1152]{0:T(1024)S(1)} %copy-done.52, bf16[1152,3456]{1,0:T(8,128)(2,1)} %bitcast.195, ...), kind=kOutput, calls=%fused_computation.88 | convolution fusion | flops 4088657408 | bytes 16240128 | tf_op jit(solution)/shard_map/dot_general | solution.py:42
  563.0 11.5 %collective-permute-start.20 = (bf16[512,1152]{1,0:T(8,128)(2,1)S(1)}, bf16[512,1152]{1,0:T(8,128)(2,1)S(1)}, u32[]{:S(2)}, u32[]{:S(2)}) collective-permute-start(bf16[512,1152]{1,0:T(8,128)(2,1)S(1)} %add_convert_fusion.1), channel_id=1, source_target_pairs={{0,4},{4,0},{8,12},{12,8},{16,20},{20,16},{24,28},{28,24},{1,5},{5... | collective-permute-start | bytes 3538952 | tf_op jit(solution)/shard_map/ppermute | solution.py:816
  577.0 6.2 convolution_convert_fusion
  583.8 201.8 %sum_gradients.1 = (bf16[4,144,1152]{2,1,0:T(8,128)(2,1)}, bf16[1,144,4608]{2,1,0:T(8,128)(2,1)}, bf16[1,144,1152]{2,1,0:T(8,128)(2,1)}, bf16[1,144,3456]{2,1,0:...) custom-call(bf16[8,4,144,512]{3,2,1,0:T(8,128)(2,1)} %bitcast.167, ...), custom_call_target="tpu_custom_call" | custom-call | flops 16307453952 | bytes 600000000 | tf_op jit(solution)/shard_map/sum_gradients/pallas_call | solution.py:729
  (358 shorter events, 201.5 us)
Async XLA Ops:
  7.2 283.0 %all-gather.5.cloned.1.call-start = ((), (), s32[]{:S(2)}) async-start(), calls=%async_computation.3 | async-start | bytes 11943936 | tf_op jit(solution)/shard_map/all_gather | solution.py:885
  7.9 303.8 %all-gather.7.cloned.1.call-start = ((), (), s32[]{:S(2)}) async-start(), calls=%async_computation.4 | async-start | bytes 11943936 | tf_op jit(solution)/shard_map/all_gather | solution.py:885
  8.7 317.8 %all-gather.9.cloned.1.call-start = ((), (), s32[]{:S(2)}) async-start(), calls=%async_computation.5 | async-start | bytes 5308416 | tf_op jit(solution)/shard_map/all_gather | solution.py:885
  8.7 18.1 %collective-permute-start.3 = (s32[2]{0:T(128)S(1)}, s32[2]{0:T(128)S(1)}, u32[]{:S(2)}, u32[]{:S(2)}) collective-permute-start(s32[2]{0:T(128)S(1)} %copy-done.75), channel_id=1, source_target_pairs={{0,4},{4,0},{8,12},{12,8},{16,20},{20,16},{24,28},{28,24},{1,5},{5... | collective-permute-start | bytes 32 | tf_op jit(solution)/shard_map/ppermute | solution.py:816
  12.9 140.6 %collective-permute-start.2 = (bf16[384,1152]{1,0:T(8,128)(2,1)}, bf16[384,1152]{1,0:T(8,128)(2,1)}, u32[]{:S(2)}, u32[]{:S(2)}) collective-permute-start(bf16[384,1152]{1,0:T(8,128)(2,1)} %get-tuple-element.168), channel_id=1, source_target_pairs={{3,0},{0,1},{5,6},{6,7},{11,8},{8,9},{13,14},{14,15},{19,16},{16,1... | collective-permute-start | bytes 2654216 | tf_op jit(solution)/shard_map/ppermute | solution.py:848
  17.5 135.9 %collective-permute-start = (bf16[384,1152]{1,0:T(8,128)(2,1)}, bf16[384,1152]{1,0:T(8,128)(2,1)}, u32[]{:S(2)}, u32[]{:S(2)}) collective-permute-start(bf16[384,1152]{1,0:T(8,128)(2,1)} %get-tuple-element.169), channel_id=1, source_target_pairs={{1,0},{2,1},{7,6},{4,7},{9,8},{10,9},{15,14},{12,15},{17,16},{18,1... | collective-permute-start | bytes 2654216 | tf_op jit(solution)/shard_map/ppermute | solution.py:848
  18.8 134.6 %collective-permute-start.1 = (bf16[384,1152]{1,0:T(8,128)(2,1)}, bf16[384,1152]{1,0:T(8,128)(2,1)}, u32[]{:S(2)}, u32[]{:S(2)}) collective-permute-start(bf16[384,1152]{1,0:T(8,128)(2,1)} %get-tuple-element.171), channel_id=1, source_target_pairs={{2,0},{3,1},{4,6},{5,7},{10,8},{11,9},{12,14},{13,15},{18,16},{19,... | collective-permute-start | bytes 2654216 | tf_op jit(solution)/shard_map/ppermute | solution.py:848
  20.2 313.4 %all-gather.11.cloned.1.call-start = ((), (), s32[]{:S(2)}) async-start(), calls=%async_computation.6 | async-start | bytes 9437184 | tf_op jit(solution)/shard_map/all_gather | solution.py:885
  27.1 3.5 collective-permute-start.4
  30.8 3.5 collective-permute-start.5
  36.5 3.8 collective-permute-start.6
  40.4 6.7 collective-permute-start.7
  47.1 8.2 %collective-permute-start.8 = (f32[32256]{0:T(1024)S(1)}, f32[32256]{0:T(1024)S(1)}, u32[]{:S(2)}, u32[]{:S(2)}) collective-permute-start(f32[32256]{0:T(1024)S(1)} %add.469), channel_id=1, source_target_pairs={{0,16},{4,20},{8,24},{12,28},{16,0},{20,4},{24,8},{28,12},{1,17},{... | collective-permute-start | bytes 387080 | tf_op jit(solution)/shard_map/ppermute | solution.py:816
  162.4 4.4 collective-permute-start.9
  166.8 94.0 %copy-start.51 = (f32[1152]{0:T(1024)}, f32[1152]{0:T(1024)S(1)}, u32[]{:S(2)}) copy-start(f32[1152]{0:T(1024)S(1)} %get-tuple-element.143) | copy-start | bytes 13828
  166.8 94.0 %copy-start.53 = (f32[1152]{0:T(1024)}, f32[1152]{0:T(1024)S(1)}, u32[]{:S(2)}) copy-start(f32[1152]{0:T(1024)S(1)} %get-tuple-element.144) | copy-start | bytes 13828
  166.8 95.9 %copy-start.55 = (f32[1152]{0:T(1024)}, f32[1152]{0:T(1024)S(1)}, u32[]{:S(2)}) copy-start(f32[1152]{0:T(1024)S(1)} %get-tuple-element.141) | copy-start | bytes 13828
  170.4 90.5 %copy-start.57 = (f32[512]{0:T(512)}, f32[512]{0:T(512)S(1)}, u32[]{:S(2)}) copy-start(f32[512]{0:T(512)S(1)} %broadcast_multiply_fusion.1) | copy-start | bytes 6148
  184.6 18.8 %collective-permute-start.10 = (bf16[512,2304]{1,0:T(8,128)(2,1)}, bf16[512,2304]{1,0:T(8,128)(2,1)}, u32[]{:S(2)}, u32[]{:S(2)}) collective-permute-start(bf16[512,2304]{1,0:T(8,128)(2,1)} %slice.78), channel_id=1, source_target_pairs={{0,4},{4,0},{8,12},{12,8},{16,20},{20,16},{24,28},{28,24},{1,5},{5... | collective-permute-start | bytes 7077896 | tf_op jit(solution)/shard_map/ppermute | solution.py:816
  184.7 259.7 %reduce-scatter.4.cloned.1.call-start = ((), (), s32[]{:S(2)}) async-start(), calls=%async_computation.7 | async-start | bytes 3538944 | tf_op jit(solution)/shard_map/reduce_scatter | solution.py:898
  193.0 71.3 %collective-permute-start.13 = (bf16[384,1920]{1,0:T(8,128)(2,1)}, bf16[384,1920]{1,0:T(8,128)(2,1)}, u32[]{:S(2)}, u32[]{:S(2)}) collective-permute-start(bf16[384,1920]{1,0:T(8,128)(2,1)} %get-tuple-element.163), channel_id=1, source_target_pairs={{3,0},{0,1},{5,6},{6,7},{11,8},{8,9},{13,14},{14,15},{19,16},{16,1... | collective-permute-start | bytes 4423688 | tf_op jit(solution)/shard_map/ppermute | solution.py:848
  196.4 67.8 %collective-permute-start.12 = (bf16[384,1920]{1,0:T(8,128)(2,1)}, bf16[384,1920]{1,0:T(8,128)(2,1)}, u32[]{:S(2)}, u32[]{:S(2)}) collective-permute-start(bf16[384,1920]{1,0:T(8,128)(2,1)} %get-tuple-element.164), channel_id=1, source_target_pairs={{2,0},{3,1},{4,6},{5,7},{10,8},{11,9},{12,14},{13,15},{18,16},{19,... | collective-permute-start | bytes 4423688 | tf_op jit(solution)/shard_map/ppermute | solution.py:848
  197.7 66.5 %collective-permute-start.11 = (bf16[384,1920]{1,0:T(8,128)(2,1)}, bf16[384,1920]{1,0:T(8,128)(2,1)}, u32[]{:S(2)}, u32[]{:S(2)}) collective-permute-start(bf16[384,1920]{1,0:T(8,128)(2,1)} %get-tuple-element.165), channel_id=1, source_target_pairs={{1,0},{2,1},{7,6},{4,7},{9,8},{10,9},{15,14},{12,15},{17,16},{18,1... | collective-permute-start | bytes 4423688 | tf_op jit(solution)/shard_map/ppermute | solution.py:848
  277.7 8.9 %collective-permute-start.18 = (bf16[512,1920]{1,0:T(8,128)(2,1)}, bf16[512,1920]{1,0:T(8,128)(2,1)}, u32[]{:S(2)}, u32[]{:S(2)}) collective-permute-start(bf16[512,1920]{1,0:T(8,128)(2,1)} %constant_dynamic-slice_fusion), channel_id=1, source_target_pairs={{0,4},{4,0},{8,12},{12,8},{16,20},{20,16},{24,28},{28,24},{1,5},{5... | collective-permute-start | bytes 5898248 | tf_op jit(solution)/shard_map/ppermute | solution.py:816
  352.3 141.5 %reduce-scatter.6.cloned.1.call-start = ((), (), s32[]{:S(2)}) async-start(), calls=%async_computation.8 | async-start | bytes 9437184 | tf_op jit(solution)/shard_map/reduce_scatter | solution.py:898
  352.3 84.0 %collective-permute-start.14 = (bf16[512,1152]{1,0:T(8,128)(2,1)S(1)}, bf16[512,1152]{1,0:T(8,128)(2,1)}, u32[]{:S(2)}, u32[]{:S(2)}) collective-permute-start(bf16[512,1152]{1,0:T(8,128)(2,1)S(1)} %add_convert_fusion.2), channel_id=1, source_target_pairs={{0,4},{4,0},{8,12},{12,8},{16,20},{20,16},{24,28},{28,24},{1,5},{5... | collective-permute-start | bytes 3538952 | tf_op jit(solution)/shard_map/ppermute | solution.py:816
  367.9 215.3 %reduce-scatter.8.cloned.1.call-start = ((), (), s32[]{:S(2)}) async-start(), calls=%async_computation.9 | async-start | bytes 5308416 | tf_op jit(solution)/shard_map/reduce_scatter | solution.py:898
  507.3 42.1 %collective-permute-start.19 = (bf16[512,2304]{1,0:T(8,128)(2,1)}, bf16[512,2304]{1,0:T(8,128)(2,1)}, u32[]{:S(2)}, u32[]{:S(2)}) collective-permute-start(bf16[512,2304]{1,0:T(8,128)(2,1)} %pad_maximum_fusion.2), channel_id=1, source_target_pairs={{0,4},{4,0},{8,12},{12,8},{16,20},{20,16},{24,28},{28,24},{1,5},{5... | collective-permute-start | bytes 7077896 | tf_op jit(solution)/shard_map/ppermute | solution.py:816
  509.1 12.1 %collective-permute-start.15 = (bf16[384,1152]{1,0:T(8,128)(2,1)}, bf16[384,1152]{1,0:T(8,128)(2,1)S(1)}, u32[]{:S(2)}, u32[]{:S(2)}) collective-permute-start(bf16[384,1152]{1,0:T(8,128)(2,1)} %get-tuple-element.160), channel_id=1, source_target_pairs={{0,1},{1,2},{6,7},{7,4},{8,9},{9,10},{14,15},{15,12},{16,17},{17,1... | collective-permute-start | bytes 2654216 | tf_op jit(solution)/shard_map/ppermute | solution.py:875
  510.4 26.7 %collective-permute-start.17 = (bf16[384,1152]{1,0:T(8,128)(2,1)}, bf16[384,1152]{1,0:T(8,128)(2,1)}, u32[]{:S(2)}, u32[]{:S(2)}) collective-permute-start(bf16[384,1152]{1,0:T(8,128)(2,1)} %get-tuple-element.161), channel_id=1, source_target_pairs={{0,3},{1,0},{6,5},{7,6},{8,11},{9,8},{14,13},{15,14},{16,19},{17,1... | collective-permute-start | bytes 2654216 | tf_op jit(solution)/shard_map/ppermute | solution.py:875
  512.4 27.9 %collective-permute-start.16 = (bf16[384,1152]{1,0:T(8,128)(2,1)}, bf16[384,1152]{1,0:T(8,128)(2,1)}, u32[]{:S(2)}, u32[]{:S(2)}) collective-permute-start(bf16[384,1152]{1,0:T(8,128)(2,1)} %get-tuple-element.162), channel_id=1, source_target_pairs={{0,2},{1,3},{6,4},{7,5},{8,10},{9,11},{14,12},{15,13},{16,18},{17,... | collective-permute-start | bytes 2654216 | tf_op jit(solution)/shard_map/ppermute | solution.py:875
  563.0 14.0 %collective-permute-start.20 = (bf16[512,1152]{1,0:T(8,128)(2,1)S(1)}, bf16[512,1152]{1,0:T(8,128)(2,1)S(1)}, u32[]{:S(2)}, u32[]{:S(2)}) collective-permute-start(bf16[512,1152]{1,0:T(8,128)(2,1)S(1)} %add_convert_fusion.1), channel_id=1, source_target_pairs={{0,4},{4,0},{8,12},{12,8},{16,20},{20,16},{24,28},{28,24},{1,5},{5... | collective-permute-start | bytes 3538952 | tf_op jit(solution)/shard_map/ppermute | solution.py:816
  (81 other events, 547.9 us)
Sparse Core Ops, SparseCore 0:
  9.9 87.5 all-gather.4
  99.4 79.4 all-gather.6
  180.7 38.9 all-gather.8
  221.4 54.4 all-gather.10
  352.4 44.2 reduce-scatter.3
  400.4 71.2 reduce-scatter.5
  515.4 54.0 reduce-scatter.7

commit v3 on v2

--- a/solution.py
+++ b/solution.py
@@ -13,6 +13,7 @@
 LROWS = 32
 TOTAL = LROWS * RW
 SCALE = HDIM ** (-0.5)
+LOG2E = 1.4426950408889634
 LAST = (((1,), (1,)), ((), ()))
 FIRST = (((0,), (0,)), ((), ()))
 
@@ -58,129 +59,221 @@
     return jax.vjp(gelu_tanh, operand)[1](gradient)[0]
 
 
-def attend_kernel(q_ref, k_ref, v_ref, o_ref, lse_ref):
-    length = q_ref.shape[1]
+MESH = pl.DeviceIdType.MESH
+WINDOW = 256
+
+
+def head_window(head, width):
+    first = jnp.minimum(head * HDIM // 128, (width - WINDOW) // 128) * 128
+    lane = lax.broadcasted_iota(jnp.int32, (1, WINDOW), 1) + first - head * HDIM
+    return first, (lane >= 0) & (lane < HDIM)
+
+
+def columns_at(first, part, width):
+    return pl.ds(pl.multiple_of(first + part * width, 128), WINDOW)
+
+
+def attend_kernel(own_ref, rest_ref, mix_ref, lse_ref):
+    length, width = mix_ref.shape
     block = min(256, length)
-    keys, values = k_ref[0], v_ref[0]
-    for at in range(0, length, block):
-        rows = pl.ds(at, block)
-        scores = lax.dot_general(q_ref[0, rows, :], keys, LAST, preferred_element_type=jnp.float32)
-        scores = scores * SCALE
-        top = jnp.max(scores, axis=1, keepdims=True)
-        weight = jnp.exp(scores - top)
-        total = jnp.sum(weight, axis=1, keepdims=True)
-        mixed = jnp.dot(weight.astype(jnp.bfloat16), values, preferred_element_type=jnp.float32)
-        o_ref[0, rows, :] = (mixed / total).astype(o_ref.dtype)
-        log_total = jnp.broadcast_to(top + jnp.log(total), (block, 128))
-        lse_ref[0, :, rows] = log_total.T[:1, :]
-
-
-def attend(queries, keys, values):
-    heads, length, width = queries.shape
-    span = keys.shape[1]
+
+    def one_head(head, carry):
+        first, mine = head_window(head, width)
+        mix_columns = columns_at(first, 0, width)
+        key_refs = [own_ref.at[:, columns_at(first, 1, width)]]
+        key_refs.append(rest_ref.at[:, columns_at(first, 0, width)])
+        value_refs = [own_ref.at[:, columns_at(first, 2, width)]]
+        value_refs.append(rest_ref.at[:, columns_at(first, 1, width)])
+        keys, values = [ref[...] for ref in key_refs], [ref[...] for ref in value_refs]
+        for at in range(0, length, block):
+            rows = pl.ds(at, block)
+            queries = jnp.where(mine, own_ref[rows, mix_columns], jnp.bfloat16(0))
+            scores = [
+                lax.dot_general(queries, part, LAST, preferred_element_type=jnp.float32)
+                for part in keys
+            ]
+            tops = [jnp.max(part, axis=1, keepdims=True) for part in scores]
+            top = jnp.maximum(tops[0], tops[1])
+            top = top * (SCALE * LOG2E)
+            weights = [jnp.exp2(part * (SCALE * LOG2E) - top) for part in scores]
+            total = sum(jnp.sum(part, axis=1, keepdims=True) for part in weights)
+            mixed = sum(
+                jnp.dot(part.astype(jnp.bfloat16), value, preferred_element_type=jnp.float32)
+                for part, value in zip(weights, values)
+            )
+            mixed = (mixed / total).astype(mix_ref.dtype)
+            mix_ref[rows, mix_columns] = jnp.where(mine, mixed, mix_ref[rows, mix_columns])
+            log_total = jnp.broadcast_to(top + jnp.log(total) * LOG2E, (block, 128))
+            lse_ref[head, :, rows] = log_total.T[:1, :]
+        return carry
+
+    mix_ref[...] = jnp.zeros_like(mix_ref)
+    lax.fori_loop(0, HEADS, one_head, 0)
+
+
+def attend(own, rest, width):
+    length, span = own.shape[0], own.shape[0] + rest.shape[0]
+    vmem, bf16 = pl.BlockSpec(memory_space=pltpu.VMEM), jnp.bfloat16
     return pl.pallas_call(
         attend_kernel,
-        grid=(heads,),
-        in_specs=[
-            pl.BlockSpec((1, length, width), lambda h: (h, 0, 0)),
-            pl.BlockSpec((1, span, width), lambda h: (h, 0, 0)),
-            pl.BlockSpec((1, span, width), lambda h: (h, 0, 0)),
+        in_specs=[vmem] * 2,
+        out_specs=[vmem] * 2,
+        out_shape=[
+            jax.ShapeDtypeStruct((length, width), bf16),
+            jax.ShapeDtypeStruct((HEADS, 1, length), jnp.float32),
         ],
-        out_specs=[
-            pl.BlockSpec((1, length, width), lambda h: (h, 0, 0)),
-            pl.BlockSpec((1, 1, length), lambda h: (h, 0, 0)),
-        ],
-        out_shape=[
-            jax.ShapeDtypeStruct((heads, length, width), jnp.bfloat16),
-            jax.ShapeDtypeStruct((heads, 1, length), jnp.float32),
-        ],
-        compiler_params=pltpu.CompilerParams(vmem_limit_bytes=48 * 1024 * 1024),
+        compiler_params=pltpu.CompilerParams(vmem_limit_bytes=56 * 1024 * 1024),
         cost_estimate=pl.CostEstimate(
-            flops=4 * heads * length * span * 256,
-            bytes_accessed=4 * heads * (length + span) * 128,
-            transcendentals=heads * length * span,
+            flops=4 * HEADS * length * span * 256,
+            bytes_accessed=4 * (length + span) * width * 2,
+            transcendentals=HEADS * length * span,
         ),
         name="attend",
-    )(queries, keys, values)
-
-
-def attend_back_kernel(q_ref, k_ref, v_ref, o_ref, d_ref, lse_ref, dq_ref, dk_ref, dv_ref):
-    length, width = q_ref.shape[1], q_ref.shape[2]
-    span = k_ref.shape[1]
+    )(own, rest)
+
+
+def greet(where):
+    barrier = pltpu.get_barrier_semaphore()
+    pl.semaphore_signal(barrier, inc=1, device_id=where, device_id_type=MESH)
+
+
+class Give:
+    def __init__(self, group, per, spread, given, send_sem, recv_sem):
+        self.group, self.per = group, per
+        self.spread, self.given, self.send_sem, self.recv_sem = spread, given, send_sem, recv_sem
+        self.row = lax.axis_index("row")
+        self.slots = given.shape[1]
+
+    def greet(self):
+        for shift in range(1, 4):
+            greet({"row": lax.rem(self.row + shift, 4)})
+
+    def copy(self, shift, rows):
+        return pltpu.make_async_remote_copy(
+            src_ref=self.spread.at[shift, rows, :],
+            dst_ref=self.given.at[shift - 1, rows, :],
+            send_sem=self.send_sem.at[shift - 1],
+            recv_sem=self.recv_sem.at[shift - 1],
+            device_id={"row": lax.rem(self.row + shift, 4)},
+            device_id_type=MESH,
+        )
+
+    def from_here(self, row):
+        return (row // self.group) // self.per == lax.rem(lax.axis_index("img"), 2)
+
+    def start(self, at, amount):
+        @pl.when((at < self.slots // amount) & self.from_here(self.row))
+        def _():
+            for shift in range(1, 4):
+                rows = pl.ds(pl.multiple_of(at * amount, amount), amount)
+                self.copy(shift, rows).start()
+
+    def wait(self):
+        for shift in range(1, 4):
+            whole = self.copy(shift, pl.ds(0, self.slots))
+
+            @pl.when(self.from_here(self.row))
+            def _(whole=whole):
+                whole.wait_send()
+
+            @pl.when(self.from_here(lax.rem(self.row + 4 - shift, 4)))
+            def _(whole=whole):
+                whole.wait_recv()
+
+
+def attend_back_kernel(
+    give, own_ref, rest_ref, mix_ref, d_ref, lse_ref, spread, dq_ref, own_out, rest_out, given, *sems
+):
+    length, width = mix_ref.shape
     block = 256
-    queries, d_mix = q_ref[0], d_ref[0]
-    product = d_mix.astype(jnp.float32) * o_ref[0].astype(jnp.float32)
-    delta = lax.dot_general(
-        jnp.ones((8, width), jnp.float32),
-        product,
-        LAST,
-        precision=lax.Precision.HIGHEST,
-        preferred_element_type=jnp.float32,
-    )[:1, :]
-    log_total = lse_ref[0]
-    d_query = jnp.zeros((length, width), jnp.float32)
-    for at in range(0, span, block):
-        rows = pl.ds(at, block)
-        keys, values = k_ref[0, rows, :], v_ref[0, rows, :]
-        scores = lax.dot_general(keys, queries, LAST, preferred_element_type=jnp.float32) * SCALE
-        prob = jnp.exp(scores - log_total)
-        d_prob = lax.dot_general(values, d_mix, LAST, preferred_element_type=jnp.float32)
-        d_score = (prob * (d_prob - delta)).astype(jnp.bfloat16)
-        dv_ref[0, rows, :] = jnp.dot(
-            prob.astype(jnp.bfloat16), d_mix, preferred_element_type=jnp.float32
-        ).astype(dv_ref.dtype)
-        dk_ref[0, rows, :] = (
-            jnp.dot(d_score, queries, preferred_element_type=jnp.float32) * SCALE
-        ).astype(dk_ref.dtype)
-        d_query += lax.dot_general(d_score, keys, FIRST, preferred_element_type=jnp.float32)
-    dq_ref[0] = (d_query * SCALE).astype(dq_ref.dtype)
-
-
-def attend_back(queries, keys, values, mixed, d_mix, log_total):
-    heads, length, width = queries.shape
-    span = keys.shape[1]
-    short = pl.BlockSpec((1, length, width), lambda h: (h, 0, 0))
-    long = pl.BlockSpec((1, span, width), lambda h: (h, 0, 0))
+    if give:
+        sender = Give(*give, spread, given, *sems)
+        sender.greet()
+        pl.semaphore_wait(pltpu.get_barrier_semaphore(), 3)
+        sender.start(0, given.shape[1])
+    for ref in (dq_ref, own_out, rest_out):
+        ref[...] = jnp.zeros_like(ref)
+
+    def one_head(head, carry):
+        first, mine = head_window(head, width)
+        here, next_part = columns_at(first, 0, width), columns_at(first, 1, width)
+        queries = jnp.where(mine, own_ref[:, here], jnp.bfloat16(0))
+        d_mix = jnp.where(mine, d_ref[:, here], jnp.bfloat16(0))
+        product = d_mix.astype(jnp.float32) * mix_ref[:, here].astype(jnp.float32)
+        delta = lax.dot_general(
+            jnp.ones((8, WINDOW), jnp.float32),
+            product,
+            LAST,
+            precision=lax.Precision.HIGHEST,
+            preferred_element_type=jnp.float32,
+        )[:1, :]
+        log_total = lse_ref[head]
+        d_query = jnp.zeros((length, WINDOW), jnp.float32)
+        runs = [(own_ref, 1, own_out, at) for at in range(0, length, block)]
+        runs += [(rest_ref, 0, rest_out, at) for at in range(0, rest_ref.shape[0], block)]
+        for source, part, target, at in runs:
+            rows = pl.ds(at, block)
+            keys = source[rows, columns_at(first, part, width)]
+            values = source[rows, columns_at(first, part + 1, width)]
+            scores = lax.dot_general(keys, queries, LAST, preferred_element_type=jnp.float32)
+            prob = jnp.exp2(scores * (SCALE * LOG2E) - log_total)
+            d_prob = lax.dot_general(values, d_mix, LAST, preferred_element_type=jnp.float32)
+            d_score = (prob * (d_prob - delta)).astype(jnp.bfloat16)
+            d_key = jnp.dot(d_score, queries, preferred_element_type=jnp.float32) * SCALE
+            d_value = jnp.dot(
+                prob.astype(jnp.bfloat16), d_mix, preferred_element_type=jnp.float32
+            )
+            target[rows, here] += d_key.astype(target.dtype)
+            target[rows, next_part] += d_value.astype(target.dtype)
+            d_query += lax.dot_general(d_score, keys, FIRST, preferred_element_type=jnp.float32)
+        d_query = jnp.where(mine, d_query * SCALE, 0.0)
+        dq_ref[:, here] += d_query.astype(dq_ref.dtype)
+        return carry
+
+    lax.fori_loop(0, HEADS, one_head, 0)
+    if give:
+        sender.wait()
+
+
+def attend_back(own, rest, mixed, d_mix, log_total, spread, give):
+    length, width = mixed.shape
+    span = length + rest.shape[0]
+    vmem, bf16 = pl.BlockSpec(memory_space=pltpu.VMEM), jnp.bfloat16
+    hbm = pl.BlockSpec(memory_space=pl.ANY)
+    remote = dict(collective_id=2, has_side_effects=True) if give else {}
     return pl.pallas_call(
-        attend_back_kernel,
-        grid=(heads,),
-        in_specs=[
-            short,
-            long,
-            long,
-            short,
-            short,
-            pl.BlockSpec((1, 1, length), lambda h: (h, 0, 0)),
+        functools.partial(attend_back_kernel, give),
+        in_specs=[vmem] * 5 + [hbm],
+        out_specs=[vmem] * 3 + [hbm],
+        out_shape=[
+            jax.ShapeDtypeStruct((length, width), bf16),
+            jax.ShapeDtypeStruct((length, 2 * width), bf16),
+            jax.ShapeDtypeStruct((span - length, 2 * width), bf16),
+            jax.ShapeDtypeStruct((spread.shape[0] - 1, *spread.shape[1:]), bf16),
         ],
-        out_specs=[short, long, long],
-        out_shape=[
-            jax.ShapeDtypeStruct((heads, length, width), jnp.bfloat16),
-            jax.ShapeDtypeStruct((heads, span, width), jnp.bfloat16),
-            jax.ShapeDtypeStruct((heads, span, width), jnp.bfloat16),
-        ],
-        compiler_params=pltpu.CompilerParams(vmem_limit_bytes=48 * 1024 * 1024),
+        scratch_shapes=[pltpu.SemaphoreType.DMA((3,))] * 2 if give else [],
+        compiler_params=pltpu.CompilerParams(vmem_limit_bytes=56 * 1024 * 1024, **remote),
         cost_estimate=pl.CostEstimate(
-            flops=10 * heads * length * span * 256,
-            bytes_accessed=10 * heads * (length + span) * 128,
-            transcendentals=heads * length * span,
+            flops=10 * HEADS * length * span * 256,
+            bytes_accessed=8 * (length + span) * width * 2,
+            transcendentals=HEADS * length * span,
         ),
         name="attend_back",
-    )(queries, keys, values, mixed, d_mix, log_total)
-
-
-MESH = pl.DeviceIdType.MESH
+    )(own, rest, mixed, d_mix, log_total, spread)
+
+
 TILE_ROWS = 144
 TILE_COLUMNS = 384
 CUT = 80
 SLOTS = 4
 LINE_SLOTS = 8
 LINE_TILE = 256
-SIDE_PACE = 3
+SIDE_PACE = 4
 GIVE_ROWS = 16
 
 
 def add(one, other):
-    return (one.astype(jnp.float32) + other.astype(jnp.float32)).astype(jnp.bfloat16)
+    return one + other
 
 
 def mates():
@@ -189,19 +282,117 @@
     return me, (core, x, y), (me + 1 - 2 * core, me + 2 - 4 * x, me + 4 - 8 * y)
 
 
-def greet(where):
-    barrier = pltpu.get_barrier_semaphore()
-    pl.semaphore_signal(barrier, inc=1, device_id=where, device_id_type=MESH)
-
-
-def gather_kernel(count, *refs):
-    blocks, wholes = refs[:count], refs[count : 2 * count]
-    send_sem, recv_sem, local_sem = refs[2 * count :]
+def gather_kernel(count, group, per, *refs):
+    take = iter(refs)
+    blocks = [next(take) for _ in range(count)]
+    slots = [next(take) for _ in range(3)]
+    part = next(take)
+    wholes = [next(take) for _ in range(count)]
+    arrivals = [next(take) for _ in range(3)]
+    total = next(take)
+    part_in, part_sum, send_sem, recv_sem, local_sem, slot_send, slot_recv, slot_local = [
+        next(take) for _ in range(8)
+    ]
+    part_send, part_recv = take
+    row = lax.axis_index("row")
     me, (core, x, y), (sibling, x_mate, y_mate) = mates()
     far = x_mate + 4 - 8 * y
     for mate in (sibling, x_mate, y_mate):
         greet({"img": mate})
-    pl.semaphore_wait(pltpu.get_barrier_semaphore(), 3)
+    for shift in range(1, 4):
+        greet({"row": lax.rem(row + shift, 4)})
+    pl.semaphore_wait(pltpu.get_barrier_semaphore(), 6)
+
+    def place_of(place):
+        return (place // group) // per, lax.rem(place // group, per)
+
+    takes_in = place_of(row)[0] == core
+
+    def by_row(which, shift):
+        where = lax.rem(row + 4 - shift, 4)
+        return pltpu.make_async_remote_copy(
+            src_ref=slots[which].at[place_of(where)[1]],
+            dst_ref=arrivals[which].at[row],
+            send_sem=slot_send.at[which, shift - 1],
+            recv_sem=slot_recv.at[which, shift - 1],
+            device_id={"row": where},
+            device_id_type=MESH,
+        )
+
+    def own_slots(which):
+        source = slots[which].at[place_of(row)[1]]
+        return pltpu.make_async_copy(source, arrivals[which].at[row], slot_local.at[which])
+
+    def by_core(which, shift):
+        origin = lax.rem(row + shift, 4)
+        source = arrivals[which].at[origin] if shift else slots[which].at[place_of(row)[1]]
+        return pltpu.make_async_remote_copy(
+            src_ref=source,
+            dst_ref=arrivals[which].at[origin],
+            send_sem=slot_send.at[which, 3 + shift],
+            recv_sem=slot_recv.at[which, 3 + shift],
+            device_id={"img": sibling},
+            device_id_type=MESH,
+        )
+
+    def start_slots(which):
+        for shift in range(1, 4):
+
+            @pl.when(place_of(lax.rem(row + 4 - shift, 4))[0] == core)
+            def _(shift=shift):
+                by_row(which, shift).start()
+
+        @pl.when(takes_in)
+        def _():
+            own_slots(which).start()
+            by_core(which, 0).start()
+
+    def pass_slots(which):
+        for shift in range(1, 4):
+
+            @pl.when(takes_in)
+            def _(shift=shift):
+                by_row(which, shift).wait_recv()
+                by_core(which, shift).start()
+
+    def end_slots(which):
+        for shift in range(1, 4):
+
+            @pl.when(place_of(lax.rem(row + 4 - shift, 4))[0] == core)
+            def _(shift=shift):
+                by_row(which, shift).wait_send()
+
+        @pl.when(takes_in)
+        def _():
+            own_slots(which).wait()
+            for shift in range(4):
+                by_core(which, shift).wait_send()
+
+        @pl.when(jnp.logical_not(takes_in))
+        def _():
+            for shift in range(4):
+                by_core(which, shift).wait_recv()
+
+    part_mates = [sibling, x_mate, y_mate]
+
+    def part_hop(hop):
+        return pltpu.make_async_remote_copy(
+            src_ref=part_sum.at[hop - 1] if hop else part,
+            dst_ref=part_in.at[hop],
+            send_sem=part_send.at[hop],
+            recv_sem=part_recv.at[hop],
+            device_id={"img": part_mates[hop]},
+            device_id_type=MESH,
+        )
+
+    def take_part(hop):
+        part_hop(hop).wait()
+        summed = (part_sum[hop - 1] if hop else part[...]) + part_in[hop]
+        if hop == 2:
+            total[...] = summed
+        else:
+            part_sum[hop] = summed
+            part_hop(hop + 1).start()
 
     def halves(at):
         rows = blocks[at].shape[0]
@@ -249,10 +440,15 @@
         pltpu.make_async_copy(blocks[at], wholes[at].at[me], local_sem.at[at])
         for at in range(count)
     ]
+    part_hop(0).start()
+    start_slots(0)
     for at in range(count):
         for kind in (0, 1, 6, 7):
             every[at][kind].start()
         locals_[at].start()
+    take_part(0)
+    start_slots(1)
+    start_slots(2)
     for at in range(count):
         found = every[at]
         found[0].wait_recv()
@@ -263,36 +459,107 @@
         found[5].start()
         found[3].start()
         found[9].start()
+    take_part(1)
+    pass_slots(0)
     for at in range(count):
         found = every[at]
         for kind in (4, 5, 2, 3):
             found[kind].wait_recv()
             found[8 + kind].start()
+    take_part(2)
+    pass_slots(1)
+    pass_slots(2)
     for at in range(count):
         for kind, one in enumerate(every[at]):
             if kind >= 6:
                 one.wait_recv()
             one.wait_send()
         locals_[at].wait()
-
-
-def gather_weights(blocks):
+    for which in range(3):
+        end_slots(which)
+
+
+def gather_weights(blocks, slots, part, group, per):
     count = len(blocks)
+    vmem, hbm = pl.BlockSpec(memory_space=pltpu.VMEM), pl.BlockSpec(memory_space=pl.ANY)
+    part_rows = part.size // 128
     results = pl.pallas_call(
-        functools.partial(gather_kernel, count),
-        in_specs=[pl.BlockSpec(memory_space=pl.ANY)] * count,
-        out_specs=[pl.BlockSpec(memory_space=pl.ANY)] * count,
-        out_shape=[jax.ShapeDtypeStruct((8, *block.shape), block.dtype) for block in blocks],
+        functools.partial(gather_kernel, count, group, per),
+        in_specs=[hbm] * (count + 3) + [vmem],
+        out_specs=[hbm] * (count + 3) + [vmem],
+        out_shape=[
+            *[jax.ShapeDtypeStruct((8, *block.shape), block.dtype) for block in blocks],
+            *[jax.ShapeDtypeStruct((4, *one.shape[1:]), one.dtype) for one in slots],
+            jax.ShapeDtypeStruct((part_rows, 128), jnp.float32),
+        ],
         scratch_shapes=[
+            pltpu.VMEM((3, part_rows, 128), jnp.float32),
+            pltpu.VMEM((2, part_rows, 128), jnp.float32),
             pltpu.SemaphoreType.DMA((count, 14)),
             pltpu.SemaphoreType.DMA((count, 14)),
             pltpu.SemaphoreType.DMA((count,)),
+            pltpu.SemaphoreType.DMA((3, 7)),
+            pltpu.SemaphoreType.DMA((3, 7)),
+            pltpu.SemaphoreType.DMA((3,)),
+            pltpu.SemaphoreType.DMA((3,)),
+            pltpu.SemaphoreType.DMA((3,)),
         ],
         compiler_params=pltpu.CompilerParams(collective_id=1, has_side_effects=True),
         cost_estimate=pl.CostEstimate(flops=0, bytes_accessed=200000000, transcendentals=0),
         name="gather_weights",
-    )(*blocks)
-    return [whole.reshape(-1, whole.shape[-1]) for whole in results]
+    )(*blocks, *slots, part.reshape(part_rows, 128))
+    wholes = [whole.reshape(-1, whole.shape[-1]) for whole in results[:count]]
+    return wholes, results[count : count + 3], results[-1].reshape(-1)
+
+
+def compact_kernel(places, *refs):
+    sources, (shift, scale), targets, (h_att, sems) = refs[:3], refs[3:5], refs[5:8], refs[8:]
+    amount = targets[0].shape[0] // RW
+
+    def one(at, carry):
+        begin = pl.multiple_of(places[at], RW)
+        rows = pl.ds(pl.multiple_of(at * RW, RW), RW)
+        for which in range(3):
+            source = sources[which].at[pl.ds(begin, RW), :]
+            pltpu.make_async_copy(source, targets[which].at[rows, :], sems.at[which]).start()
+        return carry
+
+    lax.fori_loop(0, amount, one, 0)
+
+    def wait(which):
+        rows = pl.ds(0, targets[which].shape[0])
+        source = sources[which].at[rows, :]
+        pltpu.make_async_copy(source, targets[which], sems.at[which]).wait()
+
+    wait(0)
+
+    def norm(at, carry):
+        rows = pl.ds(pl.multiple_of(at * 64, 64), 64)
+        block = targets[0][rows, :].astype(jnp.float32)
+        block = modulate(block, shift[...], scale[...])
+        h_att[rows, :] = block.astype(jnp.bfloat16)
+        return carry
+
+    lax.fori_loop(0, targets[0].shape[0] // 64, norm, 0)
+    wait(1)
+    wait(2)
+
+
+def compact(places, slots, shift, scale):
+    length = places.shape[0] * RW
+    flat = [one.reshape(-1, one.shape[-1]) for one in slots]
+    vmem, hbm = pl.BlockSpec(memory_space=pltpu.VMEM), pl.BlockSpec(memory_space=pl.ANY)
+    shapes = [jax.ShapeDtypeStruct((length, one.shape[1]), one.dtype) for one in flat]
+    return pl.pallas_call(
+        compact_kernel,
+        in_specs=[pl.BlockSpec(memory_space=pltpu.SMEM), *[hbm] * 3, vmem, vmem],
+        out_specs=[vmem] * 4,
+        out_shape=[*shapes, shapes[0]],
+        scratch_shapes=[pltpu.SemaphoreType.DMA((3,))],
+        compiler_params=pltpu.CompilerParams(vmem_limit_bytes=32 * 1024 * 1024),
+        cost_estimate=pl.CostEstimate(flops=0, bytes_accessed=8000000, transcendentals=0),
+        name="compact",
+    )(places, *flat, shift, scale)
 
 
 class Line:
@@ -431,25 +698,22 @@
     lefts = [next(take) for _ in range(count)]
     rights = [next(take) for _ in range(count)]
     image_part, bias_part, spread = next(take), next(take), next(take)
-    parts = [next(take) for _ in range(3)]
+    parts = [next(take) for _ in range(2)]
     results = [next(take) for _ in range(count)]
     every_image, bias_total, given = next(take), next(take), next(take)
-    part_results = [next(take) for _ in range(3)]
+    part_results = [next(take) for _ in range(2)]
     grads, core_in, pair, upper_in, lower_in, upper_two, lower_two = [next(take) for _ in range(7)]
     main_buffers = [next(take) for _ in range(5)]
     tall_buffers = [next(take) for _ in range(5)]
-    flat_buffers = [next(take) for _ in range(5)]
     image_in, bias_in, small_send, small_recv = [next(take) for _ in range(4)]
     send_sem, recv_sem, store_sem, load_sem, give_send, give_recv, credit = take
     row = lax.axis_index("row")
     near_row, far_row = row + 1 - 2 * lax.rem(row, 2), lax.rem(row + 2, 4)
     main = Line(5, main_buffers, (send_sem, recv_sem, store_sem.at[0], credit))
     tall = Line(8, tall_buffers, (send_sem, recv_sem, store_sem.at[1], credit))
-    flat = Line(11, flat_buffers, (send_sem, recv_sem, store_sem.at[2], credit))
-    tall.load_sem, flat.load_sem = load_sem.at[0], load_sem.at[1]
-    lengths = [
-        left.shape[1] * (right.shape[1] // TILE_COLUMNS) for left, right in zip(lefts, rights)
-    ]
+    tall.load_sem = load_sem
+    across = [-(-right.shape[1] // TILE_COLUMNS) for right in rights]
+    lengths = [left.shape[1] * amount for left, amount in zip(lefts, across)]
     chunks = sum(lengths)
     _, (core, x, y), (sibling, x_mate, y_mate) = mates()
     upper, lower = pl.ds(0, CUT), pl.ds(CUT, TILE_ROWS - CUT)
@@ -457,9 +721,8 @@
     def main_targets(chunk, body):
         def one(which, at):
             result = results[which]
-            per_row = result.shape[2] // TILE_COLUMNS
-            columns = tile_columns(lax.rem(at, per_row), TILE_COLUMNS)
-            body(result.at[at // per_row, :, columns])
+            columns = tile_columns(lax.rem(at, across[which]), TILE_COLUMNS)
+            body(result.at[at // across[which], :, columns])
 
         pieces(lengths, chunk, one)
 
@@ -480,8 +743,7 @@
         line.sources, line.targets = view(origins), view(ends)
         return sum(amounts)
 
-    tall_tiles = side_tiles(tall, parts[1:], part_results[1:])
-    flat_tiles = side_tiles(flat, parts[:1], part_results[:1])
+    tall_tiles = side_tiles(tall, parts, part_results)
 
     def remote(stage, slot, source, target, where):
         return pltpu.make_async_remote_copy(
@@ -520,8 +782,8 @@
 
     for mate in (sibling, x_mate, y_mate):
         greet({"img": mate})
-    for shift in range(1, 4):
-        greet({"row": lax.rem(row + shift, 4)})
+    sender = Give(group, per, spread, given, give_send, give_recv)
+    sender.greet()
     pl.semaphore_wait(pltpu.get_barrier_semaphore(), 6)
 
     def small(kind, source, target, where):
@@ -558,39 +820,6 @@
             every_image[row, y, x] = summed.astype(jnp.bfloat16)
         bias_total[...] = (bias_total if hop else bias_part)[...] + bias_in[hop]
 
-    slot_len = given.shape[1]
-
-    def giving(shift, rows):
-        return pltpu.make_async_remote_copy(
-            src_ref=spread.at[shift, rows, :],
-            dst_ref=given.at[shift - 1, rows, :],
-            send_sem=give_send.at[shift - 1],
-            recv_sem=give_recv.at[shift - 1],
-            device_id={"row": lax.rem(row + shift, 4)},
-            device_id_type=MESH,
-        )
-
-    def owner_core(place):
-        return (place // group) // per
-
-    def give_some(at):
-        @pl.when((at < slot_len // GIVE_ROWS) & (owner_core(row) == core))
-        def _():
-            for shift in range(1, 4):
-                giving(shift, pl.ds(pl.multiple_of(at * GIVE_ROWS, GIVE_ROWS), GIVE_ROWS)).start()
-
-    def give_wait():
-        for shift in range(1, 4):
-            whole = giving(shift, pl.ds(0, slot_len))
-
-            @pl.when(owner_core(row) == core)
-            def _(whole=whole):
-                whole.wait_send()
-
-            @pl.when(owner_core(lax.rem(row + 4 - shift, 4)) == core)
-            def _(whole=whole):
-                whole.wait_recv()
-
     def own_shard(chunk, slot):
         line_slot = lax.rem(chunk, LINE_SLOTS)
         upper_second(slot).wait()
@@ -631,16 +860,30 @@
     def multiply(chunk, slot):
         def one(which, at):
             left, right = lefts[which], rights[which]
-            per_row = right.shape[1] // TILE_COLUMNS
-            values = right[:, tile_columns(lax.rem(at, per_row), TILE_COLUMNS)]
-            for half in range(2):
-                rows = left[pl.ds(4 * half, 4), at // per_row]
-                product = jnp.dot(
-                    rows.reshape(4 * TILE_ROWS, -1), values, preferred_element_type=jnp.float32
-                )
-                grads[slot, half] = product.astype(jnp.bfloat16).reshape(
-                    2, 2, TILE_ROWS, TILE_COLUMNS
-                )
+            column, whole_tiles = lax.rem(at, across[which]), right.shape[1] // TILE_COLUMNS
+
+            def times(values):
+                for half in range(2):
+                    rows = left[pl.ds(4 * half, 4), at // across[which]]
+                    rows = rows.reshape(4 * TILE_ROWS, -1)
+                    product = jnp.dot(rows, values, preferred_element_type=jnp.float32)
+                    grads[slot, half] = product.astype(jnp.bfloat16).reshape(
+                        2, 2, TILE_ROWS, TILE_COLUMNS
+                    )
+
+            if whole_tiles == across[which]:
+                times(right[:, tile_columns(column, TILE_COLUMNS)])
+                return
+
+            @pl.when(column < whole_tiles)
+            def _():
+                times(right[:, tile_columns(column, TILE_COLUMNS)])
+
+            @pl.when(column == whole_tiles)
+            def _():
+                rest = right[:, whole_tiles * TILE_COLUMNS :]
+                gap = jnp.zeros((rest.shape[0], TILE_COLUMNS - rest.shape[1]), rest.dtype)
+                times(jnp.concatenate([rest, gap], axis=1))
 
         pieces(lengths, chunk, one)
         spend(0, chunk)
@@ -668,8 +911,12 @@
             def _(hop=hop):
                 small_hop(hop, False)
 
-        give_some(at)
-        for line, tiles in ((tall, tall_tiles), (flat, flat_tiles)):
+
+        @pl.when(lax.rem(at, 3) < 2)
+        def _():
+            sender.start(2 * (at // 3) + lax.rem(at, 3), GIVE_ROWS)
+
+        for line, tiles in ((tall, tall_tiles),):
             for lag, body in (
                 (8, line.end),
                 (7, line.last),
@@ -697,9 +944,9 @@
     lax.fori_loop(0, chunks + 12, step, 0)
     for stage in range(5):
         pl.semaphore_wait(credit.at[stage], SLOTS)
-    for line in (main, tall, flat):
+    for line in (main, tall):
         line.drain()
-    give_wait()
+    sender.wait()
 
 
 def turn(operand):
@@ -710,7 +957,9 @@
 def sum_gradients(lefts, rights, image_part, bias_part, spread, parts, group, per):
     bf16 = jnp.bfloat16
     shapes = [
-        jax.ShapeDtypeStruct((left.shape[1], TILE_ROWS, right.shape[1]), bf16)
+        jax.ShapeDtypeStruct(
+            (left.shape[1], TILE_ROWS, -(-right.shape[1] // TILE_COLUMNS) * TILE_COLUMNS), bf16
+        )
         for left, right in zip(lefts, rights)
     ]
     image_rows, bias_rows = image_part.size // 128, bias_part.size // 128
@@ -728,8 +977,8 @@
     flops = 2 * sum(left.size * right.shape[1] for left, right in zip(lefts, rights))
     results = pl.pallas_call(
         functools.partial(sum_kernel, len(lefts), group, per),
-        in_specs=[vmem] * (2 * len(lefts) + 2) + [hbm] * 4,
-        out_specs=[hbm] * len(lefts) + [vmem] * 2 + [hbm] * 4,
+        in_specs=[vmem] * (2 * len(lefts) + 2) + [hbm] * 3,
+        out_specs=[hbm] * len(lefts) + [vmem] * 2 + [hbm] * 3,
         out_shape=shapes,
         scratch_shapes=[
             pltpu.VMEM((SLOTS, 2, 2, 2, *tile), bf16),
@@ -740,19 +989,18 @@
             pltpu.VMEM((SLOTS, CUT, TILE_COLUMNS), bf16),
             pltpu.VMEM((SLOTS, TILE_ROWS - CUT, TILE_COLUMNS), bf16),
             *[pltpu.VMEM((LINE_SLOTS, *tile), bf16)] * 5,
-            *[pltpu.VMEM((LINE_SLOTS, parts[1].shape[0], LINE_TILE), bf16)] * 5,
             *[pltpu.VMEM((LINE_SLOTS, parts[0].shape[0], LINE_TILE), bf16)] * 5,
             pltpu.VMEM((padded, 128), jnp.float32),
             pltpu.VMEM((5, bias_rows, 128), jnp.float32),
             pltpu.SemaphoreType.DMA((10,)),
             pltpu.SemaphoreType.DMA((10,)),
-            pltpu.SemaphoreType.DMA((14, LINE_SLOTS)),
-            pltpu.SemaphoreType.DMA((14, LINE_SLOTS)),
-            pltpu.SemaphoreType.DMA((3, LINE_SLOTS)),
+            pltpu.SemaphoreType.DMA((11, LINE_SLOTS)),
+            pltpu.SemaphoreType.DMA((11, LINE_SLOTS)),
             pltpu.SemaphoreType.DMA((2, LINE_SLOTS)),
+            pltpu.SemaphoreType.DMA((LINE_SLOTS,)),
             pltpu.SemaphoreType.DMA((3,)),
             pltpu.SemaphoreType.DMA((3,)),
-            pltpu.SemaphoreType.REGULAR((14,)),
+            pltpu.SemaphoreType.REGULAR((11,)),
         ],
         compiler_params=pltpu.CompilerParams(
             collective_id=0, has_side_effects=True, vmem_limit_bytes=56 * 1024 * 1024
@@ -763,20 +1011,13 @@
         name="sum_gradients",
     )(*lefts, *rights, image_part, bias_part, spread, *parts)
     summed = [
-        result.reshape(-1, result.shape[2]).astype(jnp.float32) for result in results[: len(lefts)]
+        result.reshape(-1, result.shape[2])[:, : right.shape[1]].astype(jnp.float32)
+        for result, right in zip(results, rights)
     ]
     every_image, bias_total, given = results[len(lefts) : len(lefts) + 3]
     parts = [part.astype(jnp.float32) for part in results[len(lefts) + 3 :]]
     every_image = every_image[:, :, :, :image_rows].reshape(4, 4, -1).transpose(1, 0, 2)
     return summed, every_image.reshape(16, -1), bias_total.reshape(-1), given, parts
-
-
-def split_heads(operand):
-    return operand.reshape(operand.shape[0], HEADS, HDIM).transpose(1, 0, 2)
-
-
-def join_heads(operand):
-    return operand.transpose(1, 0, 2).reshape(operand.shape[1], HEADS * HDIM)
 
 
 def local(
@@ -840,45 +1081,43 @@
     def image_of(shift):
         return (((row_rank - shift) % n_row) // group) % per
 
-    def bring_start(operand):
+    def bring(operand):
         pieces = []
         for shift in range(n_row):
             piece = lax.dynamic_index_in_dim(operand, image_of(shift), 0, keepdims=False)
             if shift:
                 piece = lax.ppermute(piece, ("img", "row"), route(shift, False))
             pieces.append(piece)
-        return pieces
-
-    def bring_end(pieces):
         packed = matmul(pick, jnp.concatenate(pieces, axis=0)).astype(bf16)
         own = lax.dynamic_slice_in_dim(packed, core * length, length, 0)
         other = lax.dynamic_slice_in_dim(packed, (1 - core) * length, length, 0)
         return jnp.where(receives, own, swap(other, "img", 1))
 
-    def give_start(operand):
-        other = swap(operand, "img", 1)
+    def give_start(operand, other):
         both = jnp.where(
             core == 0,
             jnp.concatenate([operand, other], axis=0),
             jnp.concatenate([other, operand], axis=0),
         )
-        return weight_grad(pick, both).astype(bf16)
-
-    def give_end(spread, given=None):
-        images = [jnp.zeros((slot_len, spread.shape[1]), bf16) for _ in range(per)]
-        for shift in range(n_row):
-            piece = spread[shift * slot_len : (shift + 1) * slot_len]
-            if shift and given is not None:
-                sender = ((row_rank - shift) % n_row) // group
-                piece = jnp.where(sender // per == core, given[shift - 1], jnp.zeros_like(piece))
-            elif shift:
-                piece = lax.ppermute(piece, ("img", "row"), route(shift, True))
-            else:
-                piece = jnp.where(receives, piece, jnp.zeros_like(piece))
-            images = [
-                image + jnp.where(image_of(shift) == at, piece, jnp.zeros_like(piece))
-                for at, image in enumerate(images)
-            ]
+        return weight_grad(pick, both).astype(bf16).reshape(n_row, slot_len, -1)
+
+    def give_send(spread):
+        sent = [
+            lax.ppermute(spread[shift], ("img", "row"), route(shift, True))
+            for shift in range(1, n_row)
+        ]
+        return [spread[0], *sent]
+
+    def give_merge(blocks):
+        images = [jnp.zeros_like(blocks[0]) for _ in range(per)]
+        for shift, block in enumerate(blocks):
+            sender = ((row_rank - shift) % n_row) // group
+            for at in range(per):
+                wanted = (sender // per == core) & (sender % per == at)
+                if group > 1:
+                    images[at] = images[at] + jnp.where(wanted, block, jnp.zeros_like(block))
+                else:
+                    images[at] = jnp.where(wanted, block, images[at])
         return jnp.stack(images)
 
     def fetch(operand):
@@ -940,9 +1179,18 @@
         jnp.zeros((ff_width,), f32), up_bias.astype(f32), (img_rank * up_bias.shape[0],)
     )
     mod_part = matmul(row_cond, ada_weight) + bias_part[None, :]
+    small_plane = n_img == 8 and n_row == 4
+    early = [qkv_weight, out_weight, proj_third]
     summed_rows = jnp.concatenate([mod_part.reshape(-1), up_bias_part])
-    for bit in [1] + chip_bits:
-        summed_rows = summed_rows + swap(summed_rows, "img", bit)
+    if small_plane:
+        early, arrived, summed_rows = gather_weights(
+            early, [tokens, cotangent, targets], summed_rows, group, per
+        )
+    else:
+        early = [fetch(one) for one in early]
+        for bit in [1] + chip_bits:
+            summed_rows = summed_rows + swap(summed_rows, "img", bit)
+    qkv_full, out_full, third_full = early
     modulation = lax.dynamic_index_in_dim(
         summed_rows[: (n_img // 2) * mod_width].reshape(n_img // 2, mod_width),
         img_rank // 2,
@@ -950,13 +1198,6 @@
         keepdims=True,
     )
     up_bias_full = summed_rows[(n_img // 2) * mod_width :]
-    small_plane = n_img == 8 and n_row == 4
-    early = [qkv_weight, out_weight, proj_third]
-    if small_plane:
-        early, modulation = lax.optimization_barrier((early, modulation))
-        qkv_full, out_full, third_full = gather_weights(early)
-    else:
-        qkv_full, out_full, third_full = [fetch(one) for one in early]
     up_full = fetch(up_weight)
     down_full = fetch(down_weight)
     first_full = fetch(proj_first)
@@ -965,32 +1206,34 @@
     shift_att, scale_att, gate_att, shift_mlp, scale_mlp, gate_mlp = jnp.split(
         modulation, 6, axis=1
     )
-    arriving, qkv_full = lax.optimization_barrier((bring_start(tokens), qkv_full))
-    source = bring_end(arriving).astype(f32)
-    later, source = lax.optimization_barrier(
-        (jnp.concatenate([cotangent, targets], axis=2), source)
-    )
-    outside = bring_start(later)
-
-    h_att = modulate(source, shift_att, scale_att).astype(bf16)
+    if small_plane:
+        image_counts = lax.dynamic_index_in_dim(together(counts, 1, 0).reshape(column, n_row), place, 0)
+        ends = jnp.cumsum(image_counts[0])
+        units = core * (length // RW) + jnp.arange(length // RW)
+        origin = jnp.sum((units[:, None] >= ends[None, :]).astype(jnp.int32), axis=1)
+        before = jnp.sum(
+            jnp.where(origin[:, None] == jnp.arange(n_row), ends - image_counts[0], 0), axis=1
+        )
+        places = origin * slot_len + (units - before) * RW
+        source, own_cotangent, own_targets, h_att = compact(
+            places.astype(jnp.int32), arrived, shift_att, scale_att
+        )
+        source = source.astype(f32)
+        own_cotangent, own_targets = own_cotangent.astype(f32), own_targets.astype(f32)
+    else:
+        source = bring(tokens).astype(f32)
+        own_cotangent, own_targets = bring(cotangent).astype(f32), bring(targets).astype(f32)
+        h_att = modulate(source, shift_att, scale_att).astype(bf16)
     qkv_rows = matmul(h_att, qkv_full).astype(bf16)
-    key_value = qkv_rows[:, width:]
-    key_value = jnp.concatenate([key_value, swap(key_value, "img", 1)], axis=0)
+    rest = swap(qkv_rows[:, width:], "img", 1)
     bits = [1 << at for at in range(group.bit_length() - 1)]
     for bit in bits:
-        key_value = jnp.concatenate([key_value, swap(key_value, "row", bit)], axis=0)
-    queries = split_heads(qkv_rows[:, :width])
-    keys = split_heads(key_value[:, :width])
-    values = split_heads(key_value[:, width:])
-    mixed, log_total = attend(queries, keys, values)
-    head_mix = join_heads(mixed)
+        near = jnp.concatenate([qkv_rows[:, width:], rest], axis=0)
+        rest = jnp.concatenate([rest, swap(near, "row", bit)], axis=0)
+    head_mix, log_total = attend(qkv_rows, rest, width)
     attn_out = matmul(head_mix, out_full)
     residual = source + gate_att * attn_out
     h_mlp = modulate(residual, shift_mlp, scale_mlp).astype(bf16)
-    outside, h_mlp = lax.optimization_barrier((outside, h_mlp))
-    outside = bring_end(outside)
-    own_cotangent = outside[:, :width].astype(f32)
-    own_targets = outside[:, width:].astype(f32)
     pre_act = matmul(h_mlp, up_full) + up_bias_full
     gelu_out = gelu_tanh(pre_act).astype(bf16)
     mlp_out = matmul(gelu_out, down_full)
@@ -1001,6 +1244,10 @@
     block_own = (residual + gate_mlp * mlp_out).astype(bf16)
     lin_one = matmul(block_own, first_full)
     hid_one = jax.nn.silu(lin_one).astype(bf16)
+    left_first = turn(block_own) if small_plane else block_own
+    block_spread = give_start(block_own, swap(block_own, "img", 1))
+    tied = lax.optimization_barrier((block_spread, left_first, hid_one))
+    block_spread, left_first, hid_one = tied
     lin_two = matmul(hid_one, second_full)
     hid_two = jax.nn.silu(lin_two).astype(bf16)
     projected = matmul(hid_two, third_full)
@@ -1017,9 +1264,6 @@
     second_sum, d_lin_two = lax.optimization_barrier((second_sum, d_lin_two))
     second_part = scattered(second_sum)
     d_lin_one = silu_back(lin_one, transposed(d_lin_two, second_full)).astype(bf16)
-    first_sum = weight_grad(block_own, d_lin_one).astype(bf16)
-    first_sum, d_lin_one = lax.optimization_barrier((first_sum, d_lin_one))
-    first_part = scattered(first_sum)
     d_res = own_cotangent + transposed(d_lin_one, first_full)
     d_gate_mlp = jnp.sum(d_res * mlp_out, axis=0)
     d_mlp = (d_res * gate_mlp).astype(bf16)
@@ -1033,36 +1277,48 @@
     d_attn = (d_residual * gate_att).astype(bf16)
     d_mixed = transposed(d_attn, out_full).astype(bf16)
     third_part, d_mixed = lax.optimization_barrier((third_part, d_mixed))
-    d_query, d_key, d_value = attend_back(
-        queries, keys, values, mixed, split_heads(d_mixed), log_total
+    d_query, d_own, d_rest, block_given = attend_back(
+        qkv_rows,
+        rest,
+        head_mix,
+        d_mixed,
+        log_total,
+        block_spread,
+        (group, per) if small_plane else None,
     )
-    second_part, d_key = lax.optimization_barrier((second_part, d_key))
-    d_key_value = jnp.concatenate([join_heads(d_key), join_heads(d_value)], axis=1)
-    for axis, bit in [("row", bit) for bit in reversed(bits)] + [("img", 1)]:
-        half = d_key_value.shape[0] // 2
-        arrived = swap(d_key_value[half:], axis, bit)
-        d_key_value = (d_key_value[:half].astype(f32) + arrived.astype(f32)).astype(bf16)
-    d_qkv = jnp.concatenate([join_heads(d_query), d_key_value], axis=1)
+    if small_plane:
+        block_out = give_merge([block_spread[0], *block_given])
+    else:
+        block_out = give_merge(give_send(block_spread))
+    second_part, d_query = lax.optimization_barrier((second_part, d_query))
+    d_own = d_own.astype(f32)
+    for bit in reversed(bits):
+        full = jnp.concatenate([d_own, d_rest.astype(f32)], axis=0)
+        half = full.shape[0] // 2
+        full = full[:half] + swap(full[half:].astype(bf16), "row", bit).astype(f32)
+        d_own, d_rest = full[:length], full[length:].astype(bf16)
+    d_own = d_own + swap(d_rest, "img", 1).astype(f32)
+    d_qkv = jnp.concatenate([d_query, d_own.astype(bf16)], axis=1)
     d_source, d_shift_att, d_scale_att = jax.vjp(modulate, source, shift_att, scale_att)[1](
         transposed(d_qkv, qkv_full)
     )
-    spread = give_start((d_residual + d_source).astype(bf16))
-    block_out = give_end(give_start(block_own))
+    tokens_own = (d_residual + d_source).astype(bf16)
+    spread = give_start(tokens_own, swap(tokens_own, "img", 1))
     own_mod = jnp.concatenate(
         [d_shift_att[0], d_scale_att[0], d_gate_att, d_shift_mlp[0], d_scale_mlp[0], d_gate_mlp]
     )
-    rights = [d_mlp, d_pre, d_attn, d_qkv]
-    proj_parts = [first_part, second_part, third_part]
+    lefts.append(left_first)
+    rights = [d_mlp, d_pre, d_attn, d_qkv, d_lin_one]
+    proj_parts = [second_part, third_part]
     if small_plane:
         tied = (spread, proj_parts, rights, own_mod, bias_sum)
         spread, proj_parts, rights, own_mod, bias_sum = lax.optimization_barrier(tied)
-        blocks = spread.reshape(n_row, slot_len, width)
         large, d_mod, bias_sum, given, proj_grads = sum_gradients(
-            lefts, rights, own_mod, bias_sum, blocks, proj_parts, group, per
-        )
-        grad_tokens = give_end(spread, given)
+            lefts, rights, own_mod, bias_sum, spread, proj_parts, group, per
+        )
+        grad_tokens = give_merge([spread[0], *given])
     else:
-        grad_tokens = give_end(spread)
+        grad_tokens = give_merge(give_send(spread))
         proj_grads = [row_sum(part, at) for at, part in enumerate(proj_parts)]
         large = [over_row(offload_shards(*pair)) for pair in zip(lefts, rights)]
         slot_id = column * (img_rank // 2) + place
@@ -1070,8 +1326,8 @@
         placed = lax.dynamic_update_slice(placed, own_mod[None, :], (slot_id, 0))
         d_mod, bias_sum = lax.psum((placed, bias_sum), ("img", "row"))
         d_mod = d_mod.astype(bf16)
-    grad_first, grad_second, grad_third = proj_grads
-    grad_down, grad_up, grad_out, grad_qkv = large
+    grad_second, grad_third = proj_grads
+    grad_down, grad_up, grad_out, grad_qkv, grad_first = large
 
     grad_ada = weight_grad(silu_cond, d_mod)
     grad_ada_bias = jnp.sum(

time: 827 us -> 689 us (0.83)
  local copies, waits for them, and re-layouts: 117 us -> 42.6 us
  Pallas kernels: 354 us -> 417 us
  starting transfers between devices: 46.3 us -> 6.55 us
  waiting for transfers between devices: 40.8 us -> 5.9 us
  matrix products: 180 us -> 152 us
  other arithmetic: 58.9 us -> 37.3 us
    pallas_call x3 -> x4, Pallas kernels: 152 us -> 209 us  [the longest x1 132 us: gather_weights(): pl.pallas_call(functools.partial(gather_kernel, count, group, per), in_sp...]
    reshape x7 -> x0, local copies, waits for them, and re-layouts: 27 us -> none  [the longest x4 16.6 us: split_heads(): return operand.reshape(operand.shape[0], HEADS, HDIM).transpose(1, 0, 2)]
    ppermute x9 -> x0, waiting for transfers between devices: 25 us -> none  [the longest x3 25 us: give_end(): piece = lax.ppermute(piece, ('img', 'row'), route(shift, True))]
    ppermute x12 -> x8, starting transfers between devices: 26.6 us -> 6.15 us  [swap(): return lax.ppermute(operand, axis, [(at, at ^ bit) for at in range(size)])]
    ppermute x9 -> x0, starting transfers between devices: 19.5 us -> none  [the longest x6 13.5 us: bring_start(): piece = lax.ppermute(piece, ('img', 'row'), route(shift, False))]
    transpose x4 -> x0, local copies, waits for them, and re-layouts: 18.2 us -> none  [join_heads(): return operand.transpose(1, 0, 2).reshape(operand.shape[1], HEADS * HDIM)]
    dot_general x10 -> x8, matrix products: 77.3 us -> 59.8 us  [matmul(): return jnp.dot(left_side, right_side, preferred_element_type=jnp.float32)]
    slice x7 -> x1, local copies, waits for them, and re-layouts: 15.8 us -> 1.66 us  [local(): rest = swap(qkv_rows[:, width:], 'img', 1)]
  transfers between devices with their start and end apart: 28 -> 14, of which waited for: 8 -> 4; matrix products, arithmetic and copies ran while one was open for 34% -> 23% of each run, Pallas kernels for 19% -> 31%
where the time goes in v3:
time: 689 us; the launch traced here: 679 us
  Pallas kernels  417 us (61%)
  matrix products  152 us (22%)
  local copies, waits for them, and re-layouts  42.6 us (6%)
  other arithmetic  37.3 us (5%)
  between operations  18.1 us (3%)
    pallas_call x1, Pallas kernels, sum_gradients(): pl.pallas_call(functools.partial(sum_kernel, len(lefts), group, per), in_...  208 us
    pallas_call x1, Pallas kernels, gather_weights(): pl.pallas_call(functools.partial(gather_kernel, count, group, per), in_sp...  132 us
    dot_general x8, matrix products, transposed(): lax.dot_general(left_side, right_side, LAST, preferred_element_type=jnp.f...  62.8 us
    dot_general x8, matrix products, matmul(): return jnp.dot(left_side, right_side, preferred_element_type=jnp.float32)  59.8 us
    pallas_call x1, Pallas kernels, attend_back(): pl.pallas_call(functools.partial(attend_back_kernel, give), in_specs=[vme...  44.8 us
    dot_general x5, matrix products, weight_grad(): lax.dot_general(left_side, right_side, FIRST, preferred_element_type=jnp....  27.3 us
    pallas_call x1, Pallas kernels, attend(): pl.pallas_call(attend_kernel, in_specs=[vmem] * 2, out_specs=[vmem] * 2,...  26 us
    unnamed x143, local copies, waits for them, and re-layouts  19.9 us
  transfers between devices with their start and end apart: 14, of which 4 were waited for; matrix products, arithmetic and copies ran while one was open for 23% of the time, Pallas kernels for 31%

profile of v3, /device:TPU:0, one launch (start us, length us, event | category | flops | bytes accessed | tf_op | source)
XLA Modules:
  0.0 679.3 jit_solution(14802482840713556265)
XLA Ops:
  11.1 2.8 collective-permute-start.2
  15.6 2.1 collective-permute-start.3
  22.0 131.6 %gather_weights.1 = (bf16[8,144,3456]{2,1,0:T(8,128)(2,1)}, bf16[8,144,1152]{2,1,0:T(8,128)(2,1)}, bf16[8,256,768]{2,1,0:T(8,128)(2,1)}, bf16[4,384,1152]{2,1,0:...) custom-call(bf16[144,3456]{1,0:T(8,128)(2,1)} %refs_0_.1, ...), custom_call_target="tpu_custom_call" | custom-call | bytes 200000000 | tf_op jit(solution)/shard_map/gather_weights/pallas_call | solution.py:486
  155.3 2.1 copy-done.3
  161.2 6.6 compact.1
  167.9 5.1 convolution_convert_fusion.3.own_ref
  185.3 2.4 copy.48
  189.7 26.0 %attend.1 = (bf16[512,1152]{1,0:T(8,128)(2,1)}, f32[16,1,512]{2,1,0:T(1,128)}) custom-call(bf16[512,3456]{1,0:T(8,128)(2,1)} %copy-done.22, bf16[512,2304]{1,0:T(8,128)(2,1)} %collective-permute-done.4.rest_ref), custom_call_target="tpu_custom_call" | custom-call | flops 8589934592 | bytes 14155776 | tf_op jit(solution)/shard_map/attend/pallas_call | solution.py:117
  215.7 5.3 fusion.84
  224.3 2.4 copy.47
  226.7 14.7 %fusion.14 = (bf16[4608,512]{0,1:T(8,128)(2,1)}, f32[512,4608]{1,0:T(8,128)}) fusion(f32[4608]{0:T(1024)S(1)} %slice_bitcast_fusion, bf16[1152,4608]{1,0:T(8,128)(2,1)} %all-gather.5.cloned.1.call-done, f32[512,1152]{1,0:T(8,128)} %copy-done.11, f32[1152]{0:T(1024)S(1)} %get-tuple-element.132, f32[1152]{0:T(1024)S(1)} %get-tuple-element.130, ...), kind=kOutput, calls=%fused_computation.17 | convolution fusion | flops 5462360064 | bytes 27163648 | tf_op jit(solution)/shard_map/dot_general | solution.py:39
  241.4 6.7 copy.45
  248.1 13.5 %fusion.15 = f32[512,1152]{1,0:T(8,128)S(1)} fusion(bf16[4608,1152]{1,0:T(8,128)(2,1)} %all-gather.7.cloned.1.call-done, f32[512,4608]{1,0:T(8,128)} %get-tuple-element.168, f32[4608]{0:T(1024)S(1)} %slice_bitcast_fusion), kind=kOutput, calls=%fused_computation.29 | convolution fusion | flops 5459410944 | bytes 22431744 | tf_op jit(solution)/shard_map/dot_general | solution.py:39
  264.9 7.9 %multiply_convert_fusion.3 = (bf16[512,2048]{1,0:T(8,128)(2,1)}, f32[512,2048]{1,0:T(8,128)}) fusion(bf16[512,1152]{1,0:T(8,128)(2,1)S(1)} %add_convert_fusion.2, bf16[1152,2048]{1,0:T(8,128)(2,1)} %all-gather.9.cloned.1.call-done), kind=kOutput, calls=%fused_computation.38 | convolution fusion | flops 2421161984 | bytes 12189696 | tf_op jit(solution)/shard_map/dot_general | solution.py:39
  272.9 8.0 %convolution_convert_fusion.2 = bf16[1536,1152]{1,0:T(8,128)(2,1)} fusion(bf16[512,1152]{1,0:T(8,128)(2,1)} %collective-permute-done.5, bf16[512,1152]{1,0:T(8,128)(2,1)S(1)} %add_convert_fusion.2, pred[]{:T(512)S(6)} %eq.199, pred[1024,384]{1,0:T(32,128)(4,1)S(1)} %copy-done.34, pred[1024,384]{1,0:T(32,128)(4,1)S(1)} %copy-done.32, ...), kind=kOutput, calls=%fused_computation.23 | convolution fusion | flops 3640983552 | bytes 7471105 | tf_op jit(solution)/shard_map/dot_general | solution.py:47
  280.9 11.0 %multiply_convert_fusion.2 = (bf16[512,2048]{1,0:T(8,128)(2,1)S(1)}, f32[512,2048]{1,0:T(8,128)}) fusion(bf16[512,2048]{1,0:T(8,128)(2,1)} %get-tuple-element.76, bf16[2048,2048]{1,0:T(8,128)(2,1)} %all-gather.11.cloned.1.call-done), kind=kOutput, calls=%fused_computation.36 | convolution fusion | flops 4300210176 | bytes 16777216 | tf_op jit(solution)/shard_map/dot_general | solution.py:39
  295.2 3.5 convolution_convert_fusion.4
  299.9 6.0 fusion.18
  307.2 6.9 %convolution_convert_fusion.1 = bf16[2048,2048]{1,0:T(8,128)(2,1)} fusion(bf16[512,2048]{1,0:T(8,128)(2,1)S(1)} %copy-done.64, bf16[512,2048]{1,0:T(8,128)(2,1)S(1)} %fusion.18), kind=kOutput, calls=%fused_computation.22 | convolution fusion | flops 4299161600 | bytes 12582912 | tf_op jit(solution)/shard_map/dot_general | solution.py:47
  314.2 10.8 %fusion.21.refs_9_ = bf16[512,2048]{1,0:T(8,128)(2,1)S(1)} fusion(f32[512,2048]{1,0:T(8,128)} %get-tuple-element.170, bf16[512,2048]{1,0:T(8,128)(2,1)} %copy-done.65, bf16[2048,2048]{1,0:T(8,128)(2,1)} %all-gather.11.cloned.1.call-done), kind=kOutput, calls=%fused_computation.35 | convolution fusion | flops 4305453056 | bytes 16777216 | tf_op jit(solution)/shard_map/dot_general | solution.py:43
  325.0 4.0 multiply_convert_fusion.5
  329.0 16.6 %convert_reduce_fusion = (f32[4608]{0:T(1024)}, bf16[512,4608]{1,0:T(8,128)(2,1)S(1)}) fusion(f32[512,4608]{1,0:T(8,128)} %get-tuple-element.168, f32[4608]{0:T(1024)S(1)} %slice_bitcast_fusion, bf16[512,1152]{1,0:T(8,128)(2,1)} %get-tuple-element.99.refs_5_, bf16[4608,1152]{1,0:T(8,128)(2,1)} %all-gather.7.cloned.1.call-done), kind=kOutput, calls=%fused_computation.18 | convolution fusion | flops 5490077184 | bytes 25989120 | tf_op jit(solution)/shard_map/dot_general | solution.py:43
  345.6 12.4 %multiply_reduce_fusion.1 = (f32[1152]{0:T(1024)S(1)}, f32[512]{0:T(512)S(1)}, f32[1152]{0:T(1024)S(1)}, f32[512,1152]{1,0:T(8,128)S(1)}) fusion(f32[512,1152]{1,0:T(8,128)S(1)} %copy-done.13, f32[512]{0:T(512)S(1)} %fusion.66, f32[512]{0:T(512)S(1)} %broadcast_multiply_fusion.1, f32[1152]{0:T(1024)S(1)} %get-tuple-element.130, ...), kind=kOutput, calls=%fused_computation.71 | convolution fusion | flops 5440534016 | bytes 20073984 | tf_op jit(solution)/shard_map/dot_general | solution.py:43
  365.1 2.9 convolution_convert_fusion.5.d_ref
  368.0 44.8 %attend_back.1 = (bf16[512,1152]{1,0:T(8,128)(2,1)}, bf16[512,2304]{1,0:T(8,128)(2,1)}, bf16[512,2304]{1,0:T(8,128)(2,1)}, bf16[3,384,1152]{2,1,0:T(8,128)(2,1)}) custom-call(bf16[512,3456]{1,0:T(8,128)(2,1)} %copy-done.22, bf16[512,2304]{1,0:T(8,128)(2,1)} %collective-permute-done.4.rest_ref, bf16[512,1152]{1,0:T(8,128)(2,1)} %get-tuple-element.72.mix_ref, ...), custom_call_target="tpu_custom_call" | custom-call | flops 21474836480 | bytes 28311552 | tf_op jit(solution)/shard_map/attend_back/pallas_call | solution.py:244
  413.2 2.3 select_select_fusion.3
  417.8 4.0 add_convert_fusion
  421.8 9.6 %fusion.26 = (f32[512]{0:T(512)S(1)}, f32[512]{0:T(512)S(1)}, f32[512,1152]{1,0:T(8,128)S(1)}) fusion(bf16[512,1152]{1,0:T(8,128)(2,1)S(1)} %copy-done.2, f32[512]{0:T(512)S(1)} %broadcast_multiply_fusion, f32[1152]{0:T(1024)S(1)} %copy-done.42, bf16[1152,3456]{1,0:T(8,128)(2,1)} %bitcast.142, bf16[512,2304]{1,0:T(8,128)(2,1)} %add_convert_fusion, ...), kind=kOutput, calls=%fused_computation.54 | convolution fusion | flops 4088069120 | bytes 15051264 | tf_op jit(solution)/shard_map/dot_general | solution.py:43
  435.1 2.0 pad_maximum_fusion.refs_8_
  437.2 6.2 convolution_convert_fusion
  444.0 208.2 %sum_gradients.1 = (bf16[4,144,1152]{2,1,0:T(8,128)(2,1)}, bf16[1,144,4608]{2,1,0:T(8,128)(2,1)}, bf16[1,144,1152]{2,1,0:T(8,128)(2,1)}, bf16[1,144,3456]{2,1,0:...) custom-call(bf16[8,4,144,512]{3,2,1,0:T(8,128)(2,1)} %bitcast.114, ...), custom_call_target="tpu_custom_call" | custom-call | flops 18723373056 | bytes 600000000 | tf_op jit(solution)/shard_map/sum_gradients/pallas_call | solution.py:978
  654.1 2.7 fusion.88
  (272 shorter events, 70.4 us)
Async XLA Ops:
  7.2 13.7 %copy-start = (bf16[144,6912]{1,0:T(8,128)(2,1)S(1)}, bf16[144,6912]{1,0:T(8,128)(2,1)}, u32[]{:S(2)}) copy-start(bf16[144,6912]{1,0:T(8,128)(2,1)} %param.21) | copy-start | bytes 5971972
  7.2 12.1 %copy-start.62 = (s32[16]{0:T(128)S(1)}, s32[16]{0:T(128)}, u32[]{:S(2)}) copy-start(s32[16]{0:T(128)} %param.31) | copy-start | bytes 196
  7.2 12.3 %copy-start.61 = (bf16[64,144]{1,0:T(8,128)(2,1)S(1)}, bf16[64,144]{1,0:T(8,128)(2,1)}, u32[]{:S(2)}) copy-start(bf16[64,144]{1,0:T(8,128)(2,1)} %param.20) | copy-start | bytes 55300
  7.3 219.5 %all-gather.5.cloned.1.call-start = ((), (), s32[]{:S(2)}) async-start(), calls=%async_computation.2 | async-start | bytes 11943936 | tf_op jit(solution)/shard_map/all_gather | solution.py:1124
  8.0 240.1 %all-gather.7.cloned.1.call-start = ((), (), s32[]{:S(2)}) async-start(), calls=%async_computation.3 | async-start | bytes 11943936 | tf_op jit(solution)/shard_map/all_gather | solution.py:1124
  8.7 256.2 %all-gather.9.cloned.1.call-start = ((), (), s32[]{:S(2)}) async-start(), calls=%async_computation.4 | async-start | bytes 5308416 | tf_op jit(solution)/shard_map/all_gather | solution.py:1124
  9.5 271.4 %all-gather.11.cloned.1.call-start = ((), (), s32[]{:S(2)}) async-start(), calls=%async_computation.5 | async-start | bytes 9437184 | tf_op jit(solution)/shard_map/all_gather | solution.py:1124
  9.5 1.3 collective-permute-start.1
  10.1 7.6 %collective-permute-start = (s32[2,4]{1,0:T(2,128)S(1)}, s32[2,4]{1,0:T(2,128)S(1)}, u32[]{:S(2)}, u32[]{:S(2)}) collective-permute-start(s32[2,4]{1,0:T(2,128)S(1)} %copy-done.50), channel_id=1, source_target_pairs={{0,4},{4,0},{8,12},{12,8},{16,20},{20,16},{24,28},{28,24},{1,5},{5... | collective-permute-start | bytes 104 | tf_op jit(solution)/shard_map/ppermute | solution.py:1057
  10.2 357.8 %reduce-scatter.3.cloned.1.call-start = ((), (), s32[]{:S(2)}) async-start(), calls=%async_computation.6 | async-start | bytes 3538944 | tf_op jit(solution)/shard_map/reduce_scatter | solution.py:1137
  11.1 4.3 collective-permute-start.2
  15.6 3.6 collective-permute-start.3
  155.3 60.4 %copy-start.43 = (f32[1152]{0:T(1024)}, f32[1152]{0:T(1024)S(1)}, u32[]{:S(2)}) copy-start(f32[1152]{0:T(1024)S(1)} %get-tuple-element.131) | copy-start | bytes 13828
  167.8 47.9 %copy-start.1 = (bf16[512,1152]{1,0:T(8,128)(2,1)}, bf16[512,1152]{1,0:T(8,128)(2,1)S(1)}, u32[]{:S(2)}) copy-start(bf16[512,1152]{1,0:T(8,128)(2,1)S(1)} %get-tuple-element.73) | copy-start | bytes 3538948
  175.6 14.2 %collective-permute-start.4 = (bf16[512,2304]{1,0:T(8,128)(2,1)}, bf16[512,2304]{1,0:T(8,128)(2,1)}, u32[]{:S(2)}, u32[]{:S(2)}) collective-permute-start(bf16[512,2304]{1,0:T(8,128)(2,1)} %slice.30), channel_id=1, source_target_pairs={{0,4},{4,0},{8,12},{12,8},{16,20},{20,16},{24,28},{28,24},{1,5},{5... | collective-permute-start | bytes 7077896 | tf_op jit(solution)/shard_map/ppermute | solution.py:1057
  189.7 26.0 %copy-start.59 = (bf16[8,144,1152]{2,1,0:T(8,128)(2,1)S(1)}, bf16[8,144,1152]{2,1,0:T(8,128)(2,1)}, u32[]{:S(2)}) copy-start(bf16[8,144,1152]{2,1,0:T(8,128)(2,1)} %get-tuple-element.74) | copy-start | bytes 7962628
  248.1 13.6 %copy-start.12 = (f32[512,1152]{1,0:T(8,128)S(1)}, f32[512,1152]{1,0:T(8,128)}, u32[]{:S(2)}) copy-start(f32[512,1152]{1,0:T(8,128)} %copy-done.11) | copy-start | bytes 7077892
  263.0 9.8 %collective-permute-start.5 = (bf16[512,1152]{1,0:T(8,128)(2,1)S(1)}, bf16[512,1152]{1,0:T(8,128)(2,1)}, u32[]{:S(2)}, u32[]{:S(2)}) collective-permute-start(bf16[512,1152]{1,0:T(8,128)(2,1)S(1)} %add_convert_fusion.2), channel_id=1, source_target_pairs={{0,4},{4,0},{8,12},{12,8},{16,20},{20,16},{24,28},{28,24},{1,5},{5... | collective-permute-start | bytes 3538952 | tf_op jit(solution)/shard_map/ppermute | solution.py:1057
  264.9 7.9 %copy-start.36 = (pred[1024,384]{1,0:T(32,128)(4,1)S(1)}, pred[1024,384]{1,0:T(32,128)(4,1)}, u32[]{:S(2)}) copy-start(pred[1024,384]{1,0:T(32,128)(4,1)} %get-tuple-element.178) | copy-start | bytes 1179652
  264.9 7.9 %copy-start.38 = (pred[1024,384]{1,0:T(32,128)(4,1)S(1)}, pred[1024,384]{1,0:T(32,128)(4,1)}, u32[]{:S(2)}) copy-start(pred[1024,384]{1,0:T(32,128)(4,1)} %get-tuple-element.179) | copy-start | bytes 1179652
  280.9 11.0 %copy-start.6 = (bf16[512,768]{1,0:T(8,128)(2,1)S(1)}, bf16[512,768]{1,0:T(8,128)(2,1)}, u32[]{:S(2)}) copy-start(bf16[512,768]{1,0:T(8,128)(2,1)} %copy-done.5) | copy-start | bytes 2359300
  280.9 11.0 %copy-start.58 = (bf16[8,256,768]{2,1,0:T(8,128)(2,1)S(1)}, bf16[8,256,768]{2,1,0:T(8,128)(2,1)}, u32[]{:S(2)}) copy-start(bf16[8,256,768]{2,1,0:T(8,128)(2,1)} %get-tuple-element.78) | copy-start | bytes 9437188
  298.7 123.0 %reduce-scatter.5.cloned.1.call-start = ((), (), s32[]{:S(2)}) async-start(), calls=%async_computation.7 | async-start | bytes 9437184 | tf_op jit(solution)/shard_map/reduce_scatter | solution.py:1137
  314.1 10.8 %slice-start = ((s8[4718592]{0:T(1024)(128)(4,1)}), s8[524288]{0:T(1024)(128)(4,1)S(1)}, s32[]{:S(2)}) async-start(s8[4718592]{0:T(1024)(128)(4,1)} %bitcast.144), calls=%async_computation.8 | async-start | bytes 1048576
  314.1 10.8 %copy-start.10 = (bf16[512,1152]{1,0:T(8,128)(2,1)S(1)}, bf16[512,1152]{1,0:T(8,128)(2,1)}, u32[]{:S(2)}) copy-start(bf16[512,1152]{1,0:T(8,128)(2,1)} %copy-done.9) | copy-start | bytes 3538948
  314.2 10.8 %slice-start.1 = ((s8[4718592]{0:T(1024)(128)(4,1)}), s8[4194304]{0:T(1024)(128)(4,1)S(1)}, s32[]{:S(2)}) async-start(s8[4718592]{0:T(1024)(128)(4,1)} %bitcast.144), calls=%async_computation.9 | async-start | bytes 8388608
  329.0 16.7 %copy-start.13 = (f32[512,1152]{1,0:T(8,128)S(1)}, f32[512,1152]{1,0:T(8,128)}, u32[]{:S(2)}) copy-start(f32[512,1152]{1,0:T(8,128)} %copy-done.11) | copy-start | bytes 7077892
  345.6 12.4 %copy-start.66 = (bf16[512,4608]{1,0:T(8,128)(2,1)}, bf16[512,4608]{1,0:T(8,128)(2,1)S(1)}, u32[]{:S(2)}) copy-start(bf16[512,4608]{1,0:T(8,128)(2,1)S(1)} %get-tuple-element.100.refs_6_) | copy-start | bytes 14155780
  345.6 12.4 %copy-start.48 = (f32[512]{0:T(512)S(1)}, f32[512]{0:T(512)}, u32[]{:S(2)}) copy-start(f32[512]{0:T(512)} %copy-done.47) | copy-start | bytes 6148
  368.0 45.1 %copy-start.53 = (f32[512]{0:T(512)S(1)}, f32[512]{0:T(512)}, u32[]{:S(2)}) copy-start(f32[512]{0:T(512)} %get-tuple-element.148) | copy-start | bytes 6148
  412.8 4.9 collective-permute-start.6
  433.9 3.2 collective-permute-start.7
  (51 other events, 144.7 us)
Sparse Core Ops, SparseCore 0:
  10.0 106.5 all-gather.4
  118.4 64.0 all-gather.6
  184.4 38.8 all-gather.8
  225.1 54.3 all-gather.10
  298.9 44.8 reduce-scatter.2
  347.5 71.2 reduce-scatter.4

commit v4 on v3

--- a/solution.py
+++ b/solution.py
@@ -60,30 +60,43 @@
 
 
 MESH = pl.DeviceIdType.MESH
-WINDOW = 256
-
-
-def head_window(head, width):
-    first = jnp.minimum(head * HDIM // 128, (width - WINDOW) // 128) * 128
-    lane = lax.broadcasted_iota(jnp.int32, (1, WINDOW), 1) + first - head * HDIM
+HALF = HEADS // 2
+
+
+def head_window(head, width, window):
+    first = jnp.minimum(head * HDIM // 128, (width - window) // 128) * 128
+    lane = lax.broadcasted_iota(jnp.int32, (1, window), 1) + first - head * HDIM
     return first, (lane >= 0) & (lane < HDIM)
 
 
-def columns_at(first, part, width):
-    return pl.ds(pl.multiple_of(first + part * width, 128), WINDOW)
+def each_head(body):
+    def narrow(at, carry):
+        body(2 * at + at // (HALF // 2), 128)
+        return carry
+
+    def wide(at, carry):
+        body(2 * at + 1 - at // (HALF // 2), 256)
+        return carry
+
+    lax.fori_loop(0, HALF, narrow, 0)
+    lax.fori_loop(0, HALF, wide, 0)
+
+
+def columns_at(first, part, width, window):
+    return pl.ds(pl.multiple_of(first + part * width, 128), window)
 
 
 def attend_kernel(own_ref, rest_ref, mix_ref, lse_ref):
     length, width = mix_ref.shape
     block = min(256, length)
 
-    def one_head(head, carry):
-        first, mine = head_window(head, width)
-        mix_columns = columns_at(first, 0, width)
-        key_refs = [own_ref.at[:, columns_at(first, 1, width)]]
-        key_refs.append(rest_ref.at[:, columns_at(first, 0, width)])
-        value_refs = [own_ref.at[:, columns_at(first, 2, width)]]
-        value_refs.append(rest_ref.at[:, columns_at(first, 1, width)])
+    def one_head(head, window):
+        first, mine = head_window(head, width, window)
+        mix_columns = columns_at(first, 0, width, window)
+        key_refs = [own_ref.at[:, columns_at(first, 1, width, window)]]
+        key_refs.append(rest_ref.at[:, columns_at(first, 0, width, window)])
+        value_refs = [own_ref.at[:, columns_at(first, 2, width, window)]]
+        value_refs.append(rest_ref.at[:, columns_at(first, 1, width, window)])
         keys, values = [ref[...] for ref in key_refs], [ref[...] for ref in value_refs]
         for at in range(0, length, block):
             rows = pl.ds(at, block)
@@ -105,10 +118,9 @@
             mix_ref[rows, mix_columns] = jnp.where(mine, mixed, mix_ref[rows, mix_columns])
             log_total = jnp.broadcast_to(top + jnp.log(total) * LOG2E, (block, 128))
             lse_ref[head, :, rows] = log_total.T[:1, :]
-        return carry
 
     mix_ref[...] = jnp.zeros_like(mix_ref)
-    lax.fori_loop(0, HEADS, one_head, 0)
+    each_head(one_head)
 
 
 def attend(own, rest, width):
@@ -122,7 +134,7 @@
             jax.ShapeDtypeStruct((length, width), bf16),
             jax.ShapeDtypeStruct((HEADS, 1, length), jnp.float32),
         ],
-        compiler_params=pltpu.CompilerParams(vmem_limit_bytes=56 * 1024 * 1024),
+        compiler_params=pltpu.CompilerParams(vmem_limit_bytes=60 * 1024 * 1024),
         cost_estimate=pl.CostEstimate(
             flops=4 * HEADS * length * span * 256,
             bytes_accessed=4 * (length + span) * width * 2,
@@ -168,6 +180,22 @@
                 rows = pl.ds(pl.multiple_of(at * amount, amount), amount)
                 self.copy(shift, rows).start()
 
+    def trickle(self, at, amount):
+        block = at // 2
+
+        @pl.when((block < self.slots // amount) & self.from_here(self.row))
+        def _():
+            rows = pl.ds(pl.multiple_of(block * amount, amount), amount)
+
+            @pl.when(lax.rem(at, 2) == 0)
+            def _():
+                self.copy(1, rows).start()
+                self.copy(3, rows).start()
+
+            @pl.when(lax.rem(at, 2) == 1)
+            def _():
+                self.copy(2, rows).start()
+
     def wait(self):
         for shift in range(1, 4):
             whole = self.copy(shift, pl.ds(0, self.slots))
@@ -181,40 +209,45 @@
                 whole.wait_recv()
 
 
-def attend_back_kernel(
-    give, own_ref, rest_ref, mix_ref, d_ref, lse_ref, spread, dq_ref, own_out, rest_out, given, *sems
-):
+def attend_back_kernel(give, own_ref, rest_ref, mix_ref, d_ref, lse_ref, spread, *refs):
     length, width = mix_ref.shape
     block = 256
     if give:
+        d_own, given, d_rest, arrived, core_send, core_recv, *sems = refs
+        me = lax.axis_index("img")
+        sibling = {"img": me + 1 - 2 * lax.rem(me, 2)}
         sender = Give(*give, spread, given, *sems)
         sender.greet()
-        pl.semaphore_wait(pltpu.get_barrier_semaphore(), 3)
+        greet(sibling)
+        pl.semaphore_wait(pltpu.get_barrier_semaphore(), 4)
         sender.start(0, given.shape[1])
-    for ref in (dq_ref, own_out, rest_out):
+    else:
+        d_own, d_rest = refs
+    for ref in (d_own, d_rest):
         ref[...] = jnp.zeros_like(ref)
 
-    def one_head(head, carry):
-        first, mine = head_window(head, width)
-        here, next_part = columns_at(first, 0, width), columns_at(first, 1, width)
+    def one_head(head, window):
+        first, mine = head_window(head, width, window)
+        here = columns_at(first, 0, width, window)
         queries = jnp.where(mine, own_ref[:, here], jnp.bfloat16(0))
         d_mix = jnp.where(mine, d_ref[:, here], jnp.bfloat16(0))
         product = d_mix.astype(jnp.float32) * mix_ref[:, here].astype(jnp.float32)
         delta = lax.dot_general(
-            jnp.ones((8, WINDOW), jnp.float32),
+            jnp.ones((8, window), jnp.float32),
             product,
             LAST,
             precision=lax.Precision.HIGHEST,
             preferred_element_type=jnp.float32,
         )[:1, :]
         log_total = lse_ref[head]
-        d_query = jnp.zeros((length, WINDOW), jnp.float32)
-        runs = [(own_ref, 1, own_out, at) for at in range(0, length, block)]
-        runs += [(rest_ref, 0, rest_out, at) for at in range(0, rest_ref.shape[0], block)]
+        d_query = jnp.zeros((length, window), jnp.float32)
+        runs = [(own_ref, 1, d_own, at) for at in range(0, length, block)]
+        runs += [(rest_ref, 0, d_rest, at) for at in range(0, rest_ref.shape[0], block)]
         for source, part, target, at in runs:
             rows = pl.ds(at, block)
-            keys = source[rows, columns_at(first, part, width)]
-            values = source[rows, columns_at(first, part + 1, width)]
+            key_columns = columns_at(first, part, width, window)
+            value_columns = columns_at(first, part + 1, width, window)
+            keys, values = source[rows, key_columns], source[rows, value_columns]
             scores = lax.dot_general(keys, queries, LAST, preferred_element_type=jnp.float32)
             prob = jnp.exp2(scores * (SCALE * LOG2E) - log_total)
             d_prob = lax.dot_general(values, d_mix, LAST, preferred_element_type=jnp.float32)
@@ -223,15 +256,25 @@
             d_value = jnp.dot(
                 prob.astype(jnp.bfloat16), d_mix, preferred_element_type=jnp.float32
             )
-            target[rows, here] += d_key.astype(target.dtype)
-            target[rows, next_part] += d_value.astype(target.dtype)
+            target[rows, key_columns] += d_key.astype(target.dtype)
+            target[rows, value_columns] += d_value.astype(target.dtype)
             d_query += lax.dot_general(d_score, keys, FIRST, preferred_element_type=jnp.float32)
         d_query = jnp.where(mine, d_query * SCALE, 0.0)
-        dq_ref[:, here] += d_query.astype(dq_ref.dtype)
-        return carry
-
-    lax.fori_loop(0, HEADS, one_head, 0)
+        d_own[:, here] += d_query.astype(d_own.dtype)
+
+    each_head(one_head)
     if give:
+        swap = pltpu.make_async_remote_copy(
+            src_ref=d_rest,
+            dst_ref=arrived,
+            send_sem=core_send,
+            recv_sem=core_recv,
+            device_id=sibling,
+            device_id_type=MESH,
+        )
+        swap.start()
+        swap.wait()
+        d_own[:, pl.ds(width, 2 * width)] += arrived[...]
         sender.wait()
 
 
@@ -240,19 +283,23 @@
     span = length + rest.shape[0]
     vmem, bf16 = pl.BlockSpec(memory_space=pltpu.VMEM), jnp.bfloat16
     hbm = pl.BlockSpec(memory_space=pl.ANY)
-    remote = dict(collective_id=2, has_side_effects=True) if give else {}
+    shapes = [jax.ShapeDtypeStruct(own.shape, bf16)]
+    specs, scratch, remote = [vmem, vmem], [], {}
+    if give:
+        shapes.append(jax.ShapeDtypeStruct((spread.shape[0] - 1, *spread.shape[1:]), bf16))
+        specs = [vmem, hbm]
+        scratch = [pltpu.VMEM(rest.shape, bf16)] * 2
+        scratch += [pltpu.SemaphoreType.DMA] * 2 + [pltpu.SemaphoreType.DMA((3,))] * 2
+        remote = dict(collective_id=2, has_side_effects=True)
+    else:
+        shapes.append(jax.ShapeDtypeStruct(rest.shape, bf16))
     return pl.pallas_call(
         functools.partial(attend_back_kernel, give),
         in_specs=[vmem] * 5 + [hbm],
-        out_specs=[vmem] * 3 + [hbm],
-        out_shape=[
-            jax.ShapeDtypeStruct((length, width), bf16),
-            jax.ShapeDtypeStruct((length, 2 * width), bf16),
-            jax.ShapeDtypeStruct((span - length, 2 * width), bf16),
-            jax.ShapeDtypeStruct((spread.shape[0] - 1, *spread.shape[1:]), bf16),
-        ],
-        scratch_shapes=[pltpu.SemaphoreType.DMA((3,))] * 2 if give else [],
-        compiler_params=pltpu.CompilerParams(vmem_limit_bytes=56 * 1024 * 1024, **remote),
+        out_specs=specs,
+        out_shape=shapes,
+        scratch_shapes=scratch,
+        compiler_params=pltpu.CompilerParams(vmem_limit_bytes=60 * 1024 * 1024, **remote),
         cost_estimate=pl.CostEstimate(
             flops=10 * HEADS * length * span * 256,
             bytes_accessed=8 * (length + span) * width * 2,
@@ -264,12 +311,14 @@
 
 TILE_ROWS = 144
 TILE_COLUMNS = 384
-CUT = 80
+CUTS = (80, 64)
 SLOTS = 4
-LINE_SLOTS = 8
+LINE_SLOTS = 10
+LAST_LAG = 15
 LINE_TILE = 256
-SIDE_PACE = 4
+AT_ONCE = 2
 GIVE_ROWS = 16
+TOKEN_ROWS = 128
 
 
 def add(one, other):
@@ -293,7 +342,7 @@
     part_in, part_sum, send_sem, recv_sem, local_sem, slot_send, slot_recv, slot_local = [
         next(take) for _ in range(8)
     ]
-    part_send, part_recv = take
+    part_send, part_recv, *staged = take
     row = lax.axis_index("row")
     me, (core, x, y), (sibling, x_mate, y_mate) = mates()
     far = x_mate + 4 - 8 * y
@@ -319,9 +368,12 @@
             device_id_type=MESH,
         )
 
-    def own_slots(which):
+    def own_slots(which, leaving):
         source = slots[which].at[place_of(row)[1]]
-        return pltpu.make_async_copy(source, arrivals[which].at[row], slot_local.at[which])
+        stage = staged[count + which]
+        if leaving:
+            return pltpu.make_async_copy(stage, arrivals[which].at[row], slot_local.at[which])
+        return pltpu.make_async_copy(source, stage, slot_local.at[which])
 
     def by_core(which, shift):
         origin = lax.rem(row + shift, 4)
@@ -344,8 +396,14 @@
 
         @pl.when(takes_in)
         def _():
-            own_slots(which).start()
+            own_slots(which, False).start()
             by_core(which, 0).start()
+
+    def stage_slots(which):
+        @pl.when(takes_in)
+        def _():
+            own_slots(which, False).wait()
+            own_slots(which, True).start()
 
     def pass_slots(which):
         for shift in range(1, 4):
@@ -364,7 +422,7 @@
 
         @pl.when(takes_in)
         def _():
-            own_slots(which).wait()
+            own_slots(which, True).wait()
             for shift in range(4):
                 by_core(which, shift).wait_send()
 
@@ -437,7 +495,10 @@
 
     every = [copies(at) for at in range(count)]
     locals_ = [
-        pltpu.make_async_copy(blocks[at], wholes[at].at[me], local_sem.at[at])
+        pltpu.make_async_copy(blocks[at], staged[at], local_sem.at[at]) for at in range(count)
+    ]
+    moved = [
+        pltpu.make_async_copy(staged[at], wholes[at].at[me], local_sem.at[at])
         for at in range(count)
     ]
     part_hop(0).start()
@@ -460,6 +521,11 @@
         found[3].start()
         found[9].start()
     take_part(1)
+    for at in range(count):
+        locals_[at].wait()
+        moved[at].start()
+    for which in range(3):
+        stage_slots(which)
     pass_slots(0)
     for at in range(count):
         found = every[at]
@@ -474,7 +540,7 @@
             if kind >= 6:
                 one.wait_recv()
             one.wait_send()
-        locals_[at].wait()
+        moved[at].wait()
     for which in range(3):
         end_slots(which)
 
@@ -503,8 +569,12 @@
             pltpu.SemaphoreType.DMA((3,)),
             pltpu.SemaphoreType.DMA((3,)),
             pltpu.SemaphoreType.DMA((3,)),
+            *[pltpu.VMEM(block.shape, block.dtype) for block in blocks],
+            *[pltpu.VMEM(one.shape[1:], one.dtype) for one in slots],
         ],
-        compiler_params=pltpu.CompilerParams(collective_id=1, has_side_effects=True),
+        compiler_params=pltpu.CompilerParams(
+            collective_id=1, has_side_effects=True, vmem_limit_bytes=60 * 1024 * 1024
+        ),
         cost_estimate=pl.CostEstimate(flops=0, bytes_accessed=200000000, transcendentals=0),
         name="gather_weights",
     )(*blocks, *slots, part.reshape(part_rows, 128))
@@ -556,15 +626,15 @@
         out_specs=[vmem] * 4,
         out_shape=[*shapes, shapes[0]],
         scratch_shapes=[pltpu.SemaphoreType.DMA((3,))],
-        compiler_params=pltpu.CompilerParams(vmem_limit_bytes=32 * 1024 * 1024),
+        compiler_params=pltpu.CompilerParams(vmem_limit_bytes=60 * 1024 * 1024),
         cost_estimate=pl.CostEstimate(flops=0, bytes_accessed=8000000, transcendentals=0),
         name="compact",
     )(places, *flat, shift, scale)
 
 
 class Line:
-    def __init__(self, first_stage, buffers, sems):
-        self.first_stage = first_stage
+    def __init__(self, first_stage, slots, buffers, sems):
+        self.first_stage, self.slots = first_stage, slots
         self.shard, self.line_one, self.line_two, self.whole, self.line_three = buffers
         self.send_sem, self.recv_sem, self.store_sem, self.credit = sems
         row = lax.axis_index("row")
@@ -594,7 +664,7 @@
         return self.remote(2, slot, self.whole.at[slot], self.line_three.at[slot], self.outer)
 
     def spend(self, stage, chunk):
-        @pl.when(chunk >= LINE_SLOTS)
+        @pl.when(chunk >= self.slots)
         def _():
             pl.semaphore_wait(self.credit.at[self.first_stage + stage], 1)
 
@@ -670,12 +740,12 @@
     def drain(self):
         @pl.when(self.is_end)
         def _():
-            pl.semaphore_wait(self.credit.at[self.first_stage], LINE_SLOTS)
+            pl.semaphore_wait(self.credit.at[self.first_stage], self.slots)
 
         @pl.when(self.is_middle)
         def _():
-            pl.semaphore_wait(self.credit.at[self.first_stage + 1], LINE_SLOTS)
-            pl.semaphore_wait(self.credit.at[self.first_stage + 2], LINE_SLOTS)
+            pl.semaphore_wait(self.credit.at[self.first_stage + 1], self.slots)
+            pl.semaphore_wait(self.credit.at[self.first_stage + 2], self.slots)
 
 
 def pieces(lengths, chunk, body):
@@ -696,27 +766,65 @@
 def sum_kernel(count, group, per, *refs):
     take = iter(refs)
     lefts = [next(take) for _ in range(count)]
+    right_in = [next(take) for _ in range(count)]
+    projection_in, residual_in, source_in, pick_in = [next(take) for _ in range(4)]
+    parts = [next(take) for _ in range(2)]
+    image_part, bias_part, scale_row = next(take), next(take), next(take)
+    results = [next(take) for _ in range(count)]
+    given, own_block = next(take), next(take)
+    part_results = [next(take) for _ in range(2)]
+    every_image, bias_total = next(take), next(take)
+    units = next(take)
     rights = [next(take) for _ in range(count)]
-    image_part, bias_part, spread = next(take), next(take), next(take)
-    parts = [next(take) for _ in range(2)]
-    results = [next(take) for _ in range(count)]
-    every_image, bias_total, given = next(take), next(take), next(take)
-    part_results = [next(take) for _ in range(2)]
+    projection, residual, source, pick, both, spread, sums = [next(take) for _ in range(7)]
     grads, core_in, pair, upper_in, lower_in, upper_two, lower_two = [next(take) for _ in range(7)]
     main_buffers = [next(take) for _ in range(5)]
     tall_buffers = [next(take) for _ in range(5)]
-    image_in, bias_in, small_send, small_recv = [next(take) for _ in range(4)]
-    send_sem, recv_sem, store_sem, load_sem, give_send, give_recv, credit = take
+    image_sum, image_in, bias_in, small_send, small_recv = [next(take) for _ in range(5)]
+    send_sem, recv_sem, store_sem, load_sem, give_send, give_recv, in_sem, unit_sem, credit = take
     row = lax.axis_index("row")
     near_row, far_row = row + 1 - 2 * lax.rem(row, 2), lax.rem(row + 2, 4)
-    main = Line(5, main_buffers, (send_sem, recv_sem, store_sem.at[0], credit))
-    tall = Line(8, tall_buffers, (send_sem, recv_sem, store_sem.at[1], credit))
+    main = Line(5, LINE_SLOTS, main_buffers, (send_sem, recv_sem, store_sem.at[0], credit))
+    tall = Line(8, tall_buffers[0].shape[0], tall_buffers, (send_sem, recv_sem, store_sem.at[1], credit))
     tall.load_sem = load_sem
     across = [-(-right.shape[1] // TILE_COLUMNS) for right in rights]
     lengths = [left.shape[1] * amount for left, amount in zip(lefts, across)]
     chunks = sum(lengths)
     _, (core, x, y), (sibling, x_mate, y_mate) = mates()
-    upper, lower = pl.ds(0, CUT), pl.ds(CUT, TILE_ROWS - CUT)
+
+    plan, low = [], 0
+    for which, left in enumerate(lefts):
+        for block in range(left.shape[1]):
+            plan.append((low, which, block))
+            low += across[which]
+
+    def unit_copy(unit):
+        _, which, block = plan[unit]
+        origin = lefts[which].at[:, block]
+        return pltpu.make_async_copy(origin, units.at[unit % 2], unit_sem.at[unit % 2])
+
+    arrivals = [
+        pltpu.make_async_copy(origin, target, in_sem.at[at])
+        for at, (origin, target) in enumerate(
+            [
+                *zip(right_in, rights),
+                (projection_in, projection),
+                (residual_in, residual),
+                (source_in, source),
+                (pick_in, pick),
+            ]
+        )
+    ]
+    unit_copy(0).start()
+    for at in (0, 3, 5, 6, 7, 8, 1, 2, 4):
+        arrivals[at].start()
+
+    def both_cuts(chunk, body):
+        for parity, cut in enumerate(CUTS):
+
+            @pl.when(lax.rem(chunk, 2) == parity)
+            def _(cut=cut):
+                body(pl.ds(0, cut), pl.ds(cut, TILE_ROWS - cut), cut)
 
     def main_targets(chunk, body):
         def one(which, at):
@@ -758,17 +866,21 @@
     def to_sibling(slot):
         return remote(0, slot, grads.at[slot, :, :, 1 - core], core_in.at[slot], sibling)
 
-    def upper_first(slot):
-        return remote(1, slot, pair.at[slot, :, 1 - x, upper, :], upper_in.at[slot], x_mate)
-
-    def lower_first(slot):
-        return remote(2, slot, pair.at[slot, 1 - y, :, lower, :], lower_in.at[slot], y_mate)
-
-    def upper_second(slot):
-        return remote(3, slot, pair.at[slot, 1 - y, x, upper, :], upper_two.at[slot], y_mate)
-
-    def lower_second(slot):
-        return remote(4, slot, pair.at[slot, y, 1 - x, lower, :], lower_two.at[slot], x_mate)
+    def upper_first(slot, rows):
+        target = upper_in.at[slot, :, pl.ds(0, rows.size), :]
+        return remote(1, slot, pair.at[slot, :, 1 - x, rows, :], target, x_mate)
+
+    def lower_first(slot, rows):
+        target = lower_in.at[slot, :, pl.ds(0, rows.size), :]
+        return remote(2, slot, pair.at[slot, 1 - y, :, rows, :], target, y_mate)
+
+    def upper_second(slot, rows):
+        target = upper_two.at[slot, pl.ds(0, rows.size), :]
+        return remote(3, slot, pair.at[slot, 1 - y, x, rows, :], target, y_mate)
+
+    def lower_second(slot, rows):
+        target = lower_two.at[slot, pl.ds(0, rows.size), :]
+        return remote(4, slot, pair.at[slot, y, 1 - x, rows, :], target, x_mate)
 
     def spend(stage, chunk):
         @pl.when(chunk >= SLOTS)
@@ -798,7 +910,7 @@
 
     own_half = pl.ds(2 * (row // 2), 2)
     image_hops = [
-        (image_part, image_in, {"img": sibling}),
+        (image_sum, image_in, {"img": sibling}),
         (every_image.at[row, y, x], every_image.at[row, y, x], {"img": y_mate}),
         (every_image.at[row, :, x], every_image.at[row, :, x], {"img": x_mate}),
         (every_image.at[row], every_image.at[row], {"row": near_row}),
@@ -816,33 +928,48 @@
         image.wait()
         bias.wait()
         if hop == 0:
-            summed = image_part[...] + image_in[...]
+            summed = image_sum[...] + image_in[...]
             every_image[row, y, x] = summed.astype(jnp.bfloat16)
         bias_total[...] = (bias_total if hop else bias_part)[...] + bias_in[hop]
 
     def own_shard(chunk, slot):
         line_slot = lax.rem(chunk, LINE_SLOTS)
-        upper_second(slot).wait()
-        main.shard[line_slot, upper, :] = add(pair[slot, y, x, upper, :], upper_two[slot])
-        repay(3, y_mate)
-        lower_second(slot).wait()
-        main.shard[line_slot, lower, :] = add(pair[slot, y, x, lower, :], lower_two[slot])
-        repay(4, x_mate)
+
+        def body(upper, lower, cut):
+            upper_second(slot, upper).wait()
+            main.shard[line_slot, upper, :] = add(
+                pair[slot, y, x, upper, :], upper_two[slot, pl.ds(0, cut), :]
+            )
+            repay(3, y_mate)
+            lower_second(slot, lower).wait()
+            main.shard[line_slot, lower, :] = add(
+                pair[slot, y, x, lower, :], lower_two[slot, pl.ds(0, TILE_ROWS - cut), :]
+            )
+            repay(4, x_mate)
+
+        both_cuts(chunk, body)
         main.enter(chunk, line_slot)
 
     def second_axis(chunk, slot):
-        upper_first(slot).wait()
-        for at in range(2):
-            pair[slot, at, x, upper, :] = add(pair[slot, at, x, upper, :], upper_in[slot, at])
-        repay(1, x_mate)
-        spend(3, chunk)
-        upper_second(slot).start()
-        lower_first(slot).wait()
-        for at in range(2):
-            pair[slot, y, at, lower, :] = add(pair[slot, y, at, lower, :], lower_in[slot, at])
-        repay(2, y_mate)
-        spend(4, chunk)
-        lower_second(slot).start()
+        def body(upper, lower, cut):
+            upper_first(slot, upper).wait()
+            for at in range(2):
+                pair[slot, at, x, upper, :] = add(
+                    pair[slot, at, x, upper, :], upper_in[slot, at, pl.ds(0, cut), :]
+                )
+            repay(1, x_mate)
+            spend(3, chunk)
+            upper_second(slot, upper).start()
+            lower_first(slot, lower).wait()
+            for at in range(2):
+                pair[slot, y, at, lower, :] = add(
+                    pair[slot, y, at, lower, :], lower_in[slot, at, pl.ds(0, TILE_ROWS - cut), :]
+                )
+            repay(2, y_mate)
+            spend(4, chunk)
+            lower_second(slot, lower).start()
+
+        both_cuts(chunk, body)
 
     def first_axis(chunk, slot):
         to_sibling(slot).wait()
@@ -853,19 +980,24 @@
                 )
         repay(0, sibling)
         spend(1, chunk)
-        upper_first(slot).start()
         spend(2, chunk)
-        lower_first(slot).start()
+
+        def body(upper, lower, cut):
+            upper_first(slot, upper).start()
+            lower_first(slot, lower).start()
+
+        both_cuts(chunk, body)
 
     def multiply(chunk, slot):
         def one(which, at):
-            left, right = lefts[which], rights[which]
+            right = rights[which]
             column, whole_tiles = lax.rem(at, across[which]), right.shape[1] // TILE_COLUMNS
+            first_unit = [one_of for _, one_of, _ in plan].index(which)
+            slot_of_unit = lax.rem(first_unit + at // across[which], 2)
 
             def times(values):
                 for half in range(2):
-                    rows = left[pl.ds(4 * half, 4), at // across[which]]
-                    rows = rows.reshape(4 * TILE_ROWS, -1)
+                    rows = units[slot_of_unit, pl.ds(4 * half, 4)].reshape(4 * TILE_ROWS, -1)
                     product = jnp.dot(rows, values, preferred_element_type=jnp.float32)
                     grads[slot, half] = product.astype(jnp.bfloat16).reshape(
                         2, 2, TILE_ROWS, TILE_COLUMNS
@@ -885,52 +1017,124 @@
                 gap = jnp.zeros((rest.shape[0], TILE_COLUMNS - rest.shape[1]), rest.dtype)
                 times(jnp.concatenate([rest, gap], axis=1))
 
+        for unit, (begin, which, block) in enumerate(plan):
+
+            @pl.when(chunk == begin)
+            def _(unit=unit, which=which, block=block):
+                unit_copy(unit).wait()
+                if unit + 1 < len(plan):
+                    unit_copy(unit + 1).start()
+                if block == 0 and which != 3:
+                    arrivals[which].wait()
+
         pieces(lengths, chunk, one)
         spend(0, chunk)
         to_sibling(slot).start()
 
     stages = [
-        (12, LINE_SLOTS, main.end),
-        (11, LINE_SLOTS, main.last),
-        (9, LINE_SLOTS, main.third),
-        (7, LINE_SLOTS, main.second),
+        (LAST_LAG, LINE_SLOTS, main.end),
+        (14, LINE_SLOTS, main.last),
+        (11, LINE_SLOTS, main.third),
+        (8, LINE_SLOTS, main.second),
         (5, SLOTS, own_shard),
         (3, SLOTS, second_axis),
         (1, SLOTS, first_axis),
         (0, SLOTS, multiply),
     ]
 
+    def token_rows(at):
+        rows = pl.ds(pl.multiple_of(at * TOKEN_ROWS, TOKEN_ROWS), TOKEN_ROWS)
+        grad = lax.dot_general(
+            rights[3][rows, :], projection[...], LAST, preferred_element_type=jnp.float32
+        )
+        tokens = source[rows, :].astype(jnp.float32)
+        centre = tokens - jnp.mean(tokens, axis=-1, keepdims=True)
+        spread_of = lax.rsqrt(jnp.mean(centre * centre, axis=-1, keepdims=True) + 1e-06)
+        norm = centre * spread_of
+        sums[0:1, :] += jnp.sum(grad, axis=0, keepdims=True)
+        sums[1:2, :] += jnp.sum(grad * norm, axis=0, keepdims=True)
+        grad = grad * (1.0 + scale_row[...])
+        along = jnp.mean(grad * norm, axis=-1, keepdims=True)
+        grad = spread_of * (grad - jnp.mean(grad, axis=-1, keepdims=True) - norm * along)
+        both[core, rows, :] = (residual[rows, :] + grad).astype(jnp.bfloat16)
+
+    token_blocks = source.shape[0] // TOKEN_ROWS // AT_ONCE
+    lanes = source.shape[1] // 128
+    swapped, handed = token_blocks + 2, token_blocks + 2 + 4 // AT_ONCE
+
+    def token_swap():
+        return small(10, both.at[core], both.at[core], {"img": sibling})
+
+    def own_copy():
+        return pltpu.make_async_copy(spread.at[0], own_block, in_sem.at[9])
+
+    def tokens_step(at):
+        @pl.when(at == 0)
+        def _():
+            for which in (3, 5, 6, 7):
+                arrivals[which].wait()
+            sums[...] = jnp.zeros_like(sums)
+
+        @pl.when(at < token_blocks)
+        def _():
+            for which in range(AT_ONCE):
+                token_rows(AT_ONCE * at + which)
+
+        @pl.when(at == token_blocks)
+        def _():
+            token_swap().start()
+            image_sum[...] = image_part[...]
+            for which in range(2):
+                for lane in range(lanes):
+                    values = sums[which : which + 1, pl.ds(lane * 128, 128)]
+                    image_sum[pl.ds(which * lanes + lane, 1), :] = values
+
+        @pl.when(at == swapped)
+        def _():
+            token_swap().wait()
+            arrivals[8].wait()
+
+        @pl.when((at >= swapped) & (at < handed))
+        def _():
+            tokens = both[...].reshape(2 * both.shape[1], -1)
+            for which in range(AT_ONCE):
+                shift = AT_ONCE * (at - swapped) + which
+                laid = jnp.dot(pick[shift], tokens, preferred_element_type=jnp.float32)
+                spread[shift] = laid.astype(jnp.bfloat16)
+
+        @pl.when(at == handed)
+        def _():
+            own_copy().start()
+
+        @pl.when(at >= handed)
+        def _():
+            sender.trickle(at - handed, GIVE_ROWS)
+
     def step(at, carry):
         for hop in range(5):
 
-            @pl.when(at == 4 * hop)
+            @pl.when(at == token_blocks + 1 + 4 * hop)
             def _(hop=hop):
                 small_hop(hop, True)
 
-            @pl.when(at == 4 * hop + 3)
+            @pl.when(at == token_blocks + 4 + 4 * hop)
             def _(hop=hop):
                 small_hop(hop, False)
 
-
-        @pl.when(lax.rem(at, 3) < 2)
-        def _():
-            sender.start(2 * (at // 3) + lax.rem(at, 3), GIVE_ROWS)
-
-        for line, tiles in ((tall, tall_tiles),):
-            for lag, body in (
-                (8, line.end),
-                (7, line.last),
-                (5, line.third),
-                (3, line.second),
-                (1, line.loaded),
-                (0, functools.partial(line.load, begin=True)),
-            ):
-                tile = (at - lag) // SIDE_PACE
-                due = lax.rem(at - lag, SIDE_PACE) == 0
-
-                @pl.when((at >= lag) & due & (tile < tiles))
+        for lag, body in (
+            (8, tall.end),
+            (7, tall.last),
+            (5, tall.third),
+            (3, tall.second),
+            (1, tall.loaded),
+            (0, functools.partial(tall.load, begin=True)),
+        ):
+            for which in range(AT_ONCE):
+                tile = AT_ONCE * (at - lag) + which
+
+                @pl.when((at >= lag) & (tile < tall_tiles))
                 def _(tile=tile, body=body):
-                    body(tile, lax.rem(tile, LINE_SLOTS))
+                    body(tile, tile)
 
         for lag, slots, body in stages:
             chunk = at - lag
@@ -939,9 +1143,11 @@
             def _(chunk=chunk, slots=slots, body=body):
                 body(chunk, lax.rem(chunk, slots))
 
+        tokens_step(at)
         return carry
 
-    lax.fori_loop(0, chunks + 12, step, 0)
+    lax.fori_loop(0, chunks + LAST_LAG, step, 0)
+    own_copy().wait()
     for stage in range(5):
         pl.semaphore_wait(credit.at[stage], SLOTS)
     for line in (main, tall):
@@ -954,70 +1160,89 @@
     return operand.T.reshape(8, blocks, TILE_ROWS, operand.shape[0])
 
 
-def sum_gradients(lefts, rights, image_part, bias_part, spread, parts, group, per):
-    bf16 = jnp.bfloat16
-    shapes = [
-        jax.ShapeDtypeStruct(
-            (left.shape[1], TILE_ROWS, -(-right.shape[1] // TILE_COLUMNS) * TILE_COLUMNS), bf16
-        )
-        for left, right in zip(lefts, rights)
-    ]
+def sum_gradients(lefts, rights, tokens_side, image_part, bias_part, scale_row, parts, group, per):
+    bf16, f32 = jnp.bfloat16, jnp.float32
+    projection, residual, source, pick = tokens_side
+    length, width = source.shape
     image_rows, bias_rows = image_part.size // 128, bias_part.size // 128
     padded = -(-image_rows // 16) * 16
     image_part = jnp.pad(image_part.reshape(image_rows, 128), ((0, padded - image_rows), (0, 0)))
     bias_part = bias_part.reshape(bias_rows, 128)
-    shapes += [
+    block = (pick.shape[1], width)
+    shapes = [
+        *[
+            jax.ShapeDtypeStruct(
+                (left.shape[1], TILE_ROWS, -(-right.shape[1] // TILE_COLUMNS) * TILE_COLUMNS), bf16
+            )
+            for left, right in zip(lefts, rights)
+        ],
+        jax.ShapeDtypeStruct((3, *block), bf16),
+        jax.ShapeDtypeStruct(block, bf16),
+        *[jax.ShapeDtypeStruct(part.shape, bf16) for part in parts],
         jax.ShapeDtypeStruct((4, 2, 2, padded, 128), bf16),
-        jax.ShapeDtypeStruct((bias_rows, 128), jnp.float32),
-        jax.ShapeDtypeStruct((3, *spread.shape[1:]), bf16),
-        *[jax.ShapeDtypeStruct(part.shape, bf16) for part in parts],
+        jax.ShapeDtypeStruct((bias_rows, 128), f32),
     ]
     tile = (TILE_ROWS, TILE_COLUMNS)
     vmem, hbm = pl.BlockSpec(memory_space=pltpu.VMEM), pl.BlockSpec(memory_space=pl.ANY)
     flops = 2 * sum(left.size * right.shape[1] for left, right in zip(lefts, rights))
+    tiles = sum(part.shape[1] // LINE_TILE for part in parts)
+    most = max(LINE_SLOTS, tiles)
     results = pl.pallas_call(
         functools.partial(sum_kernel, len(lefts), group, per),
-        in_specs=[vmem] * (2 * len(lefts) + 2) + [hbm] * 3,
-        out_specs=[hbm] * len(lefts) + [vmem] * 2 + [hbm] * 3,
+        in_specs=[hbm] * (2 * len(lefts) + 6) + [vmem] * 3,
+        out_specs=[hbm] * (len(lefts) + 4) + [vmem] * 2,
         out_shape=shapes,
         scratch_shapes=[
+            pltpu.VMEM((2, 8, TILE_ROWS, length), bf16),
+            *[pltpu.VMEM(right.shape, bf16) for right in rights],
+            pltpu.VMEM(projection.shape, bf16),
+            pltpu.VMEM(residual.shape, f32),
+            pltpu.VMEM(source.shape, bf16),
+            pltpu.VMEM(pick.shape, bf16),
+            pltpu.VMEM((2, length, width), bf16),
+            pltpu.VMEM((4, *block), bf16),
+            pltpu.VMEM((2, width), f32),
             pltpu.VMEM((SLOTS, 2, 2, 2, *tile), bf16),
             pltpu.VMEM((SLOTS, 2, 2, *tile), bf16),
             pltpu.VMEM((SLOTS, 2, 2, *tile), bf16),
-            pltpu.VMEM((SLOTS, 2, CUT, TILE_COLUMNS), bf16),
-            pltpu.VMEM((SLOTS, 2, TILE_ROWS - CUT, TILE_COLUMNS), bf16),
-            pltpu.VMEM((SLOTS, CUT, TILE_COLUMNS), bf16),
-            pltpu.VMEM((SLOTS, TILE_ROWS - CUT, TILE_COLUMNS), bf16),
+            *[pltpu.VMEM((SLOTS, 2, max(CUTS), TILE_COLUMNS), bf16)] * 2,
+            *[pltpu.VMEM((SLOTS, max(CUTS), TILE_COLUMNS), bf16)] * 2,
             *[pltpu.VMEM((LINE_SLOTS, *tile), bf16)] * 5,
-            *[pltpu.VMEM((LINE_SLOTS, parts[0].shape[0], LINE_TILE), bf16)] * 5,
-            pltpu.VMEM((padded, 128), jnp.float32),
-            pltpu.VMEM((5, bias_rows, 128), jnp.float32),
-            pltpu.SemaphoreType.DMA((10,)),
-            pltpu.SemaphoreType.DMA((10,)),
-            pltpu.SemaphoreType.DMA((11, LINE_SLOTS)),
-            pltpu.SemaphoreType.DMA((11, LINE_SLOTS)),
-            pltpu.SemaphoreType.DMA((2, LINE_SLOTS)),
-            pltpu.SemaphoreType.DMA((LINE_SLOTS,)),
+            *[pltpu.VMEM((tiles, parts[0].shape[0], LINE_TILE), bf16)] * 5,
+            pltpu.VMEM((padded, 128), f32),
+            pltpu.VMEM((padded, 128), f32),
+            pltpu.VMEM((5, bias_rows, 128), f32),
+            pltpu.SemaphoreType.DMA((11,)),
+            pltpu.SemaphoreType.DMA((11,)),
+            pltpu.SemaphoreType.DMA((11, most)),
+            pltpu.SemaphoreType.DMA((11, most)),
+            pltpu.SemaphoreType.DMA((2, most)),
+            pltpu.SemaphoreType.DMA((tiles,)),
             pltpu.SemaphoreType.DMA((3,)),
             pltpu.SemaphoreType.DMA((3,)),
+            pltpu.SemaphoreType.DMA((10,)),
+            pltpu.SemaphoreType.DMA((2,)),
             pltpu.SemaphoreType.REGULAR((11,)),
         ],
         compiler_params=pltpu.CompilerParams(
-            collective_id=0, has_side_effects=True, vmem_limit_bytes=56 * 1024 * 1024
+            collective_id=0, has_side_effects=True, vmem_limit_bytes=60 * 1024 * 1024
         ),
         cost_estimate=pl.CostEstimate(
             flops=flops, bytes_accessed=600000000, transcendentals=0
         ),
         name="sum_gradients",
-    )(*lefts, *rights, image_part, bias_part, spread, *parts)
+    )(*lefts, *rights, *tokens_side, *parts, image_part, bias_part, scale_row)
+    take = iter(results)
+    summed = [next(take) for _ in lefts]
     summed = [
-        result.reshape(-1, result.shape[2])[:, : right.shape[1]].astype(jnp.float32)
-        for result, right in zip(results, rights)
+        result.reshape(-1, result.shape[2])[:, : right.shape[1]].astype(f32)
+        for result, right in zip(summed, rights)
     ]
-    every_image, bias_total, given = results[len(lefts) : len(lefts) + 3]
-    parts = [part.astype(jnp.float32) for part in results[len(lefts) + 3 :]]
+    given, own_block = next(take), next(take)
+    parts = [next(take).astype(f32) for _ in parts]
+    every_image, bias_total = take
     every_image = every_image[:, :, :, :image_rows].reshape(4, 4, -1).transpose(1, 0, 2)
-    return summed, every_image.reshape(16, -1), bias_total.reshape(-1), given, parts
+    return summed, every_image.reshape(16, -1), bias_total.reshape(-1), [own_block, *given], parts
 
 
 def local(
@@ -1074,9 +1299,9 @@
         source_row = (row_rank + shift) % n_row
         begin = lax.dynamic_index_in_dim(first_of, source_row, 0, keepdims=False)
         limit = lax.dynamic_index_in_dim(own_counts, source_row, 0, keepdims=False) * RW
-        hit = (kept[:, None] == begin + position[None, :]) & (position[None, :] < limit)
+        hit = (kept[None, :] == begin + position[:, None]) & (position[:, None] < limit)
         picks.append(hit)
-    pick = jnp.concatenate(picks, axis=1).astype(bf16)
+    pick = jnp.concatenate(picks, axis=0).astype(bf16)
 
     def image_of(shift):
         return (((row_rank - shift) % n_row) // group) % per
@@ -1088,7 +1313,7 @@
             if shift:
                 piece = lax.ppermute(piece, ("img", "row"), route(shift, False))
             pieces.append(piece)
-        packed = matmul(pick, jnp.concatenate(pieces, axis=0)).astype(bf16)
+        packed = weight_grad(pick, jnp.concatenate(pieces, axis=0)).astype(bf16)
         own = lax.dynamic_slice_in_dim(packed, core * length, length, 0)
         other = lax.dynamic_slice_in_dim(packed, (1 - core) * length, length, 0)
         return jnp.where(receives, own, swap(other, "img", 1))
@@ -1099,7 +1324,7 @@
             jnp.concatenate([operand, other], axis=0),
             jnp.concatenate([other, operand], axis=0),
         )
-        return weight_grad(pick, both).astype(bf16).reshape(n_row, slot_len, -1)
+        return matmul(pick, both).astype(bf16).reshape(n_row, slot_len, -1)
 
     def give_send(spread):
         sent = [
@@ -1218,7 +1443,7 @@
         source, own_cotangent, own_targets, h_att = compact(
             places.astype(jnp.int32), arrived, shift_att, scale_att
         )
-        source = source.astype(f32)
+        source_rows, source = source, source.astype(f32)
         own_cotangent, own_targets = own_cotangent.astype(f32), own_targets.astype(f32)
     else:
         source = bring(tokens).astype(f32)
@@ -1277,7 +1502,7 @@
     d_attn = (d_residual * gate_att).astype(bf16)
     d_mixed = transposed(d_attn, out_full).astype(bf16)
     third_part, d_mixed = lax.optimization_barrier((third_part, d_mixed))
-    d_query, d_own, d_rest, block_given = attend_back(
+    d_qkv, d_other = attend_back(
         qkv_rows,
         rest,
         head_mix,
@@ -1287,40 +1512,46 @@
         (group, per) if small_plane else None,
     )
     if small_plane:
-        block_out = give_merge([block_spread[0], *block_given])
+        block_out = give_merge([block_spread[0], *d_other])
     else:
         block_out = give_merge(give_send(block_spread))
-    second_part, d_query = lax.optimization_barrier((second_part, d_query))
-    d_own = d_own.astype(f32)
-    for bit in reversed(bits):
-        full = jnp.concatenate([d_own, d_rest.astype(f32)], axis=0)
-        half = full.shape[0] // 2
-        full = full[:half] + swap(full[half:].astype(bf16), "row", bit).astype(f32)
-        d_own, d_rest = full[:length], full[length:].astype(bf16)
-    d_own = d_own + swap(d_rest, "img", 1).astype(f32)
-    d_qkv = jnp.concatenate([d_query, d_own.astype(bf16)], axis=1)
-    d_source, d_shift_att, d_scale_att = jax.vjp(modulate, source, shift_att, scale_att)[1](
-        transposed(d_qkv, qkv_full)
-    )
-    tokens_own = (d_residual + d_source).astype(bf16)
-    spread = give_start(tokens_own, swap(tokens_own, "img", 1))
-    own_mod = jnp.concatenate(
-        [d_shift_att[0], d_scale_att[0], d_gate_att, d_shift_mlp[0], d_scale_mlp[0], d_gate_mlp]
-    )
+        d_own, d_rest = d_qkv[:, width:].astype(f32), d_other
+        for bit in reversed(bits):
+            full = jnp.concatenate([d_own, d_rest.astype(f32)], axis=0)
+            half = full.shape[0] // 2
+            full = full[:half] + swap(full[half:].astype(bf16), "row", bit).astype(f32)
+            d_own, d_rest = full[:length], full[length:].astype(bf16)
+        d_own = d_own + swap(d_rest, "img", 1).astype(f32)
+        d_qkv = jnp.concatenate([d_qkv[:, :width], d_own.astype(bf16)], axis=1)
+    second_part, d_qkv = lax.optimization_barrier((second_part, d_qkv))
+    late_mod = jnp.concatenate([d_gate_att, d_shift_mlp[0], d_scale_mlp[0], d_gate_mlp])
     lefts.append(left_first)
     rights = [d_mlp, d_pre, d_attn, d_qkv, d_lin_one]
     proj_parts = [second_part, third_part]
     if small_plane:
-        tied = (spread, proj_parts, rights, own_mod, bias_sum)
-        spread, proj_parts, rights, own_mod, bias_sum = lax.optimization_barrier(tied)
-        large, d_mod, bias_sum, given, proj_grads = sum_gradients(
-            lefts, rights, own_mod, bias_sum, spread, proj_parts, group, per
-        )
-        grad_tokens = give_merge([spread[0], *given])
+        tied = (proj_parts, rights, d_residual, late_mod, bias_sum)
+        proj_parts, rights, d_residual, late_mod, bias_sum = lax.optimization_barrier(tied)
+        large, d_mod, bias_sum, blocks, proj_grads = sum_gradients(
+            lefts,
+            rights,
+            (qkv_full, d_residual, source_rows, pick.reshape(n_row, slot_len, -1)),
+            jnp.concatenate([jnp.zeros((2 * width,), f32), late_mod]),
+            bias_sum,
+            scale_att,
+            proj_parts,
+            group,
+            per,
+        )
+        grad_tokens = give_merge(blocks)
     else:
-        grad_tokens = give_merge(give_send(spread))
+        d_source, d_shift_att, d_scale_att = jax.vjp(modulate, source, shift_att, scale_att)[1](
+            transposed(d_qkv, qkv_full)
+        )
+        tokens_own = (d_residual + d_source).astype(bf16)
+        grad_tokens = give_merge(give_send(give_start(tokens_own, swap(tokens_own, "img", 1))))
         proj_grads = [row_sum(part, at) for at, part in enumerate(proj_parts)]
         large = [over_row(offload_shards(*pair)) for pair in zip(lefts, rights)]
+        own_mod = jnp.concatenate([d_shift_att[0], d_scale_att[0], late_mod])
         slot_id = column * (img_rank // 2) + place
         placed = jnp.zeros((n_images, mod_width), f32)
         placed = lax.dynamic_update_slice(placed, own_mod[None, :], (slot_id, 0))

time: 689 us -> 665 us (0.965)
  waiting for transfers between devices: 5.9 us -> 23.1 us
  Pallas kernels: 417 us -> 405 us
  matrix products: 152 us -> 142 us
    all_gather x4, waiting for transfers between devices: 0.01 us -> 18.5 us  [fetch(): return lax.all_gather(operand, 'img', axis=0, tiled=True)]
    pallas_call x1, Pallas kernels: 132 us -> 114 us  [gather_weights(): pl.pallas_call(functools.partial(gather_kernel, count, group, per), in_sp...]
    dot_general x5 -> x3, matrix products: 27.3 us -> 13.1 us  [weight_grad(): lax.dot_general(left_side, right_side, FIRST, preferred_element_type=jnp....]
    dot_general x8 -> x9, matrix products: 59.8 us -> 72.9 us  [matmul(): return jnp.dot(left_side, right_side, preferred_element_type=jnp.float32)]
    dot_general x8 -> x7, matrix products: 62.8 us -> 54.3 us  [transposed(): lax.dot_general(left_side, right_side, LAST, preferred_element_type=jnp.f...]
    unnamed x143 -> x110, local copies, waits for them, and re-layouts: 19.9 us -> 13.8 us
    convert_element_type x9 -> x8, other arithmetic: 14.3 us -> 12.6 us  [the longest x5 6.99 us: sum_gradients(): result.reshape(-1, result.shape[2])[:, :right.shape[1]].astype(f32)]
  transfers between devices with their start and end apart: 14 -> 12, of which waited for: 4 -> 4; matrix products, arithmetic and copies ran while one was open for 23% -> 24% of each run, Pallas kernels for 31% -> 29%
where the time goes in v4:
time: 665 us; the launch traced here: 661 us
  Pallas kernels  405 us (61%)
  matrix products  142 us (21%)
  local copies, waits for them, and re-layouts  36.4 us (5%)
  other arithmetic  30.6 us (5%)
  waiting for transfers between devices  23.1 us (3%)
  between operations  17.9 us (3%)
    pallas_call x1, Pallas kernels, sum_gradients(): pl.pallas_call(functools.partial(sum_kernel, len(lefts), group, per), in_...  210 us
    pallas_call x1, Pallas kernels, gather_weights(): pl.pallas_call(functools.partial(gather_kernel, count, group, per), in_sp...  114 us
    dot_general x9, matrix products, matmul(): return jnp.dot(left_side, right_side, preferred_element_type=jnp.float32)  72.9 us
    dot_general x7, matrix products, transposed(): lax.dot_general(left_side, right_side, LAST, preferred_element_type=jnp.f...  54.3 us
    pallas_call x1, Pallas kernels, attend_back(): pl.pallas_call(functools.partial(attend_back_kernel, give), in_specs=[vme...  49.2 us
    pallas_call x1, Pallas kernels, attend(): pl.pallas_call(attend_kernel, in_specs=[vmem] * 2, out_specs=[vmem] * 2,...  24.9 us
    all_gather x4, waiting for transfers between devices, fetch(): return lax.all_gather(operand, 'img', axis=0, tiled=True)  18.5 us
    unnamed x110, local copies, waits for them, and re-layouts  13.8 us
  transfers between devices with their start and end apart: 12, of which 4 were waited for; matrix products, arithmetic and copies ran while one was open for 24% of the time, Pallas kernels for 29%

profile of v4, /device:TPU:0, one launch (start us, length us, event | category | flops | bytes accessed | tf_op | source)
XLA Modules:
  0.0 661.2 jit_solution(14576239572687210313)
XLA Ops:
  11.1 2.8 collective-permute-start.2
  15.6 2.1 collective-permute-start.3
  22.0 113.7 %gather_weights.1 = (bf16[8,144,3456]{2,1,0:T(8,128)(2,1)}, bf16[8,144,1152]{2,1,0:T(8,128)(2,1)}, bf16[8,256,768]{2,1,0:T(8,128)(2,1)}, bf16[4,384,1152]{2,1,0:...) custom-call(bf16[144,3456]{1,0:T(8,128)(2,1)} %refs_0_.1, ...), custom_call_target="tpu_custom_call" | custom-call | bytes 200000000 | tf_op jit(solution)/shard_map/gather_weights/pallas_call | solution.py:552
  137.4 6.7 %compact.1 = (bf16[512,1152]{1,0:T(8,128)(2,1)}, bf16[512,1152]{1,0:T(8,128)(2,1)}, bf16[512,768]{1,0:T(8,128)(2,1)}, bf16[512,1152]{1,0:T(8,128)(2,1)}) custom-call(s32[16]{0:T(128)} %multiply_add_fusion.3.places, bf16[1536,1152]{1,0:T(8,128)(2,1)} %bitcast.137, bf16[1536,1152]{1,0:T(8,128)(2,1)} %bitcast.138, bf16[1536,768]{1,0:T(8,128)(2,1)} %bitcast.140, ...), custom_call_target="tpu_custom_call" | custom-call | bytes 8000000 | tf_op jit(solution)/shard_map/compact/pallas_call | solution.py:623
  144.1 8.5 %convolution_convert_fusion.2.own_ref = bf16[512,3456]{1,0:T(8,128)(2,1)S(1)} fusion(bf16[512,1152]{1,0:T(8,128)(2,1)} %get-tuple-element.69, bf16[1152,3456]{1,0:T(8,128)(2,1)} %bitcast.165), kind=kOutput, calls=%fused_computation.26 | convolution fusion | flops 4078632960 | bytes 12681216 | tf_op jit(solution)/shard_map/dot_general | solution.py:39
  152.6 1.8 copy-done.18
  166.1 2.4 copy.48
  169.4 24.9 %attend.1 = (bf16[512,1152]{1,0:T(8,128)(2,1)}, f32[16,1,512]{2,1,0:T(1,128)}) custom-call(bf16[512,3456]{1,0:T(8,128)(2,1)} %copy-done.18, bf16[512,2304]{1,0:T(8,128)(2,1)} %collective-permute-done.4.rest_ref), custom_call_target="tpu_custom_call" | custom-call | flops 8589934592 | bytes 14155776 | tf_op jit(solution)/shard_map/attend/pallas_call | solution.py:129
  194.4 5.4 fusion.73
  203.1 2.4 copy.47
  205.5 15.5 %fusion.14 = (bf16[4608,512]{0,1:T(8,128)(2,1)}, f32[512,4608]{1,0:T(8,128)}) fusion(f32[4608]{0:T(1024)S(1)} %slice_bitcast_fusion, bf16[1152,4608]{1,0:T(8,128)(2,1)} %all-gather.5.cloned.1.call-done, f32[512,1152]{1,0:T(8,128)} %copy-done.1, f32[1152]{0:T(1024)S(1)} %get-tuple-element.125, f32[1152]{0:T(1024)S(1)} %get-tuple-element.123, ...), kind=kOutput, calls=%fused_computation.17 | convolution fusion | flops 5462360064 | bytes 27163648 | tf_op jit(solution)/shard_map/dot_general | solution.py:39
  221.0 6.7 %copy.45 = bf16[4608,512]{1,0:T(8,128)(2,1)} copy(bf16[4608,512]{0,1:T(8,128)(2,1)} %get-tuple-element.154) | data formatting | bytes 9437184 | tf_op jit(solution)/shard_map/convert_element_type | solution.py:1463
  227.7 13.7 %fusion.15 = f32[512,1152]{1,0:T(8,128)S(1)} fusion(bf16[4608,1152]{1,0:T(8,128)(2,1)} %all-gather.7.cloned.1.call-done, f32[512,4608]{1,0:T(8,128)} %get-tuple-element.155, f32[4608]{0:T(1024)S(1)} %slice_bitcast_fusion), kind=kOutput, calls=%fused_computation.27 | convolution fusion | flops 5459410944 | bytes 22431744 | tf_op jit(solution)/shard_map/dot_general | solution.py:39
  244.5 7.9 %multiply_convert_fusion.3 = (bf16[512,2048]{1,0:T(8,128)(2,1)}, f32[512,2048]{1,0:T(8,128)}) fusion(bf16[512,1152]{1,0:T(8,128)(2,1)S(1)} %add_convert_fusion, bf16[1152,2048]{1,0:T(8,128)(2,1)} %all-gather.9.cloned.1.call-done), kind=kOutput, calls=%fused_computation.36 | convolution fusion | flops 2421161984 | bytes 12189696 | tf_op jit(solution)/shard_map/dot_general | solution.py:39
  252.4 8.6 %convolution_convert_fusion.1 = bf16[1536,1152]{1,0:T(8,128)(2,1)} fusion(bf16[512,1152]{1,0:T(8,128)(2,1)} %collective-permute-done.5, bf16[512,1152]{1,0:T(8,128)(2,1)S(1)} %add_convert_fusion, pred[]{:T(512)S(6)} %eq.198, pred[384,1024]{1,0:T(32,128)(4,1)S(1)} %copy-done.13, pred[384,1024]{1,0:T(32,128)(4,1)S(1)} %copy-done.11, ...), kind=kOutput, calls=%fused_computation.22 | convolution fusion | flops 3640983552 | bytes 7471105 | tf_op jit(solution)/shard_map/dot_general | solution.py:39
  261.0 18.5 %all-gather.11.cloned.1.call-done = bf16[2048,2048]{1,0:T(8,128)(2,1)} async-done(((bf16[256,2048]{1,0:T(8,128)(2,1)}), bf16[2048,2048]{1,0:T(8,128)(2,1)}) %all-gather.11.cloned.1.call-update) | async-done | bytes 8388624 | tf_op jit(solution)/shard_map/all_gather | solution.py:1349
  279.5 11.0 %multiply_convert_fusion.2 = (bf16[512,2048]{1,0:T(8,128)(2,1)S(1)}, f32[512,2048]{1,0:T(8,128)}) fusion(bf16[512,2048]{1,0:T(8,128)(2,1)} %get-tuple-element.75, bf16[2048,2048]{1,0:T(8,128)(2,1)} %all-gather.11.cloned.1.call-done), kind=kOutput, calls=%fused_computation.34 | convolution fusion | flops 4300210176 | bytes 16777216 | tf_op jit(solution)/shard_map/dot_general | solution.py:39
  290.5 2.0 multiply_reduce_fusion.5
  293.8 3.5 convolution_convert_fusion.3
  298.5 5.9 fusion.18
  305.7 6.9 %convolution_convert_fusion = bf16[2048,2048]{1,0:T(8,128)(2,1)} fusion(bf16[512,2048]{1,0:T(8,128)(2,1)S(1)} %copy-done.51, bf16[512,2048]{1,0:T(8,128)(2,1)S(1)} %fusion.18), kind=kOutput, calls=%fused_computation.21 | convolution fusion | flops 4299161600 | bytes 12582912 | tf_op jit(solution)/shard_map/dot_general | solution.py:47
  313.8 3.1 fusion.70
  316.9 11.1 %fusion.21.refs_9_ = bf16[512,2048]{1,0:T(8,128)(2,1)S(1)} fusion(f32[512,2048]{1,0:T(8,128)} %get-tuple-element.157, bf16[512,2048]{1,0:T(8,128)(2,1)} %copy-done.52, bf16[2048,2048]{1,0:T(8,128)(2,1)} %all-gather.11.cloned.1.call-done), kind=kOutput, calls=%fused_computation.33 | convolution fusion | flops 4305453056 | bytes 16777216 | tf_op jit(solution)/shard_map/dot_general | solution.py:43
  328.1 3.0 multiply_convert_fusion.5
  331.1 18.6 %convert_reduce_fusion = (f32[4608]{0:T(1024)}, bf16[512,4608]{1,0:T(8,128)(2,1)}) fusion(f32[512,4608]{1,0:T(8,128)} %get-tuple-element.155, f32[4608]{0:T(1024)S(1)} %slice_bitcast_fusion, bf16[512,1152]{1,0:T(8,128)(2,1)S(1)} %get-tuple-element.96.refs_5_, bf16[4608,1152]{1,0:T(8,128)(2,1)} %all-gather.7.cloned.1.call-done), kind=kOutput, calls=%fused_computation.18 | convolution fusion | flops 5490077184 | bytes 25989120 | tf_op jit(solution)/shard_map/dot_general | solution.py:43
  349.7 12.3 %multiply_reduce_fusion.1 = (f32[1152]{0:T(1024)S(1)}, f32[512]{0:T(512)S(1)}, f32[1152]{0:T(1024)S(1)}, f32[512,1152]{1,0:T(8,128)S(1)}) fusion(f32[512,1152]{1,0:T(8,128)S(1)} %copy-done.3, f32[512]{0:T(512)S(1)} %fusion.58, f32[512]{0:T(512)S(1)} %broadcast_multiply_fusion, f32[1152]{0:T(1024)S(1)} %get-tuple-element.123, ...), kind=kOutput, calls=%fused_computation.50 | convolution fusion | flops 5440534016 | bytes 20073984 | tf_op jit(solution)/shard_map/dot_general | solution.py:43
  368.0 2.9 convolution_convert_fusion.4.d_ref
  370.9 49.2 %attend_back.1 = (bf16[512,3456]{1,0:T(8,128)(2,1)}, bf16[3,384,1152]{2,1,0:T(8,128)(2,1)}) custom-call(bf16[512,3456]{1,0:T(8,128)(2,1)} %copy-done.18, bf16[512,2304]{1,0:T(8,128)(2,1)} %collective-permute-done.4.rest_ref, bf16[512,1152]{1,0:T(8,128)(2,1)} %get-tuple-element.71.mix_ref, bf16[512,1152]{1,0:T(8,128)(2,1)} %convolution_convert_fusion.4.d_ref, ...), custom_call_target="tpu_custom_call" | custom-call | flops 21474836480 | bytes 28311552 | tf_op jit(solution)/shard_map/attend_back/pallas_call | solution.py:296
  420.1 2.3 select_select_fusion.1
  424.4 210.4 %sum_gradients.1 = (bf16[4,144,1152]{2,1,0:T(8,128)(2,1)}, bf16[1,144,4608]{2,1,0:T(8,128)(2,1)}, bf16[1,144,1152]{2,1,0:T(8,128)(2,1)}, bf16[1,144,3456]{2,1,0:...) custom-call(bf16[8,4,144,512]{3,2,1,0:T(8,128)(2,1)} %bitcast.135, ...), custom_call_target="tpu_custom_call" | custom-call | flops 18723373056 | bytes 600000000 | tf_op jit(solution)/shard_map/sum_gradients/pallas_call | solution.py:1190
  636.7 2.7 fusion.77
  645.5 1.8 bitcast_convert_fusion
  (227 shorter events, 55.3 us)
Async XLA Ops:
  7.2 13.7 %copy-start = (bf16[144,6912]{1,0:T(8,128)(2,1)S(1)}, bf16[144,6912]{1,0:T(8,128)(2,1)}, u32[]{:S(2)}) copy-start(bf16[144,6912]{1,0:T(8,128)(2,1)} %param.21) | copy-start | bytes 5971972
  7.2 12.1 %copy-start.48 = (s32[16]{0:T(128)S(1)}, s32[16]{0:T(128)}, u32[]{:S(2)}) copy-start(s32[16]{0:T(128)} %param.31) | copy-start | bytes 196
  7.2 12.3 %copy-start.47 = (bf16[64,144]{1,0:T(8,128)(2,1)S(1)}, bf16[64,144]{1,0:T(8,128)(2,1)}, u32[]{:S(2)}) copy-start(bf16[64,144]{1,0:T(8,128)(2,1)} %param.20) | copy-start | bytes 55300
  7.3 198.2 %all-gather.5.cloned.1.call-start = ((), (), s32[]{:S(2)}) async-start(), calls=%async_computation.2 | async-start | bytes 11943936 | tf_op jit(solution)/shard_map/all_gather | solution.py:1349
  8.0 219.7 %all-gather.7.cloned.1.call-start = ((), (), s32[]{:S(2)}) async-start(), calls=%async_computation.3 | async-start | bytes 11943936 | tf_op jit(solution)/shard_map/all_gather | solution.py:1349
  8.7 235.7 %all-gather.9.cloned.1.call-start = ((), (), s32[]{:S(2)}) async-start(), calls=%async_computation.4 | async-start | bytes 5308416 | tf_op jit(solution)/shard_map/all_gather | solution.py:1349
  9.5 270.0 %all-gather.11.cloned.1.call-start = ((), (), s32[]{:S(2)}) async-start(), calls=%async_computation.5 | async-start | bytes 9437184 | tf_op jit(solution)/shard_map/all_gather | solution.py:1349
  9.5 1.3 collective-permute-start.1
  10.1 7.6 %collective-permute-start = (s32[2,4]{1,0:T(2,128)S(1)}, s32[2,4]{1,0:T(2,128)S(1)}, u32[]{:S(2)}, u32[]{:S(2)}) collective-permute-start(s32[2,4]{1,0:T(2,128)S(1)} %copy-done.37), channel_id=1, source_target_pairs={{0,4},{4,0},{8,12},{12,8},{16,20},{20,16},{24,28},{28,24},{1,5},{5... | collective-permute-start | bytes 104 | tf_op jit(solution)/shard_map/ppermute | solution.py:1282
  10.2 360.8 %reduce-scatter.3.cloned.1.call-start = ((), (), s32[]{:S(2)}) async-start(), calls=%async_computation.6 | async-start | bytes 3538944 | tf_op jit(solution)/shard_map/reduce_scatter | solution.py:1362
  11.1 4.3 collective-permute-start.2
  15.6 3.6 collective-permute-start.3
  137.4 56.9 %copy-start.30 = (f32[1152]{0:T(1024)}, f32[1152]{0:T(1024)S(1)}, u32[]{:S(2)}) copy-start(f32[1152]{0:T(1024)S(1)} %get-tuple-element.124) | copy-start | bytes 13828
  156.0 12.5 %copy-start.7 = (bf16[512,768]{1,0:T(8,128)(2,1)S(1)}, bf16[512,768]{1,0:T(8,128)(2,1)}, u32[]{:S(2)}) copy-start(bf16[512,768]{1,0:T(8,128)(2,1)} %get-tuple-element.76) | copy-start | bytes 2359300
  156.0 13.5 %collective-permute-start.4 = (bf16[512,2304]{1,0:T(8,128)(2,1)}, bf16[512,2304]{1,0:T(8,128)(2,1)}, u32[]{:S(2)}, u32[]{:S(2)}) collective-permute-start(bf16[512,2304]{1,0:T(8,128)(2,1)} %slice.26), channel_id=1, source_target_pairs={{0,4},{4,0},{8,12},{12,8},{16,20},{20,16},{24,28},{28,24},{1,5},{5... | collective-permute-start | bytes 7077896 | tf_op jit(solution)/shard_map/ppermute | solution.py:1282
  169.4 24.9 %copy-start.45 = (bf16[512,1152]{1,0:T(8,128)(2,1)S(1)}, bf16[512,1152]{1,0:T(8,128)(2,1)}, u32[]{:S(2)}) copy-start(bf16[512,1152]{1,0:T(8,128)(2,1)} %get-tuple-element.72.refs_12_) | copy-start | bytes 3538948
  227.7 13.7 %copy-start.2 = (f32[512,1152]{1,0:T(8,128)S(1)}, f32[512,1152]{1,0:T(8,128)}, u32[]{:S(2)}) copy-start(f32[512,1152]{1,0:T(8,128)} %copy-done.1) | copy-start | bytes 7077892
  242.8 9.6 %collective-permute-start.5 = (bf16[512,1152]{1,0:T(8,128)(2,1)S(1)}, bf16[512,1152]{1,0:T(8,128)(2,1)}, u32[]{:S(2)}, u32[]{:S(2)}) collective-permute-start(bf16[512,1152]{1,0:T(8,128)(2,1)S(1)} %add_convert_fusion), channel_id=1, source_target_pairs={{0,4},{4,0},{8,12},{12,8},{16,20},{20,16},{24,28},{28,24},{1,5},{5... | collective-permute-start | bytes 3538952 | tf_op jit(solution)/shard_map/ppermute | solution.py:1282
  244.5 7.9 %copy-start.11 = (pred[384,1024]{1,0:T(32,128)(4,1)S(1)}, pred[384,1024]{1,0:T(32,128)(4,1)}, u32[]{:S(2)}) copy-start(pred[384,1024]{1,0:T(32,128)(4,1)} %get-tuple-element.166) | copy-start | bytes 1179652
  244.5 7.9 %copy-start.13 = (pred[384,1024]{1,0:T(32,128)(4,1)S(1)}, pred[384,1024]{1,0:T(32,128)(4,1)}, u32[]{:S(2)}) copy-start(pred[384,1024]{1,0:T(32,128)(4,1)} %get-tuple-element.167) | copy-start | bytes 1179652
  244.5 7.9 %copy-start.15 = (pred[384,1024]{1,0:T(32,128)(4,1)S(1)}, pred[384,1024]{1,0:T(32,128)(4,1)}, u32[]{:S(2)}) copy-start(pred[384,1024]{1,0:T(32,128)(4,1)} %get-tuple-element.164) | copy-start | bytes 1179652
  244.5 7.9 %copy-start.17 = (pred[384,1024]{1,0:T(32,128)(4,1)S(1)}, pred[384,1024]{1,0:T(32,128)(4,1)}, u32[]{:S(2)}) copy-start(pred[384,1024]{1,0:T(32,128)(4,1)} %get-tuple-element.165) | copy-start | bytes 1179652
  261.0 29.5 %copy-start.8 = (bf16[512,768]{1,0:T(8,128)(2,1)S(1)}, bf16[512,768]{1,0:T(8,128)(2,1)}, u32[]{:S(2)}) copy-start(bf16[512,768]{1,0:T(8,128)(2,1)} %get-tuple-element.76) | copy-start | bytes 2359300
  279.5 11.0 %copy-start.43 = (bf16[8,256,768]{2,1,0:T(8,128)(2,1)S(1)}, bf16[8,256,768]{2,1,0:T(8,128)(2,1)}, u32[]{:S(2)}) copy-start(bf16[8,256,768]{2,1,0:T(8,128)(2,1)} %get-tuple-element.77) | copy-start | bytes 9437188
  297.4 126.4 %reduce-scatter.5.cloned.1.call-start = ((), (), s32[]{:S(2)}) async-start(), calls=%async_computation.7 | async-start | bytes 9437184 | tf_op jit(solution)/shard_map/reduce_scatter | solution.py:1362
  298.5 7.2 %copy-start.51 = (bf16[512,2048]{1,0:T(8,128)(2,1)S(1)}, bf16[512,2048]{1,0:T(8,128)(2,1)}, u32[]{:S(2)}) copy-start(bf16[512,2048]{1,0:T(8,128)(2,1)} %get-tuple-element.75) | copy-start | bytes 6291460
  313.8 14.2 %slice-start = ((s8[4718592]{0:T(1024)(128)(4,1)}), s8[4194304]{0:T(1024)(128)(4,1)S(1)}, s32[]{:S(2)}) async-start(s8[4718592]{0:T(1024)(128)(4,1)} %bitcast.167), calls=%async_computation.8 | async-start | bytes 8388608
  316.9 11.1 %slice-start.1 = ((s8[4718592]{0:T(1024)(128)(4,1)}), s8[524288]{0:T(1024)(128)(4,1)S(1)}, s32[]{:S(2)}) async-start(s8[4718592]{0:T(1024)(128)(4,1)} %bitcast.167), calls=%async_computation.9 | async-start | bytes 1048576
  316.9 11.1 %copy-start.46 = (bf16[512,1152]{1,0:T(8,128)(2,1)S(1)}, bf16[512,1152]{1,0:T(8,128)(2,1)}, u32[]{:S(2)}) copy-start(bf16[512,1152]{1,0:T(8,128)(2,1)} %get-tuple-element.79) | copy-start | bytes 3538948
  331.1 18.6 %copy-start.50 = (bf16[512,1152]{1,0:T(8,128)(2,1)}, bf16[512,1152]{1,0:T(8,128)(2,1)S(1)}, u32[]{:S(2)}) copy-start(bf16[512,1152]{1,0:T(8,128)(2,1)S(1)} %get-tuple-element.96.refs_5_) | copy-start | bytes 3538948
  331.1 18.6 %copy-start.3 = (f32[512,1152]{1,0:T(8,128)S(1)}, f32[512,1152]{1,0:T(8,128)}, u32[]{:S(2)}) copy-start(f32[512,1152]{1,0:T(8,128)} %copy-done.1) | copy-start | bytes 7077892
  349.7 12.3 %copy-start.35 = (f32[512]{0:T(512)S(1)}, f32[512]{0:T(512)}, u32[]{:S(2)}) copy-start(f32[512]{0:T(512)} %copy-done.34) | copy-start | bytes 6148
  (35 other events, 73.3 us)
Sparse Core Ops, SparseCore 0:
  10.0 106.5 all-gather.4
  118.4 64.0 all-gather.6
  184.4 38.9 all-gather.8
  225.1 54.3 all-gather.10
  297.5 46.2 reduce-scatter.2
  347.5 71.2 reduce-scatter.4

commit v5 on v4

--- a/solution.py
+++ b/solution.py
@@ -60,6 +60,78 @@
 
 
 MESH = pl.DeviceIdType.MESH
+def mates():
+    me = lax.axis_index("img")
+    core, x, y = lax.rem(me, 2), lax.rem(me // 2, 2), me // 4
+    return me, (core, x, y), (me + 1 - 2 * core, me + 2 - 4 * x, me + 4 - 8 * y)
+
+
+def greet(where):
+    barrier = pltpu.get_barrier_semaphore()
+    pl.semaphore_signal(barrier, inc=1, device_id=where, device_id_type=MESH)
+
+
+def gather_copies(block, whole, send_sem, recv_sem):
+    me, (_, _, y), (sibling, x_mate, y_mate) = mates()
+    far = x_mate + 4 - 8 * y
+    rows = block.shape[0]
+    cut = (rows // 2 + 15) // 16 * 16
+    upper, lower = pl.ds(0, cut), pl.ds(cut, rows - cut)
+
+    def copy(kind, source, owner, rows, where):
+        return pltpu.make_async_remote_copy(
+            src_ref=source,
+            dst_ref=whole.at[owner, rows, :],
+            send_sem=send_sem.at[kind],
+            recv_sem=recv_sem.at[kind],
+            device_id={"img": where},
+            device_id_type=MESH,
+        )
+
+    found = [
+        copy(0, block.at[upper, :], me, upper, x_mate),
+        copy(1, block.at[lower, :], me, lower, y_mate),
+        copy(2, block.at[upper, :], me, upper, y_mate),
+        copy(3, block.at[lower, :], me, lower, x_mate),
+        copy(4, whole.at[x_mate, upper, :], x_mate, upper, y_mate),
+        copy(5, whole.at[y_mate, lower, :], y_mate, lower, x_mate),
+        copy(6, block.at[upper, :], me, upper, sibling),
+        copy(7, block.at[lower, :], me, lower, sibling),
+    ]
+    come = [(x_mate, upper), (y_mate, lower), (y_mate, upper), (x_mate, lower)]
+    come += [(far, upper), (far, lower)]
+    for kind, (owner, rows) in enumerate(come):
+        found.append(copy(8 + kind, whole.at[owner, rows, :], owner, rows, sibling))
+    return found
+
+
+def first_round(found):
+    for kind in (0, 1, 6, 7):
+        found[kind].start()
+
+
+def second_round(found):
+    found[0].wait_recv()
+    for kind in (4, 2, 8):
+        found[kind].start()
+    found[1].wait_recv()
+    for kind in (5, 3, 9):
+        found[kind].start()
+
+
+def third_round(found):
+    for kind in (4, 5, 2, 3):
+        found[kind].wait_recv()
+        found[8 + kind].start()
+
+
+def last_round(found):
+    for kind, one in enumerate(found):
+        if kind >= 6:
+            one.wait_recv()
+        one.wait_send()
+
+
 HALF = HEADS // 2
 
 
@@ -86,9 +158,24 @@
     return pl.ds(pl.multiple_of(first + part * width, 128), window)
 
 
-def attend_kernel(own_ref, rest_ref, mix_ref, lse_ref):
+def attend_kernel(remote, own_ref, *refs):
+    mix_ref, lse_ref, rest_ref = refs[:3] if remote else (refs[1], refs[2], refs[0])
     length, width = mix_ref.shape
     block = min(256, length)
+    if remote:
+        me = lax.axis_index("img")
+        sibling = {"img": me + 1 - 2 * lax.rem(me, 2)}
+        greet(sibling)
+        pl.semaphore_wait(pltpu.get_barrier_semaphore(), 1)
+        swap = pltpu.make_async_remote_copy(
+            src_ref=own_ref.at[:, pl.ds(width, 2 * width)],
+            dst_ref=rest_ref,
+            send_sem=refs[3],
+            recv_sem=refs[4],
+            device_id=sibling,
+            device_id_type=MESH,
+        )
+        swap.start()
 
     def one_head(head, window):
         first, mine = head_window(head, width, window)
@@ -120,33 +207,41 @@
             lse_ref[head, :, rows] = log_total.T[:1, :]
 
     mix_ref[...] = jnp.zeros_like(mix_ref)
+    if remote:
+        swap.wait()
     each_head(one_head)
 
 
 def attend(own, rest, width):
-    length, span = own.shape[0], own.shape[0] + rest.shape[0]
-    vmem, bf16 = pl.BlockSpec(memory_space=pltpu.VMEM), jnp.bfloat16
+    length, bf16 = own.shape[0], jnp.bfloat16
+    vmem = pl.BlockSpec(memory_space=pltpu.VMEM)
+    shapes = [
+        jax.ShapeDtypeStruct((length, width), bf16),
+        jax.ShapeDtypeStruct((HEADS, 1, length), jnp.float32),
+    ]
+    remote, operands, scratch, params = rest is None, [own], [], {}
+    span = 2 * length
+    if remote:
+        shapes.append(jax.ShapeDtypeStruct((length, 2 * width), bf16))
+        scratch = [pltpu.SemaphoreType.DMA] * 2
+        params = dict(collective_id=3, has_side_effects=True)
+    else:
+        operands.append(rest)
+        span = length + rest.shape[0]
     return pl.pallas_call(
-        attend_kernel,
-        in_specs=[vmem] * 2,
-        out_specs=[vmem] * 2,
-        out_shape=[
-            jax.ShapeDtypeStruct((length, width), bf16),
-            jax.ShapeDtypeStruct((HEADS, 1, length), jnp.float32),
-        ],
-        compiler_params=pltpu.CompilerParams(vmem_limit_bytes=60 * 1024 * 1024),
+        functools.partial(attend_kernel, remote),
+        in_specs=[vmem] * len(operands),
+        out_specs=[vmem] * len(shapes),
+        out_shape=shapes,
+        scratch_shapes=scratch,
+        compiler_params=pltpu.CompilerParams(vmem_limit_bytes=40 * 1024 * 1024, **params),
         cost_estimate=pl.CostEstimate(
             flops=4 * HEADS * length * span * 256,
             bytes_accessed=4 * (length + span) * width * 2,
             transcendentals=HEADS * length * span,
         ),
         name="attend",
-    )(own, rest)
-
-
-def greet(where):
-    barrier = pltpu.get_barrier_semaphore()
-    pl.semaphore_signal(barrier, inc=1, device_id=where, device_id_type=MESH)
+    )(*operands)
 
 
 class Give:
@@ -325,12 +420,6 @@
     return one + other
 
 
-def mates():
-    me = lax.axis_index("img")
-    core, x, y = lax.rem(me, 2), lax.rem(me // 2, 2), me // 4
-    return me, (core, x, y), (me + 1 - 2 * core, me + 2 - 4 * x, me + 4 - 8 * y)
-
-
 def gather_kernel(count, group, per, *refs):
     take = iter(refs)
     blocks = [next(take) for _ in range(count)]
@@ -345,7 +434,6 @@
     part_send, part_recv, *staged = take
     row = lax.axis_index("row")
     me, (core, x, y), (sibling, x_mate, y_mate) = mates()
-    far = x_mate + 4 - 8 * y
     for mate in (sibling, x_mate, y_mate):
         greet({"img": mate})
     for shift in range(1, 4):
@@ -452,48 +540,10 @@
             part_sum[hop] = summed
             part_hop(hop + 1).start()
 
-    def halves(at):
-        rows = blocks[at].shape[0]
-        cut = (rows // 2 + 15) // 16 * 16
-        return pl.ds(0, cut), pl.ds(cut, rows - cut)
-
-    def copy(at, kind, source, owner, rows, where):
-        return pltpu.make_async_remote_copy(
-            src_ref=source,
-            dst_ref=wholes[at].at[owner, rows, :],
-            send_sem=send_sem.at[at, kind],
-            recv_sem=recv_sem.at[at, kind],
-            device_id={"img": where},
-            device_id_type=MESH,
-        )
-
-    def copies(at):
-        upper, lower = halves(at)
-        block, whole = blocks[at], wholes[at]
-        found = [
-            copy(at, 0, block.at[upper, :], me, upper, x_mate),
-            copy(at, 1, block.at[lower, :], me, lower, y_mate),
-            copy(at, 2, block.at[upper, :], me, upper, y_mate),
-            copy(at, 3, block.at[lower, :], me, lower, x_mate),
-            copy(at, 4, whole.at[x_mate, upper, :], x_mate, upper, y_mate),
-            copy(at, 5, whole.at[y_mate, lower, :], y_mate, lower, x_mate),
-            copy(at, 6, block.at[upper, :], me, upper, sibling),
-            copy(at, 7, block.at[lower, :], me, lower, sibling),
-        ]
-        for kind, (owner, rows) in enumerate(
-            [
-                (x_mate, upper),
-                (y_mate, lower),
-                (y_mate, upper),
-                (x_mate, lower),
-                (far, upper),
-                (far, lower),
-            ]
-        ):
-            found.append(copy(at, 8 + kind, whole.at[owner, rows, :], owner, rows, sibling))
-        return found
-
-    every = [copies(at) for at in range(count)]
+    every = [
+        gather_copies(blocks[at], wholes[at], send_sem.at[at], recv_sem.at[at])
+        for at in range(count)
+    ]
     locals_ = [
         pltpu.make_async_copy(blocks[at], staged[at], local_sem.at[at]) for at in range(count)
     ]
@@ -504,22 +554,13 @@
     part_hop(0).start()
     start_slots(0)
     for at in range(count):
-        for kind in (0, 1, 6, 7):
-            every[at][kind].start()
+        first_round(every[at])
         locals_[at].start()
     take_part(0)
     start_slots(1)
     start_slots(2)
-    for at in range(count):
-        found = every[at]
-        found[0].wait_recv()
-        found[4].start()
-        found[2].start()
-        found[8].start()
-        found[1].wait_recv()
-        found[5].start()
-        found[3].start()
-        found[9].start()
+    for found in every:
+        second_round(found)
     take_part(1)
     for at in range(count):
         locals_[at].wait()
@@ -527,19 +568,13 @@
     for which in range(3):
         stage_slots(which)
     pass_slots(0)
-    for at in range(count):
-        found = every[at]
-        for kind in (4, 5, 2, 3):
-            found[kind].wait_recv()
-            found[8 + kind].start()
+    for found in every:
+        third_round(found)
     take_part(2)
     pass_slots(1)
     pass_slots(2)
     for at in range(count):
-        for kind, one in enumerate(every[at]):
-            if kind >= 6:
-                one.wait_recv()
-            one.wait_send()
+        last_round(every[at])
         moved[at].wait()
     for which in range(3):
         end_slots(which)
@@ -1058,7 +1093,7 @@
         grad = spread_of * (grad - jnp.mean(grad, axis=-1, keepdims=True) - norm * along)
         both[core, rows, :] = (residual[rows, :] + grad).astype(jnp.bfloat16)
 
-    token_blocks = source.shape[0] // TOKEN_ROWS // AT_ONCE
+    token_blocks = 1 + source.shape[0] // TOKEN_ROWS
     lanes = source.shape[1] // 128
     swapped, handed = token_blocks + 2, token_blocks + 2 + 4 // AT_ONCE
 
@@ -1069,16 +1104,15 @@
         return pltpu.make_async_copy(spread.at[0], own_block, in_sem.at[9])
 
     def tokens_step(at):
-        @pl.when(at == 0)
+        @pl.when(at == 1)
         def _():
             for which in (3, 5, 6, 7):
                 arrivals[which].wait()
             sums[...] = jnp.zeros_like(sums)
 
-        @pl.when(at < token_blocks)
-        def _():
-            for which in range(AT_ONCE):
-                token_rows(AT_ONCE * at + which)
+        @pl.when((at >= 1) & (at < token_blocks))
+        def _():
+            token_rows(at - 1)
 
         @pl.when(at == token_blocks)
         def _():
@@ -1291,17 +1325,18 @@
         return [(b, a) for a, b in pairs] if back else pairs
 
     own_counts = lax.dynamic_index_in_dim(counts, place % per, 0, keepdims=False)
-    first_of = (jnp.cumsum(own_counts) - own_counts) * RW
     position = jnp.arange(slot_len)
     kept = (row_rank % group) * 2 * length + jnp.arange(2 * length)
-    picks = []
-    for shift in range(n_row):
-        source_row = (row_rank + shift) % n_row
-        begin = lax.dynamic_index_in_dim(first_of, source_row, 0, keepdims=False)
-        limit = lax.dynamic_index_in_dim(own_counts, source_row, 0, keepdims=False) * RW
-        hit = (kept[None, :] == begin + position[:, None]) & (position[:, None] < limit)
-        picks.append(hit)
-    pick = jnp.concatenate(picks, axis=0).astype(bf16)
+    def make_pick(own_counts):
+        first_of = (jnp.cumsum(own_counts) - own_counts) * RW
+        picks = []
+        for shift in range(n_row):
+            source_row = (row_rank + shift) % n_row
+            begin = lax.dynamic_index_in_dim(first_of, source_row, 0, keepdims=False)
+            limit = lax.dynamic_index_in_dim(own_counts, source_row, 0, keepdims=False) * RW
+            hit = (kept[None, :] == begin + position[:, None]) & (position[:, None] < limit)
+            picks.append(hit)
+        return jnp.concatenate(picks, axis=0).astype(bf16)
 
     def image_of(shift):
         return (((row_rank - shift) % n_row) // group) % per
@@ -1405,7 +1440,8 @@
     )
     mod_part = matmul(row_cond, ada_weight) + bias_part[None, :]
     small_plane = n_img == 8 and n_row == 4
-    early = [qkv_weight, out_weight, proj_third]
+    pick = None if small_plane else make_pick(own_counts)
+    early = [qkv_weight, out_weight, proj_first]
     summed_rows = jnp.concatenate([mod_part.reshape(-1), up_bias_part])
     if small_plane:
         early, arrived, summed_rows = gather_weights(
@@ -1415,7 +1451,7 @@
         early = [fetch(one) for one in early]
         for bit in [1] + chip_bits:
             summed_rows = summed_rows + swap(summed_rows, "img", bit)
-    qkv_full, out_full, third_full = early
+    qkv_full, out_full, first_full = early
     modulation = lax.dynamic_index_in_dim(
         summed_rows[: (n_img // 2) * mod_width].reshape(n_img // 2, mod_width),
         img_rank // 2,
@@ -1425,8 +1461,8 @@
     up_bias_full = summed_rows[(n_img // 2) * mod_width :]
     up_full = fetch(up_weight)
     down_full = fetch(down_weight)
-    first_full = fetch(proj_first)
     second_full = fetch(proj_second)
+    third_full = fetch(proj_third)
 
     shift_att, scale_att, gate_att, shift_mlp, scale_mlp, gate_mlp = jnp.split(
         modulation, 6, axis=1
@@ -1450,12 +1486,15 @@
         own_cotangent, own_targets = bring(cotangent).astype(f32), bring(targets).astype(f32)
         h_att = modulate(source, shift_att, scale_att).astype(bf16)
     qkv_rows = matmul(h_att, qkv_full).astype(bf16)
-    rest = swap(qkv_rows[:, width:], "img", 1)
     bits = [1 << at for at in range(group.bit_length() - 1)]
-    for bit in bits:
-        near = jnp.concatenate([qkv_rows[:, width:], rest], axis=0)
-        rest = jnp.concatenate([rest, swap(near, "row", bit)], axis=0)
-    head_mix, log_total = attend(qkv_rows, rest, width)
+    if small_plane:
+        head_mix, log_total, rest = attend(qkv_rows, None, width)
+    else:
+        rest = swap(qkv_rows[:, width:], "img", 1)
+        for bit in bits:
+            near = jnp.concatenate([qkv_rows[:, width:], rest], axis=0)
+            rest = jnp.concatenate([rest, swap(near, "row", bit)], axis=0)
+        head_mix, log_total = attend(qkv_rows, rest, width)
     attn_out = matmul(head_mix, out_full)
     residual = source + gate_att * attn_out
     h_mlp = modulate(residual, shift_mlp, scale_mlp).astype(bf16)
@@ -1470,6 +1509,9 @@
     lin_one = matmul(block_own, first_full)
     hid_one = jax.nn.silu(lin_one).astype(bf16)
     left_first = turn(block_own) if small_plane else block_own
+    if small_plane:
+        own_counts, block_own = lax.optimization_barrier((own_counts, block_own))
+        pick = make_pick(own_counts)
     block_spread = give_start(block_own, swap(block_own, "img", 1))
     tied = lax.optimization_barrier((block_spread, left_first, hid_one))
     block_spread, left_first, hid_one = tied
@@ -1569,8 +1611,8 @@
     )
     d_cond = silu_back(condition, transposed(d_mod, ada_weight))
     grad_table = jnp.dot(select.T, d_cond, precision=lax.Precision.HIGHEST)
-    grad_up_bias = lax.dynamic_slice_in_dim(
-        bias_sum, img_rank * up_bias.shape[0], up_bias.shape[0], 0
+    grad_up_bias = lax.dynamic_index_in_dim(
+        bias_sum.reshape(n_img, -1), img_rank, 0, keepdims=False
     )
     return (
         block_out,

time: 665 us -> 659 us (level); the launches traced: 661 us -> 648 us
  waiting for transfers between devices: 23.1 us -> 4.43 us
  Pallas kernels: 405 us -> 413 us
    all_gather x4, waiting for transfers between devices: 18.5 us -> 0.03 us  [fetch(): return lax.all_gather(operand, 'img', axis=0, tiled=True)]
    pallas_call x1, Pallas kernels: 114 us -> 125 us  [gather_weights(): pl.pallas_call(functools.partial(gather_kernel, count, group, per), in_sp...]
    unnamed x110 -> x120, local copies, waits for them, and re-layouts: 13.8 us -> 12.2 us
  transfers between devices with their start and end apart: 12 -> 11, of which waited for: 4 -> 3; matrix products, arithmetic and copies ran while one was open for 24% -> 26% of each run, Pallas kernels for 29% -> 32%
where the time goes in v5:
time: 659 us; the launch traced here: 648 us
  Pallas kernels  413 us (63%)
  matrix products  144 us (22%)
  local copies, waits for them, and re-layouts  32.7 us (5%)
  other arithmetic  30.2 us (5%)
  between operations  18.1 us (3%)
    pallas_call x1, Pallas kernels, sum_gradients(): pl.pallas_call(functools.partial(sum_kernel, len(lefts), group, per), in_...  207 us
    pallas_call x1, Pallas kernels, gather_weights(): pl.pallas_call(functools.partial(gather_kernel, count, group, per), in_sp...  125 us
    dot_general x9, matrix products, matmul(): return jnp.dot(left_side, right_side, preferred_element_type=jnp.float32)  72.7 us
    dot_general x7, matrix products, transposed(): lax.dot_general(left_side, right_side, LAST, preferred_element_type=jnp.f...  56.7 us
    pallas_call x1, Pallas kernels, attend_back(): pl.pallas_call(functools.partial(attend_back_kernel, give), in_specs=[vme...  48.1 us
    pallas_call x1, Pallas kernels, attend(): pl.pallas_call(functools.partial(attend_kernel, remote), in_specs=[vmem]...  25.6 us
  transfers between devices with their start and end apart: 11, of which 3 were waited for; matrix products, arithmetic and copies ran while one was open for 26% of the time, Pallas kernels for 32%

profile of v5, /device:TPU:0, one launch (start us, length us, event | category | flops | bytes accessed | tf_op | source)
XLA Modules:
  0.0 648.3 jit_solution(16357394911000721411)
XLA Ops:
  11.1 2.8 collective-permute-start.2
  15.6 2.1 collective-permute-start.3
  22.0 125.2 %gather_weights.1 = (bf16[8,144,3456]{2,1,0:T(8,128)(2,1)}, bf16[8,144,1152]{2,1,0:T(8,128)(2,1)}, bf16[8,144,2048]{2,1,0:T(8,128)(2,1)}, bf16[4,384,1152]{2,1,0...) custom-call(bf16[144,3456]{1,0:T(8,128)(2,1)} %refs_0_.1, ...), custom_call_target="tpu_custom_call" | custom-call | bytes 200000000 | tf_op jit(solution)/shard_map/gather_weights/pallas_call | solution.py:587
  149.7 6.5 %compact.1 = (bf16[512,1152]{1,0:T(8,128)(2,1)}, bf16[512,1152]{1,0:T(8,128)(2,1)}, bf16[512,768]{1,0:T(8,128)(2,1)}, bf16[512,1152]{1,0:T(8,128)(2,1)}) custom-call(s32[16]{0:T(128)} %multiply_add_fusion.3.places, bf16[1536,1152]{1,0:T(8,128)(2,1)} %bitcast.136, bf16[1536,1152]{1,0:T(8,128)(2,1)} %bitcast.137, bf16[1536,768]{1,0:T(8,128)(2,1)} %bitcast.139, ...), custom_call_target="tpu_custom_call" | custom-call | bytes 8000000 | tf_op jit(solution)/shard_map/compact/pallas_call | solution.py:658
  156.2 8.5 %convolution_convert_fusion.2.own_ref = bf16[512,3456]{1,0:T(8,128)(2,1)S(1)} fusion(bf16[512,1152]{1,0:T(8,128)(2,1)} %get-tuple-element.72, bf16[1152,3456]{1,0:T(8,128)(2,1)} %bitcast.163), kind=kOutput, calls=%fused_computation.26 | convolution fusion | flops 4078632960 | bytes 12681216 | tf_op jit(solution)/shard_map/dot_general | solution.py:39
  164.7 25.6 %attend.1 = (bf16[512,1152]{1,0:T(8,128)(2,1)S(1)}, f32[16,1,512]{2,1,0:T(1,128)S(1)}, bf16[512,2304]{1,0:T(8,128)(2,1)S(1)}) custom-call(bf16[512,3456]{1,0:T(8,128)(2,1)S(1)} %convolution_convert_fusion.2.own_ref), custom_call_target="tpu_custom_call" | custom-call | flops 8589934592 | bytes 14155776 | tf_op jit(solution)/shard_map/attend/pallas_call | solution.py:231
  190.4 3.3 fusion.73
  196.6 2.5 copy.46
  200.6 2.5 copy.48
  203.4 15.2 %fusion.14 = (bf16[4608,512]{0,1:T(8,128)(2,1)}, f32[512,4608]{1,0:T(8,128)}) fusion(f32[4608]{0:T(1024)S(1)} %slice_bitcast_fusion, bf16[1152,4608]{1,0:T(8,128)(2,1)} %all-gather.5.cloned.1.call-done, f32[512,1152]{1,0:T(8,128)} %copy-done.5, f32[1152]{0:T(1024)S(1)} %get-tuple-element.131, f32[1152]{0:T(1024)S(1)} %get-tuple-element.129, ...), kind=kOutput, calls=%fused_computation.17 | convolution fusion | flops 5462360064 | bytes 27163648 | tf_op jit(solution)/shard_map/dot_general | solution.py:39
  218.5 6.6 %copy.45 = bf16[4608,512]{1,0:T(8,128)(2,1)} copy(bf16[4608,512]{0,1:T(8,128)(2,1)} %get-tuple-element.160) | data formatting | bytes 9437184 | tf_op jit(solution)/shard_map/convert_element_type | solution.py:1502
  225.2 13.2 %fusion.15 = f32[512,1152]{1,0:T(8,128)S(1)} fusion(bf16[4608,1152]{1,0:T(8,128)(2,1)} %all-gather.7.cloned.1.call-done, f32[512,4608]{1,0:T(8,128)} %get-tuple-element.161, f32[4608]{0:T(1024)S(1)} %slice_bitcast_fusion), kind=kOutput, calls=%fused_computation.27 | convolution fusion | flops 5459410944 | bytes 22431744 | tf_op jit(solution)/shard_map/dot_general | solution.py:39
  249.9 8.2 %multiply_convert_fusion.3 = (bf16[512,2048]{1,0:T(8,128)(2,1)}, f32[512,2048]{1,0:T(8,128)}) fusion(bf16[512,1152]{1,0:T(8,128)(2,1)S(1)} %add_convert_fusion, bf16[1152,2048]{1,0:T(8,128)(2,1)} %bitcast.165), kind=kOutput, calls=%fused_computation.36 | convolution fusion | flops 2421161984 | bytes 12189696 | tf_op jit(solution)/shard_map/dot_general | solution.py:39
  258.2 7.8 %convolution_convert_fusion.1 = bf16[1536,1152]{1,0:T(8,128)(2,1)} fusion(bf16[512,1152]{1,0:T(8,128)(2,1)} %collective-permute-done.4, bf16[512,1152]{1,0:T(8,128)(2,1)S(1)} %add_convert_fusion, pred[]{:T(512)S(6)} %eq.198, pred[384,1024]{1,0:T(32,128)(4,1)S(1)} %get-tuple-element.173, pred[384,1024]{1,0:T(32,128)(4,1)S(1)} %get-tuple-element.172, ...), kind=kOutput, calls=%fused_computation.22 | convolution fusion | flops 3640983552 | bytes 7471105 | tf_op jit(solution)/shard_map/dot_general | solution.py:39
  266.0 11.6 %multiply_convert_fusion.2 = (bf16[512,2048]{1,0:T(8,128)(2,1)}, f32[512,2048]{1,0:T(8,128)}) fusion(bf16[512,2048]{1,0:T(8,128)(2,1)} %get-tuple-element.82, bf16[2048,2048]{1,0:T(8,128)(2,1)} %all-gather.9.cloned.1.call-done), kind=kOutput, calls=%fused_computation.34 | convolution fusion | flops 4300210176 | bytes 16777216 | tf_op jit(solution)/shard_map/dot_general | solution.py:39
  277.7 4.5 multiply_reduce_fusion.5
  284.1 3.5 convolution_convert_fusion.3
  288.7 5.9 fusion.18
  295.9 6.9 %convolution_convert_fusion = bf16[2048,2048]{1,0:T(8,128)(2,1)} fusion(bf16[512,2048]{1,0:T(8,128)(2,1)S(1)} %copy-done.56, bf16[512,2048]{1,0:T(8,128)(2,1)S(1)} %fusion.18), kind=kOutput, calls=%fused_computation.21 | convolution fusion | flops 4299161600 | bytes 12582912 | tf_op jit(solution)/shard_map/dot_general | solution.py:47
  304.0 3.1 fusion.70
  307.1 10.4 %fusion.21.refs_9_ = bf16[512,2048]{1,0:T(8,128)(2,1)S(1)} fusion(f32[512,2048]{1,0:T(8,128)} %get-tuple-element.163, bf16[512,2048]{1,0:T(8,128)(2,1)S(1)} %copy-done.58, bf16[2048,2048]{1,0:T(8,128)(2,1)} %all-gather.9.cloned.1.call-done), kind=kOutput, calls=%fused_computation.33 | convolution fusion | flops 4305453056 | bytes 16777216 | tf_op jit(solution)/shard_map/dot_general | solution.py:43
  317.5 6.2 multiply_convert_fusion.5
  323.7 17.2 %convert_reduce_fusion = (f32[4608]{0:T(1024)}, bf16[512,4608]{1,0:T(8,128)(2,1)S(1)}) fusion(f32[512,4608]{1,0:T(8,128)} %get-tuple-element.161, f32[4608]{0:T(1024)S(1)} %slice_bitcast_fusion, bf16[512,1152]{1,0:T(8,128)(2,1)S(1)} %get-tuple-element.102.refs_5_, bf16[4608,1152]{1,0:T(8,128)(2,1)} %all-gather.7.cloned.1.call-done), kind=kOutput, calls=%fused_computation.18 | convolution fusion | flops 5490077184 | bytes 25989120 | tf_op jit(solution)/shard_map/dot_general | solution.py:43
  340.9 13.6 %multiply_reduce_fusion.1 = (f32[1152]{0:T(1024)S(1)}, f32[512]{0:T(512)S(1)}, f32[1152]{0:T(1024)S(1)}, f32[512,1152]{1,0:T(8,128)S(1)}) fusion(f32[512,1152]{1,0:T(8,128)S(1)} %copy-done.7, f32[512]{0:T(512)S(1)} %fusion.58, f32[512]{0:T(512)S(1)} %broadcast_multiply_fusion, f32[1152]{0:T(1024)S(1)} %get-tuple-element.129, ...), kind=kOutput, calls=%fused_computation.50 | convolution fusion | flops 5440534016 | bytes 20073984 | tf_op jit(solution)/shard_map/dot_general | solution.py:43
  360.2 2.9 convolution_convert_fusion.4.d_ref
  363.1 48.1 %attend_back.1 = (bf16[512,3456]{1,0:T(8,128)(2,1)}, bf16[3,384,1152]{2,1,0:T(8,128)(2,1)}) custom-call(bf16[512,3456]{1,0:T(8,128)(2,1)} %copy-done.2, bf16[512,2304]{1,0:T(8,128)(2,1)} %copy-done.3, bf16[512,1152]{1,0:T(8,128)(2,1)} %copy-done.1, bf16[512,1152]{1,0:T(8,128)(2,1)} %convolution_convert_fusion.4.d_ref, f32[16,1,512]{2,1,0:T(1,128)} %copy-done.4, ...), custom_call_target="tpu_custom_call" | custom-call | flops 21474836480 | bytes 28311552 | tf_op jit(solution)/shard_map/attend_back/pallas_call | solution.py:391
  411.2 2.3 select_select_fusion.1
  415.5 207.2 %sum_gradients.1 = (bf16[4,144,1152]{2,1,0:T(8,128)(2,1)}, bf16[1,144,4608]{2,1,0:T(8,128)(2,1)}, bf16[1,144,1152]{2,1,0:T(8,128)(2,1)}, bf16[1,144,3456]{2,1,0:...) custom-call(bf16[8,4,144,512]{3,2,1,0:T(8,128)(2,1)} %bitcast.134, ...), custom_call_target="tpu_custom_call" | custom-call | flops 18723373056 | bytes 600000000 | tf_op jit(solution)/shard_map/sum_gradients/pallas_call | solution.py:1224
  624.5 2.7 fusion.77
  630.2 1.8 bitcast_convert_fusion.1
  632.1 1.8 bitcast_convert_fusion
  635.0 1.6 convert_element_type.159
  (234 shorter events, 49.2 us)
Async XLA Ops:
  7.2 13.7 %copy-start = (bf16[144,6912]{1,0:T(8,128)(2,1)S(1)}, bf16[144,6912]{1,0:T(8,128)(2,1)}, u32[]{:S(2)}) copy-start(bf16[144,6912]{1,0:T(8,128)(2,1)} %param.21) | copy-start | bytes 5971972
  7.2 12.1 %copy-start.52 = (s32[16]{0:T(128)S(1)}, s32[16]{0:T(128)}, u32[]{:S(2)}) copy-start(s32[16]{0:T(128)} %param.31) | copy-start | bytes 196
  7.2 12.3 %copy-start.51 = (bf16[64,144]{1,0:T(8,128)(2,1)S(1)}, bf16[64,144]{1,0:T(8,128)(2,1)}, u32[]{:S(2)}) copy-start(bf16[64,144]{1,0:T(8,128)(2,1)} %param.20) | copy-start | bytes 55300
  7.3 196.1 %all-gather.5.cloned.1.call-start = ((), (), s32[]{:S(2)}) async-start(), calls=%async_computation.2 | async-start | bytes 11943936 | tf_op jit(solution)/shard_map/all_gather | solution.py:1384
  8.0 217.2 %all-gather.7.cloned.1.call-start = ((), (), s32[]{:S(2)}) async-start(), calls=%async_computation.3 | async-start | bytes 11943936 | tf_op jit(solution)/shard_map/all_gather | solution.py:1384
  8.7 257.3 %all-gather.9.cloned.1.call-start = ((), (), s32[]{:S(2)}) async-start(), calls=%async_computation.4 | async-start | bytes 9437184 | tf_op jit(solution)/shard_map/all_gather | solution.py:1384
  9.5 268.2 %all-gather.11.cloned.1.call-start = ((), (), s32[]{:S(2)}) async-start(), calls=%async_computation.5 | async-start | bytes 3538944 | tf_op jit(solution)/shard_map/all_gather | solution.py:1384
  9.5 1.3 collective-permute-start.1
  10.1 7.6 %collective-permute-start = (s32[2,4]{1,0:T(2,128)S(1)}, s32[2,4]{1,0:T(2,128)S(1)}, u32[]{:S(2)}, u32[]{:S(2)}) collective-permute-start(s32[2,4]{1,0:T(2,128)S(1)} %copy-done.44), channel_id=1, source_target_pairs={{0,4},{4,0},{8,12},{12,8},{16,20},{20,16},{24,28},{28,24},{1,5},{5... | collective-permute-start | bytes 104 | tf_op jit(solution)/shard_map/ppermute | solution.py:1316
  10.2 353.0 %reduce-scatter.3.cloned.1.call-start = ((), (), s32[]{:S(2)}) async-start(), calls=%async_computation.6 | async-start | bytes 3538944 | tf_op jit(solution)/shard_map/reduce_scatter | solution.py:1397
  11.1 4.3 collective-permute-start.2
  15.6 3.6 collective-permute-start.3
  149.7 40.7 %copy-start.33 = (f32[1152]{0:T(1024)}, f32[1152]{0:T(1024)S(1)}, u32[]{:S(2)}) copy-start(f32[1152]{0:T(1024)S(1)} %get-tuple-element.130) | copy-start | bytes 13828
  164.7 25.7 %copy-start.2 = (bf16[512,3456]{1,0:T(8,128)(2,1)}, bf16[512,3456]{1,0:T(8,128)(2,1)S(1)}, u32[]{:S(2)}) copy-start(bf16[512,3456]{1,0:T(8,128)(2,1)S(1)} %convolution_convert_fusion.2.own_ref) | copy-start | bytes 10616836
  164.7 25.7 %copy-start.47 = (bf16[8,144,1152]{2,1,0:T(8,128)(2,1)S(1)}, bf16[8,144,1152]{2,1,0:T(8,128)(2,1)}, u32[]{:S(2)}) copy-start(bf16[8,144,1152]{2,1,0:T(8,128)(2,1)} %get-tuple-element.77) | copy-start | bytes 7962628
  164.7 25.7 %copy-start.49 = (bf16[512,1152]{1,0:T(8,128)(2,1)S(1)}, bf16[512,1152]{1,0:T(8,128)(2,1)}, u32[]{:S(2)}) copy-start(bf16[512,1152]{1,0:T(8,128)(2,1)} %get-tuple-element.76.refs_12_) | copy-start | bytes 3538948
  190.4 8.8 %copy-start.1 = (bf16[512,1152]{1,0:T(8,128)(2,1)}, bf16[512,1152]{1,0:T(8,128)(2,1)S(1)}, u32[]{:S(2)}) copy-start(bf16[512,1152]{1,0:T(8,128)(2,1)S(1)} %get-tuple-element.75.mix_ref) | copy-start | bytes 3538948
  225.2 13.2 %copy-start.6 = (f32[512,1152]{1,0:T(8,128)S(1)}, f32[512,1152]{1,0:T(8,128)}, u32[]{:S(2)}) copy-start(f32[512,1152]{1,0:T(8,128)} %copy-done.5) | copy-start | bytes 7077892
  239.8 18.3 %collective-permute-start.4 = (bf16[512,1152]{1,0:T(8,128)(2,1)S(1)}, bf16[512,1152]{1,0:T(8,128)(2,1)}, u32[]{:S(2)}, u32[]{:S(2)}) collective-permute-start(bf16[512,1152]{1,0:T(8,128)(2,1)S(1)} %add_convert_fusion), channel_id=1, source_target_pairs={{0,4},{4,0},{8,12},{12,8},{16,20},{20,16},{24,28},{28,24},{1,5},{5... | collective-permute-start | bytes 3538952 | tf_op jit(solution)/shard_map/ppermute | solution.py:1316
  249.1 9.1 %copy-start.15 = (pred[384,1024]{1,0:T(32,128)(4,1)}, pred[384,1024]{1,0:T(32,128)(4,1)S(1)}, u32[]{:S(2)}) copy-start(pred[384,1024]{1,0:T(32,128)(4,1)S(1)} %get-tuple-element.172) | copy-start | bytes 1179652
  249.1 9.1 %copy-start.17 = (pred[384,1024]{1,0:T(32,128)(4,1)}, pred[384,1024]{1,0:T(32,128)(4,1)S(1)}, u32[]{:S(2)}) copy-start(pred[384,1024]{1,0:T(32,128)(4,1)S(1)} %get-tuple-element.173) | copy-start | bytes 1179652
  249.9 8.3 %copy-start.19 = (pred[384,1024]{1,0:T(32,128)(4,1)}, pred[384,1024]{1,0:T(32,128)(4,1)S(1)}, u32[]{:S(2)}) copy-start(pred[384,1024]{1,0:T(32,128)(4,1)S(1)} %get-tuple-element.170) | copy-start | bytes 1179652
  249.9 8.3 %copy-start.21 = (pred[384,1024]{1,0:T(32,128)(4,1)}, pred[384,1024]{1,0:T(32,128)(4,1)S(1)}, u32[]{:S(2)}) copy-start(pred[384,1024]{1,0:T(32,128)(4,1)S(1)} %get-tuple-element.171) | copy-start | bytes 1179652
  266.0 11.6 %copy-start.12 = (bf16[512,768]{1,0:T(8,128)(2,1)S(1)}, bf16[512,768]{1,0:T(8,128)(2,1)}, u32[]{:S(2)}) copy-start(bf16[512,768]{1,0:T(8,128)(2,1)} %get-tuple-element.83) | copy-start | bytes 2359300
  287.6 127.3 %reduce-scatter.5.cloned.1.call-start = ((), (), s32[]{:S(2)}) async-start(), calls=%async_computation.7 | async-start | bytes 9437184 | tf_op jit(solution)/shard_map/reduce_scatter | solution.py:1397
  288.7 7.2 %copy-start.56 = (bf16[512,2048]{1,0:T(8,128)(2,1)S(1)}, bf16[512,2048]{1,0:T(8,128)(2,1)}, u32[]{:S(2)}) copy-start(bf16[512,2048]{1,0:T(8,128)(2,1)} %get-tuple-element.82) | copy-start | bytes 6291460
  307.1 10.4 %copy-start.50 = (bf16[512,1152]{1,0:T(8,128)(2,1)S(1)}, bf16[512,1152]{1,0:T(8,128)(2,1)}, u32[]{:S(2)}) copy-start(bf16[512,1152]{1,0:T(8,128)(2,1)} %get-tuple-element.85) | copy-start | bytes 3538948
  317.5 6.2 copy-start.54
  323.7 17.2 %copy-start.55 = (bf16[512,1152]{1,0:T(8,128)(2,1)}, bf16[512,1152]{1,0:T(8,128)(2,1)S(1)}, u32[]{:S(2)}) copy-start(bf16[512,1152]{1,0:T(8,128)(2,1)S(1)} %get-tuple-element.102.refs_5_) | copy-start | bytes 3538948
  323.7 17.2 %copy-start.7 = (f32[512,1152]{1,0:T(8,128)S(1)}, f32[512,1152]{1,0:T(8,128)}, u32[]{:S(2)}) copy-start(f32[512,1152]{1,0:T(8,128)} %copy-done.5) | copy-start | bytes 7077892
  340.9 13.7 %copy-start.59 = (bf16[512,4608]{1,0:T(8,128)(2,1)}, bf16[512,4608]{1,0:T(8,128)(2,1)S(1)}, u32[]{:S(2)}) copy-start(bf16[512,4608]{1,0:T(8,128)(2,1)S(1)} %get-tuple-element.103.refs_6_) | copy-start | bytes 14155780
  340.9 13.7 %copy-start.39 = (f32[512]{0:T(512)S(1)}, f32[512]{0:T(512)}, u32[]{:S(2)}) copy-start(f32[512]{0:T(512)} %copy-done.38) | copy-start | bytes 6148
  (39 other events, 82.3 us)
Sparse Core Ops, SparseCore 0:
  10.0 106.7 all-gather.4
  118.6 67.1 all-gather.6
  187.8 55.6 all-gather.8
  245.2 31.8 all-gather.10
  287.7 45.6 reduce-scatter.2
  337.1 71.2 reduce-scatter.4

commit v6 on v5

--- a/solution.py
+++ b/solution.py
@@ -234,7 +234,7 @@
         out_specs=[vmem] * len(shapes),
         out_shape=shapes,
         scratch_shapes=scratch,
-        compiler_params=pltpu.CompilerParams(vmem_limit_bytes=40 * 1024 * 1024, **params),
+        compiler_params=pltpu.CompilerParams(vmem_limit_bytes=28 * 1024 * 1024, **params),
         cost_estimate=pl.CostEstimate(
             flops=4 * HEADS * length * span * 256,
             bytes_accessed=4 * (length + span) * width * 2,
@@ -304,8 +304,17 @@
                 whole.wait_recv()
 
 
-def attend_back_kernel(give, own_ref, rest_ref, mix_ref, d_ref, lse_ref, spread, *refs):
+def attend_back_kernel(give, own_in, rest_in, mix_in, d_ref, lse_ref, spread, *refs):
+    *refs, own_ref, rest_ref, mix_ref, load_sem = refs
     length, width = mix_ref.shape
+    loads = [
+        pltpu.make_async_copy(source, target, load_sem.at[at])
+        for at, (source, target) in enumerate(
+            [(own_in, own_ref), (rest_in, rest_ref), (mix_in, mix_ref)]
+        )
+    ]
+    for one in loads:
+        one.start()
     block = 256
     if give:
         d_own, given, d_rest, arrived, core_send, core_recv, *sems = refs
@@ -320,6 +329,8 @@
         d_own, d_rest = refs
     for ref in (d_own, d_rest):
         ref[...] = jnp.zeros_like(ref)
+    for one in loads:
+        one.wait()
 
     def one_head(head, window):
         first, mine = head_window(head, width, window)
@@ -390,10 +401,14 @@
         shapes.append(jax.ShapeDtypeStruct(rest.shape, bf16))
     return pl.pallas_call(
         functools.partial(attend_back_kernel, give),
-        in_specs=[vmem] * 5 + [hbm],
+        in_specs=[hbm] * 3 + [vmem] * 2 + [hbm],
         out_specs=specs,
         out_shape=shapes,
-        scratch_shapes=scratch,
+        scratch_shapes=[
+            *scratch,
+            *[pltpu.VMEM(one.shape, bf16) for one in (own, rest, mixed)],
+            pltpu.SemaphoreType.DMA((3,)),
+        ],
         compiler_params=pltpu.CompilerParams(vmem_limit_bytes=60 * 1024 * 1024, **remote),
         cost_estimate=pl.CostEstimate(
             flops=10 * HEADS * length * span * 256,

time: 659 us -> 658 us (level)
  transfers between devices with their start and end apart: 11 -> 11, of which waited for: 3 -> 3; matrix products, arithmetic and copies ran while one was open for 26% -> 26% of each run, Pallas kernels for 32% -> 31%
where the time goes in v6:
time: 658 us; the launch traced here: 647 us
  Pallas kernels  411 us (62%)
  matrix products  144 us (22%)
  local copies, waits for them, and re-layouts  32.7 us (5%)
  other arithmetic  30.2 us (5%)
  between operations  18.1 us (3%)
    pallas_call x1, Pallas kernels, sum_gradients(): pl.pallas_call(functools.partial(sum_kernel, len(lefts), group, per), in_...  208 us
    pallas_call x1, Pallas kernels, gather_weights(): pl.pallas_call(functools.partial(gather_kernel, count, group, per), in_sp...  125 us
    dot_general x9, matrix products, matmul(): return jnp.dot(left_side, right_side, preferred_element_type=jnp.float32)  72.7 us
    dot_general x7, matrix products, transposed(): lax.dot_general(left_side, right_side, LAST, preferred_element_type=jnp.f...  56.7 us
    pallas_call x1, Pallas kernels, attend_back(): pl.pallas_call(functools.partial(attend_back_kernel, give), in_specs=[hbm...  46 us
    pallas_call x1, Pallas kernels, attend(): pl.pallas_call(functools.partial(attend_kernel, remote), in_specs=[vmem]...  25.6 us
  transfers between devices with their start and end apart: 11, of which 3 were waited for; matrix products, arithmetic and copies ran while one was open for 26% of the time, Pallas kernels for 31%

profile of v6, /device:TPU:0, one launch (start us, length us, event | category | flops | bytes accessed | tf_op | source)
XLA Modules:
  0.0 646.5 jit_solution(17610689604143590986)
XLA Ops:
  11.1 2.8 collective-permute-start.2
  15.6 2.1 collective-permute-start.3
  22.0 125.2 %gather_weights.1 = (bf16[8,144,3456]{2,1,0:T(8,128)(2,1)}, bf16[8,144,1152]{2,1,0:T(8,128)(2,1)}, bf16[8,144,2048]{2,1,0:T(8,128)(2,1)}, bf16[4,384,1152]{2,1,0...) custom-call(bf16[144,3456]{1,0:T(8,128)(2,1)} %refs_0_.1, ...), custom_call_target="tpu_custom_call" | custom-call | bytes 200000000 | tf_op jit(solution)/shard_map/gather_weights/pallas_call | solution.py:602
  149.7 6.5 %compact.1 = (bf16[512,1152]{1,0:T(8,128)(2,1)}, bf16[512,1152]{1,0:T(8,128)(2,1)}, bf16[512,768]{1,0:T(8,128)(2,1)}, bf16[512,1152]{1,0:T(8,128)(2,1)}) custom-call(s32[16]{0:T(128)} %multiply_add_fusion.3.places, bf16[1536,1152]{1,0:T(8,128)(2,1)} %bitcast.136, bf16[1536,1152]{1,0:T(8,128)(2,1)} %bitcast.137, bf16[1536,768]{1,0:T(8,128)(2,1)} %bitcast.139, ...), custom_call_target="tpu_custom_call" | custom-call | bytes 8000000 | tf_op jit(solution)/shard_map/compact/pallas_call | solution.py:673
  156.2 8.5 %convolution_convert_fusion.2.own_ref.own_in = bf16[512,3456]{1,0:T(8,128)(2,1)S(1)} fusion(bf16[512,1152]{1,0:T(8,128)(2,1)} %get-tuple-element.72, bf16[1152,3456]{1,0:T(8,128)(2,1)} %bitcast.163), kind=kOutput, calls=%fused_computation.26 | convolution fusion | flops 4078632960 | bytes 12681216 | tf_op jit(solution)/shard_map/dot_general | solution.py:39
  164.7 25.6 %attend.1 = (bf16[512,1152]{1,0:T(8,128)(2,1)S(1)}, f32[16,1,512]{2,1,0:T(1,128)S(1)}, bf16[512,2304]{1,0:T(8,128)(2,1)S(1)}) custom-call(bf16[512,3456]{1,0:T(8,128)(2,1)S(1)} %convolution_convert_fusion.2.own_ref.own_in), custom_call_target="tpu_custom_call" | custom-call | flops 8589934592 | bytes 14155776 | tf_op jit(solution)/shard_map/attend/pallas_call | solution.py:231
  190.4 3.3 fusion.73
  196.6 2.5 copy.46
  200.6 2.5 copy.48
  203.4 15.2 %fusion.14 = (bf16[4608,512]{0,1:T(8,128)(2,1)}, f32[512,4608]{1,0:T(8,128)}) fusion(f32[4608]{0:T(1024)S(1)} %slice_bitcast_fusion, bf16[1152,4608]{1,0:T(8,128)(2,1)} %all-gather.5.cloned.1.call-done, f32[512,1152]{1,0:T(8,128)} %copy-done.5, f32[1152]{0:T(1024)S(1)} %get-tuple-element.131, f32[1152]{0:T(1024)S(1)} %get-tuple-element.129, ...), kind=kOutput, calls=%fused_computation.17 | convolution fusion | flops 5462360064 | bytes 27163648 | tf_op jit(solution)/shard_map/dot_general | solution.py:39
  218.5 6.6 %copy.45 = bf16[4608,512]{1,0:T(8,128)(2,1)} copy(bf16[4608,512]{0,1:T(8,128)(2,1)} %get-tuple-element.160) | data formatting | bytes 9437184 | tf_op jit(solution)/shard_map/convert_element_type | solution.py:1517
  225.2 13.2 %fusion.15 = f32[512,1152]{1,0:T(8,128)S(1)} fusion(bf16[4608,1152]{1,0:T(8,128)(2,1)} %all-gather.7.cloned.1.call-done, f32[512,4608]{1,0:T(8,128)} %get-tuple-element.161, f32[4608]{0:T(1024)S(1)} %slice_bitcast_fusion), kind=kOutput, calls=%fused_computation.27 | convolution fusion | flops 5459410944 | bytes 22431744 | tf_op jit(solution)/shard_map/dot_general | solution.py:39
  249.9 8.2 %multiply_convert_fusion.3 = (bf16[512,2048]{1,0:T(8,128)(2,1)}, f32[512,2048]{1,0:T(8,128)}) fusion(bf16[512,1152]{1,0:T(8,128)(2,1)S(1)} %add_convert_fusion, bf16[1152,2048]{1,0:T(8,128)(2,1)} %bitcast.165), kind=kOutput, calls=%fused_computation.36 | convolution fusion | flops 2421161984 | bytes 12189696 | tf_op jit(solution)/shard_map/dot_general | solution.py:39
  258.2 7.8 %convolution_convert_fusion.1 = bf16[1536,1152]{1,0:T(8,128)(2,1)} fusion(bf16[512,1152]{1,0:T(8,128)(2,1)} %collective-permute-done.4, bf16[512,1152]{1,0:T(8,128)(2,1)S(1)} %add_convert_fusion, pred[]{:T(512)S(6)} %eq.198, pred[384,1024]{1,0:T(32,128)(4,1)S(1)} %get-tuple-element.173, pred[384,1024]{1,0:T(32,128)(4,1)S(1)} %get-tuple-element.172, ...), kind=kOutput, calls=%fused_computation.22 | convolution fusion | flops 3640983552 | bytes 7471105 | tf_op jit(solution)/shard_map/dot_general | solution.py:39
  266.0 11.6 %multiply_convert_fusion.2 = (bf16[512,2048]{1,0:T(8,128)(2,1)}, f32[512,2048]{1,0:T(8,128)}) fusion(bf16[512,2048]{1,0:T(8,128)(2,1)} %get-tuple-element.82, bf16[2048,2048]{1,0:T(8,128)(2,1)} %all-gather.9.cloned.1.call-done), kind=kOutput, calls=%fused_computation.34 | convolution fusion | flops 4300210176 | bytes 16777216 | tf_op jit(solution)/shard_map/dot_general | solution.py:39
  277.7 4.5 multiply_reduce_fusion.5
  284.1 3.5 convolution_convert_fusion.3
  288.7 5.9 fusion.18
  295.9 6.9 %convolution_convert_fusion = bf16[2048,2048]{1,0:T(8,128)(2,1)} fusion(bf16[512,2048]{1,0:T(8,128)(2,1)S(1)} %copy-done.56, bf16[512,2048]{1,0:T(8,128)(2,1)S(1)} %fusion.18), kind=kOutput, calls=%fused_computation.21 | convolution fusion | flops 4299161600 | bytes 12582912 | tf_op jit(solution)/shard_map/dot_general | solution.py:47
  304.0 3.1 fusion.70
  307.1 10.4 %fusion.21.refs_9_ = bf16[512,2048]{1,0:T(8,128)(2,1)S(1)} fusion(f32[512,2048]{1,0:T(8,128)} %get-tuple-element.163, bf16[512,2048]{1,0:T(8,128)(2,1)S(1)} %copy-done.58, bf16[2048,2048]{1,0:T(8,128)(2,1)} %all-gather.9.cloned.1.call-done), kind=kOutput, calls=%fused_computation.33 | convolution fusion | flops 4305453056 | bytes 16777216 | tf_op jit(solution)/shard_map/dot_general | solution.py:43
  317.5 6.2 multiply_convert_fusion.5
  323.7 17.2 %convert_reduce_fusion = (f32[4608]{0:T(1024)}, bf16[512,4608]{1,0:T(8,128)(2,1)S(1)}) fusion(f32[512,4608]{1,0:T(8,128)} %get-tuple-element.161, f32[4608]{0:T(1024)S(1)} %slice_bitcast_fusion, bf16[512,1152]{1,0:T(8,128)(2,1)S(1)} %get-tuple-element.102.refs_5_, bf16[4608,1152]{1,0:T(8,128)(2,1)} %all-gather.7.cloned.1.call-done), kind=kOutput, calls=%fused_computation.18 | convolution fusion | flops 5490077184 | bytes 25989120 | tf_op jit(solution)/shard_map/dot_general | solution.py:43
  340.9 13.6 %multiply_reduce_fusion.1 = (f32[1152]{0:T(1024)S(1)}, f32[512]{0:T(512)S(1)}, f32[1152]{0:T(1024)S(1)}, f32[512,1152]{1,0:T(8,128)S(1)}) fusion(f32[512,1152]{1,0:T(8,128)S(1)} %copy-done.7, f32[512]{0:T(512)S(1)} %fusion.58, f32[512]{0:T(512)S(1)} %broadcast_multiply_fusion, f32[1152]{0:T(1024)S(1)} %get-tuple-element.129, ...), kind=kOutput, calls=%fused_computation.50 | convolution fusion | flops 5440534016 | bytes 20073984 | tf_op jit(solution)/shard_map/dot_general | solution.py:43
  360.2 2.9 convolution_convert_fusion.4.d_ref
  363.1 46.0 %attend_back.1 = (bf16[512,3456]{1,0:T(8,128)(2,1)}, bf16[3,384,1152]{2,1,0:T(8,128)(2,1)}) custom-call(bf16[512,3456]{1,0:T(8,128)(2,1)} %copy-done.2, bf16[512,2304]{1,0:T(8,128)(2,1)} %copy-done.3, bf16[512,1152]{1,0:T(8,128)(2,1)} %copy-done.1, bf16[512,1152]{1,0:T(8,128)(2,1)} %convolution_convert_fusion.4.d_ref, f32[16,1,512]{2,1,0:T(1,128)} %copy-done.4, ...), custom_call_target="tpu_custom_call" | custom-call | flops 21474836480 | bytes 28311552 | tf_op jit(solution)/shard_map/attend_back/pallas_call | solution.py:402
  409.1 2.3 select_select_fusion.1
  413.4 207.5 %sum_gradients.1 = (bf16[4,144,1152]{2,1,0:T(8,128)(2,1)}, bf16[1,144,4608]{2,1,0:T(8,128)(2,1)}, bf16[1,144,1152]{2,1,0:T(8,128)(2,1)}, bf16[1,144,3456]{2,1,0:...) custom-call(bf16[8,4,144,512]{3,2,1,0:T(8,128)(2,1)} %bitcast.134, ...), custom_call_target="tpu_custom_call" | custom-call | flops 18723373056 | bytes 600000000 | tf_op jit(solution)/shard_map/sum_gradients/pallas_call | solution.py:1239
  622.8 2.7 fusion.77
  628.4 1.8 bitcast_convert_fusion.1
  630.3 1.8 bitcast_convert_fusion
  633.2 1.6 convert_element_type.159
  (234 shorter events, 49.2 us)
Async XLA Ops:
  7.2 13.7 %copy-start = (bf16[144,6912]{1,0:T(8,128)(2,1)S(1)}, bf16[144,6912]{1,0:T(8,128)(2,1)}, u32[]{:S(2)}) copy-start(bf16[144,6912]{1,0:T(8,128)(2,1)} %param.21) | copy-start | bytes 5971972
  7.2 12.1 %copy-start.52 = (s32[16]{0:T(128)S(1)}, s32[16]{0:T(128)}, u32[]{:S(2)}) copy-start(s32[16]{0:T(128)} %param.31) | copy-start | bytes 196
  7.2 12.3 %copy-start.51 = (bf16[64,144]{1,0:T(8,128)(2,1)S(1)}, bf16[64,144]{1,0:T(8,128)(2,1)}, u32[]{:S(2)}) copy-start(bf16[64,144]{1,0:T(8,128)(2,1)} %param.20) | copy-start | bytes 55300
  7.3 196.1 %all-gather.5.cloned.1.call-start = ((), (), s32[]{:S(2)}) async-start(), calls=%async_computation.2 | async-start | bytes 11943936 | tf_op jit(solution)/shard_map/all_gather | solution.py:1399
  8.0 217.2 %all-gather.7.cloned.1.call-start = ((), (), s32[]{:S(2)}) async-start(), calls=%async_computation.3 | async-start | bytes 11943936 | tf_op jit(solution)/shard_map/all_gather | solution.py:1399
  8.7 257.3 %all-gather.9.cloned.1.call-start = ((), (), s32[]{:S(2)}) async-start(), calls=%async_computation.4 | async-start | bytes 9437184 | tf_op jit(solution)/shard_map/all_gather | solution.py:1399
  9.5 268.2 %all-gather.11.cloned.1.call-start = ((), (), s32[]{:S(2)}) async-start(), calls=%async_computation.5 | async-start | bytes 3538944 | tf_op jit(solution)/shard_map/all_gather | solution.py:1399
  9.5 1.3 collective-permute-start.1
  10.1 7.6 %collective-permute-start = (s32[2,4]{1,0:T(2,128)S(1)}, s32[2,4]{1,0:T(2,128)S(1)}, u32[]{:S(2)}, u32[]{:S(2)}) collective-permute-start(s32[2,4]{1,0:T(2,128)S(1)} %copy-done.44), channel_id=1, source_target_pairs={{0,4},{4,0},{8,12},{12,8},{16,20},{20,16},{24,28},{28,24},{1,5},{5... | collective-permute-start | bytes 104 | tf_op jit(solution)/shard_map/ppermute | solution.py:1331
  10.2 353.0 %reduce-scatter.3.cloned.1.call-start = ((), (), s32[]{:S(2)}) async-start(), calls=%async_computation.6 | async-start | bytes 3538944 | tf_op jit(solution)/shard_map/reduce_scatter | solution.py:1412
  11.1 4.3 collective-permute-start.2
  15.6 3.6 collective-permute-start.3
  149.7 40.7 %copy-start.33 = (f32[1152]{0:T(1024)}, f32[1152]{0:T(1024)S(1)}, u32[]{:S(2)}) copy-start(f32[1152]{0:T(1024)S(1)} %get-tuple-element.130) | copy-start | bytes 13828
  164.7 25.7 %copy-start.2 = (bf16[512,3456]{1,0:T(8,128)(2,1)}, bf16[512,3456]{1,0:T(8,128)(2,1)S(1)}, u32[]{:S(2)}) copy-start(bf16[512,3456]{1,0:T(8,128)(2,1)S(1)} %convolution_convert_fusion.2.own_ref.own_in) | copy-start | bytes 10616836
  164.7 25.7 %copy-start.47 = (bf16[8,144,1152]{2,1,0:T(8,128)(2,1)S(1)}, bf16[8,144,1152]{2,1,0:T(8,128)(2,1)}, u32[]{:S(2)}) copy-start(bf16[8,144,1152]{2,1,0:T(8,128)(2,1)} %get-tuple-element.77) | copy-start | bytes 7962628
  164.7 25.7 %copy-start.49 = (bf16[512,1152]{1,0:T(8,128)(2,1)S(1)}, bf16[512,1152]{1,0:T(8,128)(2,1)}, u32[]{:S(2)}) copy-start(bf16[512,1152]{1,0:T(8,128)(2,1)} %get-tuple-element.76.refs_12_) | copy-start | bytes 3538948
  190.4 8.8 %copy-start.1 = (bf16[512,1152]{1,0:T(8,128)(2,1)}, bf16[512,1152]{1,0:T(8,128)(2,1)S(1)}, u32[]{:S(2)}) copy-start(bf16[512,1152]{1,0:T(8,128)(2,1)S(1)} %get-tuple-element.75.mix_in) | copy-start | bytes 3538948
  225.2 13.2 %copy-start.6 = (f32[512,1152]{1,0:T(8,128)S(1)}, f32[512,1152]{1,0:T(8,128)}, u32[]{:S(2)}) copy-start(f32[512,1152]{1,0:T(8,128)} %copy-done.5) | copy-start | bytes 7077892
  239.8 18.3 %collective-permute-start.4 = (bf16[512,1152]{1,0:T(8,128)(2,1)S(1)}, bf16[512,1152]{1,0:T(8,128)(2,1)}, u32[]{:S(2)}, u32[]{:S(2)}) collective-permute-start(bf16[512,1152]{1,0:T(8,128)(2,1)S(1)} %add_convert_fusion), channel_id=1, source_target_pairs={{0,4},{4,0},{8,12},{12,8},{16,20},{20,16},{24,28},{28,24},{1,5},{5... | collective-permute-start | bytes 3538952 | tf_op jit(solution)/shard_map/ppermute | solution.py:1331
  249.1 9.1 %copy-start.15 = (pred[384,1024]{1,0:T(32,128)(4,1)}, pred[384,1024]{1,0:T(32,128)(4,1)S(1)}, u32[]{:S(2)}) copy-start(pred[384,1024]{1,0:T(32,128)(4,1)S(1)} %get-tuple-element.172) | copy-start | bytes 1179652
  249.1 9.1 %copy-start.17 = (pred[384,1024]{1,0:T(32,128)(4,1)}, pred[384,1024]{1,0:T(32,128)(4,1)S(1)}, u32[]{:S(2)}) copy-start(pred[384,1024]{1,0:T(32,128)(4,1)S(1)} %get-tuple-element.173) | copy-start | bytes 1179652
  249.9 8.3 %copy-start.19 = (pred[384,1024]{1,0:T(32,128)(4,1)}, pred[384,1024]{1,0:T(32,128)(4,1)S(1)}, u32[]{:S(2)}) copy-start(pred[384,1024]{1,0:T(32,128)(4,1)S(1)} %get-tuple-element.170) | copy-start | bytes 1179652
  249.9 8.3 %copy-start.21 = (pred[384,1024]{1,0:T(32,128)(4,1)}, pred[384,1024]{1,0:T(32,128)(4,1)S(1)}, u32[]{:S(2)}) copy-start(pred[384,1024]{1,0:T(32,128)(4,1)S(1)} %get-tuple-element.171) | copy-start | bytes 1179652
  266.0 11.6 %copy-start.12 = (bf16[512,768]{1,0:T(8,128)(2,1)S(1)}, bf16[512,768]{1,0:T(8,128)(2,1)}, u32[]{:S(2)}) copy-start(bf16[512,768]{1,0:T(8,128)(2,1)} %get-tuple-element.83) | copy-start | bytes 2359300
  287.6 125.2 %reduce-scatter.5.cloned.1.call-start = ((), (), s32[]{:S(2)}) async-start(), calls=%async_computation.7 | async-start | bytes 9437184 | tf_op jit(solution)/shard_map/reduce_scatter | solution.py:1412
  288.7 7.2 %copy-start.56 = (bf16[512,2048]{1,0:T(8,128)(2,1)S(1)}, bf16[512,2048]{1,0:T(8,128)(2,1)}, u32[]{:S(2)}) copy-start(bf16[512,2048]{1,0:T(8,128)(2,1)} %get-tuple-element.82) | copy-start | bytes 6291460
  307.1 10.4 %copy-start.50 = (bf16[512,1152]{1,0:T(8,128)(2,1)S(1)}, bf16[512,1152]{1,0:T(8,128)(2,1)}, u32[]{:S(2)}) copy-start(bf16[512,1152]{1,0:T(8,128)(2,1)} %get-tuple-element.85) | copy-start | bytes 3538948
  317.5 6.2 copy-start.54
  323.7 17.2 %copy-start.55 = (bf16[512,1152]{1,0:T(8,128)(2,1)}, bf16[512,1152]{1,0:T(8,128)(2,1)S(1)}, u32[]{:S(2)}) copy-start(bf16[512,1152]{1,0:T(8,128)(2,1)S(1)} %get-tuple-element.102.refs_5_) | copy-start | bytes 3538948
  323.7 17.2 %copy-start.7 = (f32[512,1152]{1,0:T(8,128)S(1)}, f32[512,1152]{1,0:T(8,128)}, u32[]{:S(2)}) copy-start(f32[512,1152]{1,0:T(8,128)} %copy-done.5) | copy-start | bytes 7077892
  340.9 13.7 %copy-start.59 = (bf16[512,4608]{1,0:T(8,128)(2,1)}, bf16[512,4608]{1,0:T(8,128)(2,1)S(1)}, u32[]{:S(2)}) copy-start(bf16[512,4608]{1,0:T(8,128)(2,1)S(1)} %get-tuple-element.103.refs_6_) | copy-start | bytes 14155780
  340.9 13.7 %copy-start.39 = (f32[512]{0:T(512)S(1)}, f32[512]{0:T(512)}, u32[]{:S(2)}) copy-start(f32[512]{0:T(512)} %copy-done.38) | copy-start | bytes 6148
  (39 other events, 82.3 us)
Sparse Core Ops, SparseCore 0:
  10.0 106.7 all-gather.4
  118.6 67.1 all-gather.6
  187.8 55.6 all-gather.8
  245.2 31.8 all-gather.10
  287.7 45.6 reduce-scatter.2
  337.1 71.2 reduce-scatter.4
